TPU v7x, 32 devices: a whole 2x2x4 slice. The times are simulated.
32 devices in a mesh: dp: 8 (over z, x), ctx: 4 (over y, core).
Axes of the slice: x: 2, y: 2, z: 4, core: 2. Of those that a mesh axis runs over, the one named last changes fastest.
Arguments:
- tokens: bfloat16 [2, 16384, 576], P(None, ('dp', 'ctx')), may hold values from -6 to 6
- lengths: int32 [2, 8, 4], P(None, 'dp'), may hold values from 1 to 2045, as said below
- weights: float32 [3538944], P(('dp', 'ctx'))
- momentum: float32 [3538944], P(('dp', 'ctx'))
- norm_gains: float32 [2, 576], replicated, may hold values from 0.5 to 1.5
- gain_first: float32 [2, 576], replicated, may hold values from -57.926186 to 57.926186
- gain_second: float32 [2, 576], replicated, may hold values from 425.984 to 6553.6
- cotangent: bfloat16 [2, 16384, 576], P(None, ('dp', 'ctx')), may hold values from -12 to 12
Outputs:
- outputs: float32 [2, 16384, 576], P(None, ('dp', 'ctx'))
- d_tokens: float32 [2, 16384, 576], P(None, ('dp', 'ctx'))
- weight_grads: float32 [3538944], P(('dp', 'ctx'))
- new_momentum: float32 [3538944], P(('dp', 'ctx'))
- new_weights: float32 [3538944], P(('dp', 'ctx'))
- gain_first_new: float32 [2, 576], replicated
- gain_second_new: float32 [2, 576], replicated
- new_gains: float32 [2, 576], replicated
Inputs may be any that keep to these rules, and one draw needn't show every extreme that they name: Each row of lengths sums to 2048; its entry 1 equals 2048 minus the other three, and each other entry lies between 1 and 255. In every draw one buffer has all three other entries equal to 1.
All inputs are finite; a program needn't handle non-finite values.
Results may differ from a plain program's by a relative error of at most 0.015.
Values may be sent and summed in bfloat16 or wider, within the bound.
No kernel may reach another device: no remote copies, remote signals or barrier semaphores. Data moves between devices by JAX's collectives and lax.ppermute only.
A program may use at most 384 MiB of HBM per device.

v0:
```python
from functools import partial
import math

import jax
import jax.numpy as jnp
from jax import lax
from jax.sharding import PartitionSpec as P

HEADS = 9
KV_HEADS = 3
HEAD_DIM = 64
FF = 1536
NS_STEPS = 5
ADAM_STEP = 10
D = 576
KV_WIDTH = 192


norm_epsilon = 1e-05
rope_base = 100000.0
masked_score = -1e30
newton_first = 3.4445
newton_second = -4.775
newton_third = 2.0315
momentum_decay = 0.95
matrix_rate = 0.2
weight_decay = 0.1
gain_rate = 0.2
first_decay = 0.9
second_decay = 0.95
adam_epsilon = 1e-08
frobenius_epsilon = 1e-07


def matrix_shapes():
    return [(D, D), (D, KV_WIDTH), (D, KV_WIDTH), (D, D), (D, FF), (D, FF), (FF, D)]


def unpack(flat_vector):
    matrices = []
    offset = 0
    for height, breadth in matrix_shapes():
        matrices.append(flat_vector[offset : offset + height * breadth].reshape(height, breadth))
        offset = offset + height * breadth
    return matrices


def multiply_high(left, right):
    return jnp.dot(left, right, precision=lax.Precision.HIGHEST, preferred_element_type=jnp.float32)


def layout(lengths_row, places):
    finish = jnp.cumsum(lengths_row)
    firsts = finish - lengths_row
    document = jnp.sum((places[:, None] >= finish[None, :-1]).astype(jnp.int32), axis=1)
    begins = jnp.max(jnp.where(places[:, None] >= firsts[None, :], firsts[None, :], 0), axis=1)
    return (places - begins, document)


def rotate(values, offsets, direction):
    rotary_half_width = values.shape[-1] // 2
    inverse = jnp.exp(
        jnp.arange(rotary_half_width, dtype=jnp.float32)
        * (-2.0 * math.log(rope_base) / values.shape[-1])
    )
    angles = offsets.astype(jnp.float32)[:, None] * inverse[None, :]
    rotary_cosine = jnp.cos(angles)[:, None, :]
    sine_part = direction * jnp.sin(angles)[:, None, :]
    former = values[..., :rotary_half_width]
    latter = values[..., rotary_half_width:]
    return jnp.concatenate(
        [former * rotary_cosine - latter * sine_part, latter * rotary_cosine + former * sine_part],
        axis=-1,
    )


def normalize(values, gain):
    scaling = lax.rsqrt(jnp.mean(values * values, axis=-1, keepdims=True) + norm_epsilon)
    return values * scaling * gain


def normalize_back(values, gain, upstream):
    scaling = lax.rsqrt(jnp.mean(values * values, axis=-1, keepdims=True) + norm_epsilon)
    weighted = upstream * gain
    gain_grad = jnp.sum(upstream * values * scaling, axis=0)
    inner_term = jnp.mean(weighted * values, axis=-1, keepdims=True)
    return (scaling * weighted - values * (scaling * scaling * scaling) * inner_term, gain_grad)


def orthogonalize(matrix):
    flipped = matrix.shape[0] > matrix.shape[1]
    current = matrix.T if flipped else matrix
    current = current / (jnp.sqrt(jnp.sum(current * current)) + frobenius_epsilon)
    for iteration in range(NS_STEPS):
        square = multiply_high(current, current.T)
        mixer = newton_second * square + newton_third * multiply_high(square, square)
        current = newton_first * current + multiply_high(mixer, current)
    result = current.T if flipped else current
    return result * (0.2 * math.sqrt(max(matrix.shape)))


def own_matrix(matrix_index, source):
    shapes = matrix_shapes()
    matrices = unpack(source)
    result = orthogonalize(matrices[matrix_index]).reshape(-1)
    before = sum((height * breadth for height, breadth in shapes[:matrix_index]))
    after = source.shape[0] - before - result.shape[0]
    return jnp.concatenate(
        [jnp.zeros((before,), jnp.float32), result, jnp.zeros((after,), jnp.float32)]
    )


def empty_update(source):
    return jnp.zeros_like(source)


def owned_updates(device_index, owners, source):
    total = jnp.zeros_like(source)
    for matrix_index in range(len(owners)):
        total = total + lax.cond(
            device_index == owners[matrix_index],
            partial(own_matrix, matrix_index),
            empty_update,
            source,
        )
    return total


def masked_scores(queries, key_block, key_places, key_docs, query_places, query_docs):
    raw_scores = jnp.einsum(
        "tgrd,kgd->grtk", queries, key_block, preferred_element_type=jnp.float32
    )
    allowed = (query_docs[:, None] == key_docs[None, :]) & (
        key_places[None, :] <= query_places[:, None]
    )
    return jnp.where(allowed, raw_scores * 0.125, masked_score)


def key_blocks(keyvals, key_docs):
    total_rows = keyvals.shape[0]
    block_rows = min(512, total_rows)
    block_count = total_rows // block_rows
    key_part = keyvals[:, :KV_WIDTH].reshape(block_count, block_rows, KV_HEADS, HEAD_DIM)
    value_part = keyvals[:, KV_WIDTH:].reshape(block_count, block_rows, KV_HEADS, HEAD_DIM)
    places = jnp.arange(total_rows, dtype=jnp.int32).reshape(block_count, block_rows)
    return (key_part, value_part, places, key_docs.reshape(block_count, block_rows))


def attend_forward(queries, keyvals, query_places, query_docs, key_docs):
    key_part, value_part, places, block_docs = key_blocks(keyvals, key_docs)
    local_rows = queries.shape[0]
    repeats = HEADS // KV_HEADS

    def measure(carry, block_item):
        running_top, running_total = carry
        key_block, block_places, docs_block = block_item
        scores = masked_scores(
            queries, key_block, block_places, docs_block, query_places, query_docs
        )
        new_top = jnp.maximum(running_top, jnp.max(scores, axis=-1))
        new_total = running_total * jnp.exp(running_top - new_top) + jnp.sum(
            jnp.exp(scores - new_top[..., None]), axis=-1
        )
        return ((new_top, new_total), None)

    start_top = jnp.full((KV_HEADS, repeats, local_rows), masked_score, jnp.float32)
    start_total = jnp.zeros((KV_HEADS, repeats, local_rows), jnp.float32)
    (final_top, final_total), unused = lax.scan(
        measure, (start_top, start_total), (key_part, places, block_docs)
    )
    log_total = final_top + jnp.log(final_total)

    def collect(carry, block_item):
        key_block, value_block, block_places, docs_block = block_item
        scores = masked_scores(
            queries, key_block, block_places, docs_block, query_places, query_docs
        )
        probs_low = jnp.exp(scores - log_total[..., None]).astype(jnp.bfloat16)
        return (
            carry
            + jnp.einsum(
                "grtk,kgd->tgrd", probs_low, value_block, preferred_element_type=jnp.float32
            ),
            None,
        )

    start_mixed = jnp.zeros((local_rows, KV_HEADS, repeats, HEAD_DIM), jnp.float32)
    mixed, unused_more = lax.scan(collect, start_mixed, (key_part, value_part, places, block_docs))
    return (mixed.reshape(local_rows, HEADS * HEAD_DIM).astype(jnp.bfloat16), log_total)


def attend_back(queries, keyvals, query_places, query_docs, key_docs, log_total, mixed, grad_mixed):
    key_part, value_part, places, block_docs = key_blocks(keyvals, key_docs)
    local_rows = queries.shape[0]
    repeats = HEADS // KV_HEADS
    output_gradient = grad_mixed.reshape(local_rows, KV_HEADS, repeats, HEAD_DIM)
    combined_head_output = mixed.reshape(local_rows, KV_HEADS, repeats, HEAD_DIM)
    softmax_correction = jnp.einsum(
        "vyuc,vyuc->yuv", output_gradient, combined_head_output, preferred_element_type=jnp.float32
    )

    def sweep(carry, block_item):
        key_block, value_block, block_places, docs_block = block_item
        scores = masked_scores(
            queries, key_block, block_places, docs_block, query_places, query_docs
        )
        probs = jnp.exp(scores - log_total[..., None])
        grad_probs = jnp.einsum(
            "tgrd,kgd->grtk", output_gradient, value_block, preferred_element_type=jnp.float32
        )
        grad_scores = (probs * (grad_probs - softmax_correction[..., None]) * 0.125).astype(
            jnp.bfloat16
        )
        query_term = carry + jnp.einsum(
            "grtk,kgd->tgrd", grad_scores, key_block, preferred_element_type=jnp.float32
        )
        key_grad = jnp.einsum(
            "grtk,tgrd->kgd", grad_scores, queries, preferred_element_type=jnp.float32
        )
        value_grad = jnp.einsum(
            "grtk,tgrd->kgd",
            probs.astype(jnp.bfloat16),
            output_gradient,
            preferred_element_type=jnp.float32,
        )
        block_rows = key_block.shape[0]
        joined = jnp.concatenate(
            [key_grad.reshape(block_rows, KV_WIDTH), value_grad.reshape(block_rows, KV_WIDTH)],
            axis=-1,
        )
        return (query_term, joined)

    start_query = jnp.zeros((local_rows, KV_HEADS, repeats, HEAD_DIM), jnp.float32)
    query_grad, keyval_grads = lax.scan(
        sweep, start_query, (key_part, value_part, places, block_docs)
    )
    return (
        query_grad.reshape(local_rows, HEADS, HEAD_DIM),
        keyval_grads.reshape(keyvals.shape[0], 2 * KV_WIDTH),
    )


def micro_step(tokens_part, lengths_row, full_weights, norm_gains, back_part):
    local_rows = tokens_part.shape[0]
    total_rows = local_rows * lax.axis_size("ctx")
    query_places = lax.axis_index("ctx") * local_rows + jnp.arange(local_rows, dtype=jnp.int32)
    key_places = jnp.arange(total_rows, dtype=jnp.int32)
    query_offsets, query_docs = layout(lengths_row, query_places)
    key_docs = layout(lengths_row, key_places)[1]
    w_query, w_key, w_value, w_out, w_gate, w_up, w_down = unpack(full_weights)
    inputs = tokens_part.astype(jnp.float32)
    normed = normalize(inputs, norm_gains[0]).astype(jnp.bfloat16)
    query_lin = jnp.dot(normed, w_query, preferred_element_type=jnp.float32).reshape(
        local_rows, HEADS, HEAD_DIM
    )
    queries = (
        rotate(query_lin, query_offsets, 1.0)
        .astype(jnp.bfloat16)
        .reshape(local_rows, KV_HEADS, HEADS // KV_HEADS, HEAD_DIM)
    )
    key_lin = jnp.dot(normed, w_key, preferred_element_type=jnp.float32).reshape(
        local_rows, KV_HEADS, HEAD_DIM
    )
    keys_low = (
        rotate(key_lin, query_offsets, 1.0).astype(jnp.bfloat16).reshape(local_rows, KV_WIDTH)
    )
    values_low = jnp.dot(normed, w_value, preferred_element_type=jnp.float32).astype(jnp.bfloat16)
    keyvals = lax.all_gather(
        jnp.concatenate([keys_low, values_low], axis=-1), "ctx", axis=0, tiled=True
    )
    mixed, log_total = attend_forward(queries, keyvals, query_places, query_docs, key_docs)
    hidden_state = inputs + jnp.dot(mixed, w_out, preferred_element_type=jnp.float32)
    normed_two = normalize(hidden_state, norm_gains[1]).astype(jnp.bfloat16)
    gate = jnp.dot(normed_two, w_gate, preferred_element_type=jnp.float32)
    upward = jnp.dot(normed_two, w_up, preferred_element_type=jnp.float32)
    sigmoid_gate = jax.nn.sigmoid(gate)
    activated = gate * sigmoid_gate
    hidden = (activated * upward).astype(jnp.bfloat16)
    result = hidden_state + jnp.dot(hidden, w_down, preferred_element_type=jnp.float32)
    grad_w_down = jnp.einsum("tf,td->fd", hidden, back_part, preferred_element_type=jnp.float32)
    grad_hidden = jnp.einsum("td,fd->tf", back_part, w_down, preferred_element_type=jnp.float32)
    grad_gate = (grad_hidden * upward * sigmoid_gate * (1.0 + gate * (1.0 - sigmoid_gate))).astype(
        jnp.bfloat16
    )
    grad_upward = (grad_hidden * activated).astype(jnp.bfloat16)
    grad_w_gate = jnp.einsum("td,tf->df", normed_two, grad_gate, preferred_element_type=jnp.float32)
    grad_w_up = jnp.einsum("td,tf->df", normed_two, grad_upward, preferred_element_type=jnp.float32)
    grad_normed_two = jnp.einsum(
        "tf,df->td", grad_gate, w_gate, preferred_element_type=jnp.float32
    ) + jnp.einsum("tf,df->td", grad_upward, w_up, preferred_element_type=jnp.float32)
    grad_state_norm, gain_two_grad = normalize_back(hidden_state, norm_gains[1], grad_normed_two)
    grad_state = back_part.astype(jnp.float32) + grad_state_norm
    grad_state_low = grad_state.astype(jnp.bfloat16)
    grad_w_out = jnp.einsum("td,te->de", mixed, grad_state_low, preferred_element_type=jnp.float32)
    grad_mixed = jnp.einsum(
        "te,de->td", grad_state_low, w_out, preferred_element_type=jnp.float32
    ).astype(jnp.bfloat16)
    query_grad, keyval_grads = attend_back(
        queries, keyvals, query_places, query_docs, key_docs, log_total, mixed, grad_mixed
    )
    keyval_local = lax.psum_scatter(
        keyval_grads.astype(jnp.bfloat16), "ctx", scatter_dimension=0, tiled=True
    ).astype(jnp.float32)
    grad_query = (
        rotate(query_grad, query_offsets, -1.0)
        .reshape(local_rows, HEADS * HEAD_DIM)
        .astype(jnp.bfloat16)
    )
    grad_key = (
        rotate(
            keyval_local[:, :KV_WIDTH].reshape(local_rows, KV_HEADS, HEAD_DIM), query_offsets, -1.0
        )
        .reshape(local_rows, KV_WIDTH)
        .astype(jnp.bfloat16)
    )
    grad_value = keyval_local[:, KV_WIDTH:].astype(jnp.bfloat16)
    grad_w_query = jnp.einsum("td,te->de", normed, grad_query, preferred_element_type=jnp.float32)
    grad_w_key = jnp.einsum("td,te->de", normed, grad_key, preferred_element_type=jnp.float32)
    grad_w_value = jnp.einsum("td,te->de", normed, grad_value, preferred_element_type=jnp.float32)
    grad_normed = jnp.einsum("te,de->td", grad_query, w_query, preferred_element_type=jnp.float32)
    grad_normed = grad_normed + jnp.einsum(
        "te,de->td", grad_key, w_key, preferred_element_type=jnp.float32
    )
    grad_normed = grad_normed + jnp.einsum(
        "te,de->td", grad_value, w_value, preferred_element_type=jnp.float32
    )
    grad_input_norm, gain_one_grad = normalize_back(inputs, norm_gains[0], grad_normed)
    grad_inputs = grad_state + grad_input_norm
    flat_grads = jnp.concatenate(
        [
            matrix.reshape(-1)
            for matrix in [
                grad_w_query,
                grad_w_key,
                grad_w_value,
                grad_w_out,
                grad_w_gate,
                grad_w_up,
                grad_w_down,
            ]
        ]
    )
    return (result, grad_inputs, flat_grads, jnp.stack([gain_one_grad, gain_two_grad]))


def owner_table(device_count, shard_length):
    shapes = matrix_shapes()
    bounds = []
    owners = []
    offset = 0
    for matrix_index, (height, breadth) in enumerate(shapes):
        middle_device = (offset + height * breadth // 2) // shard_length
        if matrix_index % 2 == 1:
            middle_device = middle_device + device_count // 2
        owners.append(middle_device % device_count)
        offset = offset + height * breadth
        bounds.append(offset)
    return (bounds, owners)


def per_device(tokens, lengths, weights, momentum, norm_gains, gain_first, gain_second, cotangent):
    low_weights = weights.astype(jnp.bfloat16)
    results = []
    input_grads = []
    summed_shard = None
    gain_total = None
    for micro_index in range(tokens.shape[0]):
        full_weights = lax.all_gather(low_weights, ("dp", "ctx"), axis=0, tiled=True)
        result, grad_inputs, flat_grads, gain_grads = micro_step(
            tokens[micro_index],
            lengths[micro_index, 0],
            full_weights,
            norm_gains,
            cotangent[micro_index],
        )
        results.append(result)
        input_grads.append(grad_inputs)
        gain_total = gain_grads if gain_total is None else gain_total + gain_grads
        reduced = lax.psum_scatter(flat_grads, ("dp", "ctx"), scatter_dimension=0, tiled=True)
        summed_shard = reduced if summed_shard is None else summed_shard + reduced
    new_momentum = momentum_decay * momentum + summed_shard
    device_count = lax.axis_size(("dp", "ctx"))
    device_index = lax.axis_index(("dp", "ctx"))
    shard_length = new_momentum.shape[0]
    bounds, owners = owner_table(device_count, shard_length)
    gathered_momentum = lax.all_gather(
        new_momentum.astype(jnp.bfloat16), ("dp", "ctx"), axis=0, tiled=True
    ).astype(new_momentum.dtype)
    owned = owned_updates(device_index, owners, gathered_momentum)
    orthogonal_shard = lax.psum_scatter(owned, ("dp", "ctx"), scatter_dimension=0, tiled=True)
    new_weights = weights * (1.0 - matrix_rate * weight_decay) - matrix_rate * orthogonal_shard
    gain_grad = lax.psum(gain_total, ("dp", "ctx"))
    first_new = first_decay * gain_first + (1.0 - first_decay) * gain_grad
    second_new = second_decay * gain_second + (1.0 - second_decay) * gain_grad * gain_grad
    debiased_first_moment = first_new / (1.0 - first_decay**ADAM_STEP)
    corrected_second = second_new / (1.0 - second_decay**ADAM_STEP)
    new_gains = norm_gains * (
        1.0 - gain_rate * weight_decay
    ) - gain_rate * debiased_first_moment / (jnp.sqrt(corrected_second) + adam_epsilon)
    return (
        jnp.stack(results),
        jnp.stack(input_grads),
        summed_shard,
        new_momentum,
        new_weights,
        first_new,
        second_new,
        new_gains,
    )


def solution(mesh):
    placed = (
        P(None, ("dp", "ctx"), None),
        P(None, "dp", None),
        P(("dp", "ctx")),
        P(("dp", "ctx")),
        P(),
        P(),
        P(),
        P(None, ("dp", "ctx"), None),
    )
    return jax.shard_map(
        per_device,
        mesh=mesh,
        in_specs=placed,
        out_specs=(
            P(None, ("dp", "ctx"), None),
            P(None, ("dp", "ctx"), None),
            P(("dp", "ctx")),
            P(("dp", "ctx")),
            P(("dp", "ctx")),
            P(),
            P(),
            P(),
        ),
        check_vma=False,
    )
```

profile of v0, /device:TPU:8, one launch (start us, length us, event | category | flops | bytes accessed | tf_op | source)
XLA Modules:
  0.0 1433.5 jit_solution(13076330932351218763)
XLA Ops:
  17.1 68.2 %all-gather.5.cloned.1.call-done = bf16[3538944]{0:T(1024)(128)(2,1)} async-done(((bf16[110592]{0:T(1024)(128)(2,1)}), bf16[3538944]{0:T(1024)(128)(2,1)}) %all-gather.5.cloned.1.call-update) | async-done | bytes 7077904 | tf_op jit(solution)/shard_map/all_gather | solution.py:368
  90.1 5.0 fusion.472
  98.9 4.3 slice.319
  106.1 4.4 slice.317
  110.6 4.5 slice.315
  131.6 22.2 %while.74 = (s32[]{:T(128)}, f32[3,3,512]{2,1,0:T(4,128)S(1)}, f32[3,3,512]{2,1,0:T(4,128)S(1)}, s32[512]{0:T(512)S(1)}, s32[4,512]{1,0:T(4,128)}, /*index=5*/s3...) while((s32[]{:T(128)}, f32[3,3,512]{2,1,0:T(4,128)S(1)}, ...), condition=%wide.region_8.9_spmd.clone, body=%wide.region_5.8_spmd.clone.sunk | while | flops 319314944 | bytes 20705420 | solution.py:168
  153.8 21.6 %while.75 = (s32[]{:T(128)}, f32[512,3,3,64]{0,3,2,1:T(8,128)S(1)}, bf16[4,512,3,64]{1,3,2,0:T(8,128)(2,1)}, s32[512]{0:T(512)S(1)}, s32[4,512]{1,0:T(4,128)}, /...) while((s32[]{:T(128)}, f32[512,3,3,64]{0,3,2,1:T(8,128)S(1)}, ...), condition=%wide.region_10.11_spmd.clone, body=%wide.region_9.10_spmd.clone.sunk | while | flops 614793728 | bytes 3905166 | solution.py:188
  154.9 4.3 fusion.833
  160.2 4.3 fusion.833
  165.6 4.3 fusion.833
  170.9 4.3 fusion.833
  183.4 3.9 multiply_convert_fusion.2
  202.6 18.5 %while.76 = (s32[]{:T(128)}, f32[3,3,512]{2,1,0:T(4,128)S(1)}, f32[3,3,512]{2,1,0:T(4,128)S(1)}, s32[512]{0:T(512)S(1)}, s32[4,512]{1,0:T(4,128)}, /*index=5*/s3...) while((s32[]{:T(128)}, f32[3,3,512]{2,1,0:T(4,128)S(1)}, ...), condition=%wide.region_20.21_spmd.clone, body=%wide.region_17.20_spmd.clone.sunk | while | flops 319314944 | bytes 20705420 | solution.py:168
  221.8 26.0 %while.77 = (s32[]{:T(128)}, f32[512,3,3,64]{0,3,2,1:T(8,128)}, bf16[4,512,3,64]{1,3,2,0:T(8,128)(2,1)}, s32[512]{0:T(512)S(1)}, s32[4,512]{1,0:T(4,128)}, /*ind...) while((s32[]{:T(128)}, f32[512,3,3,64]{0,3,2,1:T(8,128)}, ...), condition=%wide.region_22.23_spmd.clone, body=%wide.region_21.22_spmd.clone.sunk | while | flops 614793728 | bytes 3911310 | solution.py:188
  223.2 5.0 fusion.841
  229.2 5.5 fusion.841
  235.7 5.5 fusion.841
  242.2 5.5 fusion.841
  260.0 3.7 multiply_convert_fusion
  279.3 4.6 reshape.840
  283.9 4.7 reshape.839
  288.6 4.8 fusion.420
  293.3 5.3 reshape.841
  302.6 63.1 %while.78 = (s32[]{:T(128)}, f32[512,3,3,64]{0,3,2,1:T(8,128)S(1)}, bf16[4,512,384]{2,1,0:T(8,128)(2,1)}, bf16[4,512,3,64]{1,3,2,0:T(8,128)(2,1)}, s32[512]{0:T(...) while((s32[]{:T(128)}, f32[512,3,3,64]{0,3,2,1:T(8,128)S(1)}, ...), condition=%wide.region_26.27_spmd.clone, body=%wide.region_25.26_spmd.clone.sunk | while | flops 1538064896 | bytes 51388596 | solution.py:234
  309.6 4.4 fusion.853
  321.9 3.4 fusion.855
  325.3 4.4 fusion.853
  337.6 3.4 fusion.855
  341.0 4.4 fusion.853
  353.3 3.4 fusion.855
  356.7 4.4 fusion.853
  370.0 68.5 %while.79 = (s32[]{:T(128)}, f32[512,3,3,64]{0,3,2,1:T(8,128)S(1)}, bf16[4,512,384]{2,1,0:T(8,128)(2,1)}, bf16[4,512,3,64]{1,3,2,0:T(8,128)(2,1)}, s32[512]{0:T(...) while((s32[]{:T(128)}, f32[512,3,3,64]{0,3,2,1:T(8,128)S(1)}, ...), condition=%wide.region_31.32_spmd.clone, body=%wide.region_30.31_spmd.clone.sunk | while | flops 1538064896 | bytes 53760208 | solution.py:234
  376.8 4.3 fusion.868
  393.8 4.3 fusion.868
  410.9 4.3 fusion.868
  428.0 4.3 fusion.868
  457.5 4.6 reshape.847
  462.1 4.7 reshape.846
  466.8 4.8 fusion.416
  471.6 5.3 reshape.848
  481.8 24.6 %reduce-scatter.3.cloned.1.call-done = bf16[512,384]{0,1:T(8,128)(2,1)} async-done(((bf16[2048,384]{0,1:T(8,128)(2,1)}), bf16[512,384]{0,1:T(8,128)(2,1)}) %reduce-scatter.3.cloned.1.call-update) | async-done | bytes 393232 | tf_op jit(solution)/shard_map/reduce_scatter | solution.py:301
  520.0 4.8 constant_dynamic-update-slice_fusion.6
  535.6 4.0 copy-done.9
  539.6 5.8 add.563
  545.5 247.0 %all-reduce.7.cloned.1.call-done = f32[3538944]{0:T(1024)} async-done(((f32[3538944]{0:T(1024)}), f32[3538944]{0:T(1024)}) %all-reduce.7.cloned.1.call-update) | async-done | bytes 14155792
  794.6 74.1 %all-gather.11.cloned.1.call-done = bf16[3538944]{0:T(1024)(128)(2,1)} async-done(((bf16[110592]{0:T(1024)(128)(2,1)}), bf16[3538944]{0:T(1024)(128)(2,1)}) %all-gather.11.cloned.1.call-update) | async-done | bytes 7077904 | tf_op jit(solution)/shard_map/all_gather | solution.py:386
  868.7 8.5 convert_element_type.344
  877.1 12.7 conditional.12
  877.1 5.2 broadcast.517
  889.9 11.1 conditional.9
  889.9 5.2 broadcast.494
  900.9 16.0 %conditional.13 = (f32[3538944]{0:T(1024)}) conditional(s32[]{:T(128)} %convert_element_type.349, () %tuple.86, f32[3538944]{0:T(1024)} %convert_element_type.344), branch_computations={%region_54.55_spmd, %region_55.57_spmd} | conditional | flops 72654192640 | bytes 245514336 | solution.py:120
  901.0 5.2 broadcast.524
  916.9 17.8 %conditional.11 = (f32[3538944]{0:T(1024)}) conditional(s32[]{:T(128)} %convert_element_type.348, () %tuple.84, f32[3538944]{0:T(1024)} %convert_element_type.344), branch_computations={%region_48.49_spmd, %region_49.51_spmd} | conditional | flops 72643575808 | bytes 178274400 | solution.py:120
  916.9 5.3 broadcast.510
  934.7 17.1 %conditional.10 = (f32[3538944]{0:T(1024)}) conditional(s32[]{:T(128)} %convert_element_type.347, () %tuple.83, f32[3538944]{0:T(1024)} %convert_element_type.344), branch_computations={%region_45.46_spmd, %region_46.48_spmd} | conditional | flops 34415235072 | bytes 108822600 | solution.py:120
  934.7 5.2 broadcast.503
  951.8 5.3 conditional.8
  951.8 5.3 broadcast.485
  957.1 23.5 %conditional.7 = (f32[3538944]{0:T(1024)}) conditional(s32[]{:T(128)} %convert_element_type.342, () %tuple.80, f32[3538944]{0:T(1024)} %convert_element_type.344), branch_computations={%region_36.37_spmd, %region_37.39_spmd} | conditional | flops 34408157184 | bytes 77856808 | solution.py:120
  966.3 5.2 broadcast.478
  980.6 36.2 %add_add_fusion = f32[3538944]{0:T(1024)} fusion(f32[3538944]{0:T(1024)} %get-tuple-element.1838, f32[3538944]{0:T(1024)} %get-tuple-element.1837, f32[3538944]{0:T(1024)} %get-tuple-element.1836, f32[3538944]{0:T(1024)} %get-tuple-element.1835, f32[3538944]{0:T(1024)} %get-tuple-element.1834, f32[3538944]{0:T(1024)} %get-tuple-element.1832, ...), kind=kLoop, calls=%fused_computation.450 | loop fusion | flops 21233664 | bytes 113246208 | tf_op jit(solution)/shard_map/add | solution.py:120
  1032.8 200.4 %psum.7 = f32[2,576]{1,0:T(2,128)S(1)} all-reduce(f32[2,576]{1,0:T(2,128)} %maximum_add_fusion), channel_id=1, replica_groups=mesh['dp'=8,'ctx'=4] {'dp','ctx'}, use_global_device_ids=true, to_apply=%region_62.63 | all-reduce | flops 1152 | bytes 9216 | tf_op jit(solution)/shard_map/psum | solution.py:392
  1239.2 185.5 %all-reduce.9.cloned.1.call-done = f32[3538944]{0:T(1024)} async-done(((f32[3538944]{0:T(1024)}), f32[3538944]{0:T(1024)}) %all-reduce.9.cloned.1.call-update) | async-done | bytes 14155792
  (572 shorter events, 304.9 us)
Async XLA Ops:
  7.2 78.2 %all-gather.5.cloned.1.call-start = ((), (), s32[]{:S(2)}) async-start(), calls=%async_computation.2 | async-start | bytes 7299072 | tf_op jit(solution)/shard_map/all_gather | solution.py:368
  9.0 113.2 %all-gather.7.cloned.1.call-start = ((), (), s32[]{:S(2)}) async-start(), calls=%async_computation.3 | async-start | bytes 1966080 | tf_op jit(solution)/shard_map/all_gather | solution.py:268
  12.9 107.1 %copy-start.101 = (f32[576]{0:T(1024)}, f32[576]{0:T(1024)S(1)}, u32[]{:S(2)}) copy-start(f32[576]{0:T(1024)S(1)} %get-tuple-element.943) | copy-start | bytes 6916
  15.3 72.4 %copy-start.24 = (bf16[2,512,576]{1,2,0:T(8,128)(2,1)S(1)}, bf16[2,512,576]{1,2,0:T(8,128)(2,1)}, u32[]{:S(2)}) copy-start(bf16[2,512,576]{1,2,0:T(8,128)(2,1)} %param.34) | copy-start | bytes 3538948
  15.9 101.3 %copy-start.107 = (f32[512]{0:T(512)}, f32[512]{0:T(512)S(1)}, u32[]{:S(2)}) copy-start(f32[512]{0:T(512)S(1)} %get-tuple-element.1157) | copy-start | bytes 6148
  15.9 104.1 %copy-start.110 = (f32[512]{0:T(512)}, f32[512]{0:T(512)S(1)}, u32[]{:S(2)}) copy-start(f32[512]{0:T(512)S(1)} %get-tuple-element.1176) | copy-start | bytes 6148
  17.1 102.0 %copy-start.74 = (f32[512,32]{0,1:T(8,128)}, f32[512,32]{0,1:T(8,128)S(1)}, u32[]{:S(2)}) copy-start(f32[512,32]{0,1:T(8,128)S(1)} %get-tuple-element.1167) | copy-start | bytes 196612
  17.1 103.8 %copy-start.71 = (f32[512,32]{0,1:T(8,128)}, f32[512,32]{0,1:T(8,128)S(1)}, u32[]{:S(2)}) copy-start(f32[512,32]{0,1:T(8,128)S(1)} %get-tuple-element.1150) | copy-start | bytes 196612
  86.6 2.5 copy-start.53
  87.7 28.3 %copy-start.77 = (bf16[576,192]{1,0:T(8,128)(2,1)}, bf16[576,192]{1,0:T(8,128)(2,1)S(1)}, u32[]{:S(2)}) copy-start(bf16[576,192]{1,0:T(8,128)(2,1)S(1)} %slice.303) | copy-start | bytes 663556
  90.1 102.1 %all-gather.9.cloned.1.call-start = ((), (), s32[]{:S(2)}) async-start(), calls=%async_computation.4 | async-start | bytes 1966080 | tf_op jit(solution)/shard_map/all_gather | solution.py:268
  104.9 5.6 copy-start.20
  110.6 4.5 copy-start.98
  121.3 359.4 %reduce-scatter.5.cloned.1.call-start = ((), (), s32[]{:S(2)}) async-start(), calls=%async_computation.6 | async-start | bytes 1966080 | tf_op jit(solution)/shard_map/reduce_scatter | solution.py:301
  128.2 3.4 copy-start.59
  128.2 3.4 copy-start.81
  153.8 22.7 %copy-start.33 = (bf16[576,576]{1,0:T(8,128)(2,1)S(1)}, bf16[576,576]{1,0:T(8,128)(2,1)}, u32[]{:S(2)}) copy-start(bf16[576,576]{1,0:T(8,128)(2,1)} %slice.312) | copy-start | bytes 1990660
  177.9 88.9 %copy-start.22 = (f32[512,576]{0,1:T(8,128)}, f32[512,576]{0,1:T(8,128)S(1)}, u32[]{:S(2)}) copy-start(f32[512,576]{0,1:T(8,128)S(1)} %get-tuple-element.1170) | copy-start | bytes 3538948
  179.8 9.6 copy-start.29
  197.4 5.3 copy-start.58
  197.4 5.2 copy-start.80
  247.7 3.9 copy-start.8
  251.6 15.2 %copy-start.48 = (f32[512,576]{0,1:T(8,128)}, f32[512,576]{0,1:T(8,128)S(1)}, u32[]{:S(2)}) copy-start(f32[512,576]{0,1:T(8,128)S(1)} %get-tuple-element.1172) | copy-start | bytes 3538948
  251.7 2.9 copy-start.32
  251.7 2.9 copy-start.76
  267.5 3.7 copy-start.4
  267.5 4.3 copy-start.6
  271.8 26.9 %copy-start.62 = (bf16[512,576]{0,1:T(8,128)(2,1)}, bf16[512,576]{0,1:T(8,128)(2,1)S(1)}, u32[]{:S(2)}) copy-start(bf16[512,576]{0,1:T(8,128)(2,1)S(1)} %convolution_convert_fusion) | copy-start | bytes 1769476
  283.9 4.7 copy-start.46
  293.3 5.4 copy-start.50
  299.9 2.7 copy-start.3
  299.9 2.7 copy-start.105
  371.3 2.4 copy-start.63
  405.4 2.4 copy-start.63
  422.5 2.4 copy-start.63
  441.2 65.2 %reduce-scatter.3.cloned.1.call-start = ((), (), s32[]{:S(2)}) async-start(), calls=%async_computation.5 | async-start | bytes 1966080 | tf_op jit(solution)/shard_map/reduce_scatter | solution.py:301
  451.2 2.9 copy-start.72
  451.2 2.9 copy-start.87
  462.1 4.7 copy-start.47
  476.9 2.7 copy-start.43
  479.5 312.9 %all-reduce.7.cloned.1.call-start = ((), (), s32[]{:S(2)}) async-start(), calls=%async_computation.8 | async-start | bytes 28311552
  480.7 26.7 %copy-start.73 = (f32[512,32]{0,1:T(8,128)S(1)}, f32[512,32]{0,1:T(8,128)}, u32[]{:S(2)}) copy-start(f32[512,32]{0,1:T(8,128)} %copy-done.71) | copy-start | bytes 196612
  480.7 26.7 %copy-start.88 = (f32[512,32]{0,1:T(8,128)S(1)}, f32[512,32]{0,1:T(8,128)}, u32[]{:S(2)}) copy-start(f32[512,32]{0,1:T(8,128)} %get-tuple-element.1148) | copy-start | bytes 196612
  512.5 16.4 %slice-start = ((s8[14155776]{0:T(1024)(128)(4,1)}), s8[1572864]{0:T(1024)(128)(4,1)S(1)}, s32[]{:S(2)}) async-start(s8[14155776]{0:T(1024)(128)(4,1)} %bitcast.836), calls=%async_computation.10 | async-start | bytes 3145728
  516.1 2.7 copy-start.42
  518.8 6.0 copy-start.12
  518.8 10.1 slice-start.1
  520.0 6.9 copy-start.10
  520.0 9.3 slice-start.2
  524.8 6.3 slice-start.3
  526.9 4.3 copy-start.70
  526.9 4.6 copy-start.41
  531.5 2.8 copy-start.13
  531.5 3.8 copy-start.11
  533.3 6.3 copy-start.9
  545.4 247.0 %copy-start.94 = (f32[110592]{0:T(1024)S(1)}, f32[110592]{0:T(1024)}, u32[]{:S(2)}) copy-start(f32[110592]{0:T(1024)} %param.37) | copy-start | bytes 1327108
  545.4 323.2 %all-gather.11.cloned.1.call-start = ((), (), s32[]{:S(2)}) async-start(), calls=%async_computation.7 | async-start | bytes 7299072 | tf_op jit(solution)/shard_map/all_gather | solution.py:386
  794.5 630.1 %all-reduce.9.cloned.1.call-start = ((), (), s32[]{:S(2)}) async-start(), calls=%async_computation.9 | async-start | bytes 28311552
  1018.6 2.8 copy-start.49
  1018.6 2.8 copy-start.57
  1018.6 3.0 copy-start.66
  1029.9 204.7 %copy-start.5 = (f32[512,576]{0,1:T(8,128)S(1)}, f32[512,576]{0,1:T(8,128)}, u32[]{:S(2)}) copy-start(f32[512,576]{0,1:T(8,128)} %copy-done.4) | copy-start | bytes 3538948
  1029.9 204.7 %copy-start.7 = (f32[512,576]{0,1:T(8,128)S(1)}, f32[512,576]{0,1:T(8,128)}, u32[]{:S(2)}) copy-start(f32[512,576]{0,1:T(8,128)} %copy-done.6) | copy-start | bytes 3538948
  1236.9 187.7 %copy-start.69 = (f32[110592]{0:T(1024)S(1)}, f32[110592]{0:T(1024)}, u32[]{:S(2)}) copy-start(f32[110592]{0:T(1024)} %param.36) | copy-start | bytes 1327108
  (60 other events, 86.3 us)
Sparse Core Ops, SparseCore 0:
  11.5 73.8 all-gather.4
  90.2 18.1 all-gather.6
  121.4 18.1 all-gather.8
  441.3 26.6 reduce-scatter.4
  479.6 26.7 reduce-scatter.2
  545.5 246.8 all-reduce.6
  795.9 72.7 all-gather.10
  1017.0 407.6 all-reduce.8
where the time goes:
time: 1450 us; the launch traced here: 1430 us
  waiting for transfers between devices  599 us (41%)
  matrix products  231 us (16%)
  local copies, waits for them, and re-layouts  216 us (15%)
  blocking collectives  200 us (14%)
  other arithmetic  102 us (7%)
  loops' own time  68.7 us (5%)
  between operations  15.6 us (1%)
    unnamed x10, waiting for transfers between devices  433 us
    psum x1, blocking collectives, per_device(): gain_grad = lax.psum(gain_total, ('dp', 'ctx'))  200 us
    all_gather x1, waiting for transfers between devices, per_device(): lax.all_gather(new_momentum.astype(jnp.bfloat16), ('dp', 'ctx'), axis=0,...  74.1 us
    all_gather x1, waiting for transfers between devices, per_device(): lax.all_gather(low_weights, ('dp', 'ctx'), axis=0, tiled=True)  68.2 us
    another operation x7, loops' own time, owned_updates(): lax.cond(device_index == owners[matrix_index], partial(own_matrix, matrix...  66.7 us
    unnamed x240, local copies, waits for them, and re-layouts  46.9 us
    reshape x14, local copies, waits for them, and re-layouts, micro_step(): matrix.reshape(-1)  43.6 us
    another operation x10, local copies, waits for them, and re-layouts  40 us
  transfers between devices with their start and end apart: 8, of which 5 were waited for; matrix products, arithmetic and copies ran while one was open for 11% of the time, Pallas kernels for 0%

commit v1 on v0

v1 whole, which is shorter than its diff:
```python
from functools import partial
import math

import jax
import jax.numpy as jnp
from jax import lax
from jax.experimental import pallas as pl
from jax.experimental.pallas import tpu as pltpu
from jax.sharding import Mesh, PartitionSpec as P

HEADS = 9
KV_HEADS = 3
HEAD_DIM = 64
FF = 1536
NS_STEPS = 5
ADAM_STEP = 10
D = 576
KV_WIDTH = 192
GROUPS = HEADS // KV_HEADS
TOK = 512
TILE = 256
COLS = GROUPS * TILE
ROW_CUT = 4
COL_CUT = 2
PLANE = ("half", "ctx")
EVERY = ("quarter", "rep", "half", "ctx")


norm_epsilon = 1e-05
rope_base = 100000.0
masked_score = -1e30
newton_first = 3.4445
newton_second = -4.775
newton_third = 2.0315
momentum_decay = 0.95
matrix_rate = 0.2
weight_decay = 0.1
gain_rate = 0.2
first_decay = 0.9
second_decay = 0.95
adam_epsilon = 1e-08
frobenius_epsilon = 1e-07


def layout(lengths_row, places):
    finish = jnp.cumsum(lengths_row)
    firsts = finish - lengths_row
    begins = jnp.max(jnp.where(places[:, None] >= firsts[None, :], firsts[None, :], 0), axis=1)
    return (places - begins, begins)


def rope_tables(offsets):
    half_width = HEAD_DIM // 2
    inverse = jnp.exp(
        jnp.arange(half_width, dtype=jnp.float32) * (-2.0 * math.log(rope_base) / HEAD_DIM)
    )
    angles = inverse[:, None] * offsets.astype(jnp.float32)[None, :]
    return (jnp.cos(angles), jnp.sin(angles))


def rotate_columns(values, cosine, sine):
    shaped = values.reshape(-1, 2, HEAD_DIM // 2, values.shape[-1])
    former, latter = shaped[:, 0], shaped[:, 1]
    return jnp.stack(
        [former * cosine - latter * sine, latter * cosine + former * sine], axis=1
    ).reshape(values.shape)


def normalize(values, gain):
    scaling = lax.rsqrt(jnp.mean(values * values, axis=-1, keepdims=True) + norm_epsilon)
    return values * scaling * gain


def normalize_back(values, gain, upstream):
    scaling = lax.rsqrt(jnp.mean(values * values, axis=-1, keepdims=True) + norm_epsilon)
    weighted = upstream * gain
    gain_grad = jnp.sum(upstream * values * scaling, axis=0)
    inner_term = jnp.mean(weighted * values, axis=-1, keepdims=True)
    return (scaling * weighted - values * (scaling * scaling * scaling) * inner_term, gain_grad)


def dot32(left, right):
    return jnp.dot(left, right, preferred_element_type=jnp.float32)


def masked(scores, key_block, begins, places):
    keys = key_block * TILE + lax.broadcasted_iota(jnp.int32, scores.shape, 0)
    return jnp.where((keys >= begins) & (keys <= places), scores, masked_score)


def tile_row(row, tile):
    part = row[:, tile * TILE : (tile + 1) * TILE]
    return jnp.concatenate([part] * GROUPS, axis=1)


def tile_heads(ref, group, tile):
    return jnp.concatenate(
        [ref[group, head, :, tile * TILE : (tile + 1) * TILE] for head in range(GROUPS)], axis=1
    )


def key_ranges(info, tile):
    first, full, last = info[1 + 3 * tile], info[2 + 3 * tile], info[3 + 3 * tile]
    return ((first, full, True), (full, last, False), (last, last + 1, True))


def forward_kernel(info, q_ref, kv_ref, begin_ref, o_ref, lse_ref, k_nat, v_ext):
    own = info[0]
    for block in range(4):

        @pl.when(block <= own)
        def _():
            for group in range(KV_HEADS):
                low = HEAD_DIM * group
                k_nat[group, TOK * block : TOK * (block + 1), :] = kv_ref[
                    block, low : low + HEAD_DIM, :
                ].T
                low = low + KV_WIDTH
                for part in range(TOK // TILE):
                    spot = block * (TOK // TILE) + part
                    v_ext[group, spot, :HEAD_DIM, :] = kv_ref[
                        block, low : low + HEAD_DIM, part * TILE : (part + 1) * TILE
                    ]
                    v_ext[group, spot, HEAD_DIM:, :] = jnp.ones((16, TILE), jnp.bfloat16)

    def one_group(group, unused):
        for tile in range(TOK // TILE):
            queries = tile_heads(q_ref, group, tile)
            begins = tile_row(begin_ref[...], tile)
            column = lax.broadcasted_iota(jnp.int32, (1, COLS), 1)
            places = own * TOK + tile * TILE + lax.rem(column, TILE)

            def step(is_masked, key_block, carry):
                top, total = carry
                start = pl.multiple_of(key_block * TILE, TILE)
                scores = dot32(k_nat[group, pl.ds(start, TILE), :], queries)
                if is_masked:
                    scores = masked(scores, key_block, begins, places)
                new_top = jnp.maximum(top, jnp.max(scores, axis=0, keepdims=True))
                probs = jnp.exp(scores - new_top).astype(jnp.bfloat16)
                total = total * jnp.exp(top - new_top) + dot32(v_ext[group, key_block], probs)
                return (new_top, total)

            carry = (
                jnp.full((1, COLS), masked_score, jnp.float32),
                jnp.zeros((HEAD_DIM + 16, COLS), jnp.float32),
            )
            for low, high, is_masked in key_ranges(info, tile):
                carry = lax.fori_loop(low, high, partial(step, is_masked), carry)
            top, total = carry
            weight = total[HEAD_DIM : HEAD_DIM + 1, :]
            mixed = (total[:HEAD_DIM, :] / weight).astype(jnp.bfloat16)
            log_total = top + jnp.log(weight)
            for head in range(GROUPS):
                o_ref[group, head, :, tile * TILE : (tile + 1) * TILE] = mixed[
                    :, head * TILE : (head + 1) * TILE
                ]
                lse_ref[group, head, :, tile * TILE : (tile + 1) * TILE] = log_total[
                    :, head * TILE : (head + 1) * TILE
                ]
        return unused

    lax.fori_loop(0, KV_HEADS, one_group, 0)


def backward_kernel(
    info, q_ref, kv_ref, begin_ref, o_ref, lse_ref, do_ref, cos_ref, sin_ref,
    dq_ref, dkv_ref, k_nat, v_nat, k_tall, dk_ref, dv_ref,
):
    own = info[0]
    for block in range(4):

        @pl.when(block <= own)
        def _():
            rows = slice(TOK * block, TOK * (block + 1))
            for group in range(KV_HEADS):
                low = HEAD_DIM * group
                k_nat[group, rows, :] = kv_ref[block, low : low + HEAD_DIM, :].T
                for part in range(TOK // TILE):
                    k_tall[group, block * (TOK // TILE) + part] = kv_ref[
                        block, low : low + HEAD_DIM, part * TILE : (part + 1) * TILE
                    ]
                low = low + KV_WIDTH
                v_nat[group, rows, :] = kv_ref[block, low : low + HEAD_DIM, :].T
                dk_ref[group, rows, :] = jnp.zeros((TOK, HEAD_DIM), jnp.float32)
                dv_ref[group, rows, :] = jnp.zeros((TOK, HEAD_DIM), jnp.float32)

    def one_group(group, unused):
        for tile in range(TOK // TILE):
            queries = tile_heads(q_ref, group, tile)
            upstream = tile_heads(do_ref, group, tile)
            mixed = tile_heads(o_ref, group, tile)
            log_total = tile_heads(lse_ref, group, tile)
            delta = jnp.sum(
                upstream.astype(jnp.float32) * mixed.astype(jnp.float32), axis=0, keepdims=True
            )
            queries_nat = queries.T
            upstream_nat = upstream.T
            begins = tile_row(begin_ref[...], tile)
            column = lax.broadcasted_iota(jnp.int32, (1, COLS), 1)
            places = own * TOK + tile * TILE + lax.rem(column, TILE)

            def step(is_masked, key_block, dq):
                start = pl.multiple_of(key_block * TILE, TILE)
                rows = pl.ds(start, TILE)
                scores = dot32(k_nat[group, rows, :], queries)
                if is_masked:
                    scores = masked(scores, key_block, begins, places)
                probs = jnp.exp(scores - log_total)
                grad_probs = dot32(v_nat[group, rows, :], upstream)
                grad_scores = (probs * (grad_probs - delta)).astype(jnp.bfloat16)
                dv_ref[group, rows, :] += dot32(probs.astype(jnp.bfloat16), upstream_nat)
                dk_ref[group, rows, :] += dot32(grad_scores, queries_nat)
                return dq + dot32(k_tall[group, key_block], grad_scores)

            dq = jnp.zeros((HEAD_DIM, COLS), jnp.float32)
            for low, high, is_masked in key_ranges(info, tile):
                dq = lax.fori_loop(low, high, partial(step, is_masked), dq)
            dq = dq * 0.125
            half_width = HEAD_DIM // 2
            cosine = tile_row(cos_ref[...], tile)
            sine = tile_row(sin_ref[...], tile)
            former, latter = dq[:half_width], dq[half_width:]
            turned = jnp.concatenate(
                [former * cosine + latter * sine, latter * cosine - former * sine], axis=0
            ).astype(jnp.bfloat16)
            for head in range(GROUPS):
                dq_ref[group, head, :, tile * TILE : (tile + 1) * TILE] = turned[
                    :, head * TILE : (head + 1) * TILE
                ]
        return unused

    lax.fori_loop(0, KV_HEADS, one_group, 0)
    for block in range(4):
        rows = slice(TOK * block, TOK * (block + 1))

        @pl.when(block <= own)
        def _():
            for group in range(KV_HEADS):
                low = HEAD_DIM * group
                dkv_ref[block, low : low + HEAD_DIM, :] = dk_ref[group, rows, :].T.astype(
                    jnp.bfloat16
                )
                low = low + KV_WIDTH
                dkv_ref[block, low : low + HEAD_DIM, :] = dv_ref[group, rows, :].T.astype(
                    jnp.bfloat16
                )

        @pl.when(block > own)
        def _():
            dkv_ref[block] = jnp.zeros((2 * KV_WIDTH, TOK), jnp.bfloat16)


def vmem():
    return pl.BlockSpec(memory_space=pltpu.VMEM)


def smem():
    return pl.BlockSpec(memory_space=pltpu.SMEM)


kernel_params = pltpu.CompilerParams(vmem_limit_bytes=48 * 1024 * 1024)
heads_shape = (KV_HEADS, GROUPS, HEAD_DIM, TOK)


def attend_forward(info, queries, keyvals, begins):
    return pl.pallas_call(
        forward_kernel,
        out_shape=(
            jax.ShapeDtypeStruct(heads_shape, jnp.bfloat16),
            jax.ShapeDtypeStruct((KV_HEADS, GROUPS, 1, TOK), jnp.float32),
        ),
        in_specs=[smem(), vmem(), vmem(), vmem()],
        out_specs=(vmem(), vmem()),
        scratch_shapes=[
            pltpu.VMEM((KV_HEADS, 4 * TOK, HEAD_DIM), jnp.bfloat16),
            pltpu.VMEM((KV_HEADS, 4 * TOK // TILE, HEAD_DIM + 16, TILE), jnp.bfloat16),
        ],
        compiler_params=kernel_params,
        cost_estimate=pl.CostEstimate(
            flops=4 * 9 * 64 * TOK * 2048, bytes_accessed=4000000, transcendentals=9 * TOK * 2048
        ),
        name="attend_forward",
    )(info, queries, keyvals, begins)


def attend_back(info, queries, keyvals, begins, mixed, log_total, grad_mixed, cosine, sine):
    return pl.pallas_call(
        backward_kernel,
        out_shape=(
            jax.ShapeDtypeStruct(heads_shape, jnp.bfloat16),
            jax.ShapeDtypeStruct((4, 2 * KV_WIDTH, TOK), jnp.bfloat16),
        ),
        in_specs=[smem()] + [vmem()] * 8,
        out_specs=(vmem(), vmem()),
        scratch_shapes=[
            pltpu.VMEM((KV_HEADS, 4 * TOK, HEAD_DIM), jnp.bfloat16),
            pltpu.VMEM((KV_HEADS, 4 * TOK, HEAD_DIM), jnp.bfloat16),
            pltpu.VMEM((KV_HEADS, 4 * TOK // TILE, HEAD_DIM, TILE), jnp.bfloat16),
            pltpu.VMEM((KV_HEADS, 4 * TOK, HEAD_DIM), jnp.float32),
            pltpu.VMEM((KV_HEADS, 4 * TOK, HEAD_DIM), jnp.float32),
        ],
        compiler_params=kernel_params,
        cost_estimate=pl.CostEstimate(
            flops=10 * 9 * 64 * TOK * 2048, bytes_accessed=8000000, transcendentals=9 * TOK * 2048
        ),
        name="attend_back",
    )(info, queries, keyvals, begins, mixed, log_total, grad_mixed, cosine, sine)


def quarter_matrix(quarter, flat):
    def mixed_case(flat):
        square = D * D
        narrow = D * KV_WIDTH
        return jnp.concatenate(
            [
                flat[:square].reshape(D, D),
                flat[square : square + narrow].reshape(D, KV_WIDTH),
                flat[square + narrow : square + 2 * narrow].reshape(D, KV_WIDTH),
                flat[square + 2 * narrow :].reshape(D, D),
            ],
            axis=1,
        )

    def wide_case(flat):
        return flat.reshape(D, FF)

    def tall_case(flat):
        return flat.reshape(FF, D).T

    return lax.switch(quarter, [mixed_case, wide_case, wide_case, tall_case], flat)


def newton(matrix, scale):
    current = matrix / (jnp.sqrt(jnp.sum(matrix * matrix)) + frobenius_epsilon)
    for iteration in range(NS_STEPS):
        low = current.astype(jnp.bfloat16)
        square = lax.dot_general(
            low, low, (((1,), (1,)), ((), ())), preferred_element_type=jnp.float32
        )
        square_low = square.astype(jnp.bfloat16)
        mixer = newton_second * square + newton_third * dot32(square_low, square_low)
        current = newton_first * current + dot32(mixer.astype(jnp.bfloat16), low)
    return current * (0.2 * math.sqrt(scale))


def own_update(quarter, within, shard_length, gradient, total):
    square = D * D
    narrow = D * KV_WIDTH

    def square_case(gradient, total):
        second = within >= square + 2 * narrow
        column = jnp.where(second, FF - D, 0)
        row = (within - jnp.where(second, square + 2 * narrow, 0)) // D
        rows = shard_length // D
        part = lax.dynamic_slice(total, (0, column), (D, D))
        result = newton(part, D)
        return (
            lax.dynamic_slice(gradient, (row, column), (rows, D)).reshape(-1),
            lax.dynamic_slice(result, (row, 0), (rows, D)).reshape(-1),
        )

    def narrow_case(gradient, total):
        second = within >= square + narrow
        column = D + jnp.where(second, KV_WIDTH, 0)
        row = (within - square - jnp.where(second, narrow, 0)) // KV_WIDTH
        rows = shard_length // KV_WIDTH
        part = lax.dynamic_slice(total, (0, column), (D, KV_WIDTH))
        result = newton(part.T, D).T
        return (
            lax.dynamic_slice(gradient, (row, column), (rows, KV_WIDTH)).reshape(-1),
            lax.dynamic_slice(result, (row, 0), (rows, KV_WIDTH)).reshape(-1),
        )

    def wide_case(gradient, total):
        row = within // FF
        rows = shard_length // FF
        result = newton(total, FF)
        return (
            lax.dynamic_slice(gradient, (row, 0), (rows, FF)).reshape(-1),
            lax.dynamic_slice(result, (row, 0), (rows, FF)).reshape(-1),
        )

    def tall_case(gradient, total):
        column = within // D
        columns = shard_length // D
        result = newton(total, FF)
        return (
            lax.dynamic_slice(gradient, (0, column), (D, columns)).T.reshape(-1),
            lax.dynamic_slice(result, (0, column), (D, columns)).T.reshape(-1),
        )

    is_narrow = (within >= square) & (within < square + 2 * narrow)
    kind = jnp.where(quarter == 0, jnp.where(is_narrow, 1, 0), jnp.where(quarter == 3, 3, 2))
    return lax.switch(
        kind, [square_case, narrow_case, wide_case, tall_case], gradient, total
    )


def cut(matrix):
    shaped = matrix.reshape(ROW_CUT, D // ROW_CUT, COL_CUT, FF // COL_CUT)
    return shaped.transpose(0, 2, 1, 3).reshape(ROW_CUT * COL_CUT, D // ROW_CUT, FF // COL_CUT)


def uncut(pieces):
    shaped = pieces.reshape(ROW_CUT, COL_CUT, D // ROW_CUT, FF // COL_CUT)
    return shaped.transpose(0, 2, 1, 3).reshape(D, FF)


def attention_info(ctx, begins):
    fields = [ctx]
    for tile in range(TOK // TILE):
        last = ctx * (TOK // TILE) + tile
        first = begins[tile * TILE] // TILE
        full = jnp.minimum(last, (begins[(tile + 1) * TILE - 1] + TILE - 1) // TILE)
        fields = fields + [first, full, last]
    return jnp.stack(fields).astype(jnp.int32)


def per_device(tokens, lengths, weights, momentum, norm_gains, gain_first, gain_second, cotangent):
    micro_count = tokens.shape[0]
    ctx = lax.axis_index("ctx")
    quarter = lax.axis_index("quarter")
    reps = lax.axis_size("rep")
    shard_length = weights.shape[0]
    within = lax.axis_index(("rep", "half", "ctx")) * shard_length

    full_weights = lax.all_gather(weights.astype(jnp.bfloat16), EVERY, axis=0, tiled=True)
    square, narrow, broad = D * D, D * KV_WIDTH, D * FF
    places_in = [0, square, square + narrow, square + 2 * narrow]
    w_qkv = jnp.concatenate(
        [
            full_weights[:square].reshape(D, D),
            full_weights[places_in[1] : places_in[2]].reshape(D, KV_WIDTH),
            full_weights[places_in[2] : places_in[3]].reshape(D, KV_WIDTH),
        ],
        axis=1,
    )
    w_out = full_weights[places_in[3] : places_in[3] + square].reshape(D, D)
    w_gate = full_weights[broad : 2 * broad].reshape(D, FF)
    w_up = full_weights[2 * broad : 3 * broad].reshape(D, FF)
    w_down = full_weights[3 * broad :].reshape(FF, D)

    own_places = ctx * TOK + jnp.arange(TOK, dtype=jnp.int32)
    inputs = tokens.astype(jnp.float32).reshape(-1, D)
    back = cotangent.reshape(-1, D)
    normed = normalize(inputs, norm_gains[0]).astype(jnp.bfloat16)
    infos, begin_rows, tables = [], [], []
    for micro in range(micro_count):
        offsets, begins = layout(lengths[micro, 0], own_places)
        infos.append(attention_info(ctx, begins))
        begin_rows.append(begins.reshape(1, TOK))
        tables.append(rope_tables(offsets))

    queries, keyvals, mixed, log_totals = [], [], [], []
    for micro in range(micro_count):
        rows = normed[micro * TOK : (micro + 1) * TOK]
        linear = jnp.einsum("de,td->et", w_qkv, rows, preferred_element_type=jnp.float32)
        turned = rotate_columns(linear[: D + KV_WIDTH], *tables[micro])
        scaled = turned[:D].astype(jnp.bfloat16) * jnp.bfloat16(0.125)
        queries.append(scaled.reshape(heads_shape))
        own_keyvals = jnp.concatenate([turned[D:], linear[D + KV_WIDTH :]], axis=0)
        keyvals.append(
            lax.all_gather(own_keyvals.astype(jnp.bfloat16), "ctx", axis=0, tiled=False)
        )
    for micro in range(micro_count):
        mixed_one, log_total = attend_forward(
            infos[micro], queries[micro], keyvals[micro], begin_rows[micro]
        )
        mixed.append(mixed_one)
        log_totals.append(log_total)
    mixed_all = jnp.concatenate([part.reshape(D, TOK) for part in mixed], axis=1)
    hidden_state = inputs + jnp.einsum(
        "et,ed->td", mixed_all, w_out, preferred_element_type=jnp.float32
    )
    normed_two = normalize(hidden_state, norm_gains[1]).astype(jnp.bfloat16)
    gate = dot32(normed_two, w_gate)
    upward = dot32(normed_two, w_up)
    sigmoid_gate = jax.nn.sigmoid(gate)
    activated = gate * sigmoid_gate
    hidden = (activated * upward).astype(jnp.bfloat16)
    result = hidden_state + dot32(hidden, w_down)
    grad_hidden = jnp.einsum("td,fd->tf", back, w_down, preferred_element_type=jnp.float32)
    grad_gate = (grad_hidden * upward * sigmoid_gate * (1.0 + gate * (1.0 - sigmoid_gate))).astype(
        jnp.bfloat16
    )
    grad_upward = (grad_hidden * activated).astype(jnp.bfloat16)

    def weight_term(left, right):
        return jnp.einsum(
            "td,tf->df", left, right, preferred_element_type=jnp.float32
        ).astype(jnp.bfloat16)

    grad_w_down = weight_term(back, hidden)
    grad_w_gate = weight_term(normed_two, grad_gate)
    grad_w_up = weight_term(normed_two, grad_upward)
    grad_normed_two = jnp.einsum(
        "tf,df->td", grad_gate, w_gate, preferred_element_type=jnp.float32
    ) + jnp.einsum("tf,df->td", grad_upward, w_up, preferred_element_type=jnp.float32)
    grad_state_norm, gain_two_grad = normalize_back(hidden_state, norm_gains[1], grad_normed_two)
    grad_state = back.astype(jnp.float32) + grad_state_norm
    grad_state_low = grad_state.astype(jnp.bfloat16)
    early = jnp.stack([cut(grad_w_gate), cut(grad_w_up), cut(grad_w_down)], axis=1)
    early = lax.psum_scatter(early, PLANE, scatter_dimension=0, tiled=False)
    grad_mixed = jnp.einsum(
        "ed,td->et", w_out, grad_state_low, preferred_element_type=jnp.float32
    ).astype(jnp.bfloat16)
    grad_w_out = jnp.einsum(
        "et,td->ed", mixed_all, grad_state_low, preferred_element_type=jnp.float32
    ).astype(jnp.bfloat16)

    grad_columns = []
    for micro in range(micro_count):
        dq, dkv = attend_back(
            infos[micro],
            queries[micro],
            keyvals[micro],
            begin_rows[micro],
            mixed[micro],
            log_totals[micro],
            grad_mixed[:, micro * TOK : (micro + 1) * TOK].reshape(heads_shape),
            *tables[micro],
        )
        dkv = lax.psum_scatter(dkv, "ctx", scatter_dimension=0, tiled=False)
        cosine, sine = tables[micro]
        dk = rotate_columns(dkv[:KV_WIDTH].astype(jnp.float32), cosine, -sine)
        grad_columns.append(
            jnp.concatenate(
                [dq.reshape(D, TOK), dk.astype(jnp.bfloat16), dkv[KV_WIDTH:]], axis=0
            )
        )
    grad_qkv = jnp.concatenate(grad_columns, axis=1)
    grad_w_qkv = jnp.einsum(
        "td,et->de", normed, grad_qkv, preferred_element_type=jnp.float32
    ).astype(jnp.bfloat16)
    late = cut(jnp.concatenate([grad_w_qkv, grad_w_out], axis=1))
    late = lax.psum_scatter(late, PLANE, scatter_dimension=0, tiled=False)
    grad_normed = jnp.einsum("et,de->td", grad_qkv, w_qkv, preferred_element_type=jnp.float32)
    grad_input_norm, gain_one_grad = normalize_back(inputs, norm_gains[0], grad_normed)
    grad_inputs = grad_state + grad_input_norm

    piece = lax.psum_scatter(
        jnp.concatenate([late[None], early], axis=0), "quarter", scatter_dimension=0, tiled=False
    )
    if reps > 1:
        piece = lax.psum(piece, "rep")
    gradient = uncut(lax.all_gather(piece, PLANE, axis=0, tiled=False))
    old = lax.all_gather(
        momentum.astype(jnp.bfloat16), ("rep", "half", "ctx"), axis=0, tiled=True
    )
    total = momentum_decay * quarter_matrix(quarter, old).astype(jnp.float32) + gradient.astype(
        jnp.float32
    )
    grad_shard, update_shard = own_update(quarter, within, shard_length, gradient, total)
    grad_shard = grad_shard.astype(jnp.float32)
    new_momentum = momentum_decay * momentum + grad_shard
    new_weights = weights * (1.0 - matrix_rate * weight_decay) - matrix_rate * update_shard

    gain_grad = lax.psum(jnp.stack([gain_one_grad, gain_two_grad]), EVERY)
    first_new = first_decay * gain_first + (1.0 - first_decay) * gain_grad
    second_new = second_decay * gain_second + (1.0 - second_decay) * gain_grad * gain_grad
    debiased_first_moment = first_new / (1.0 - first_decay**ADAM_STEP)
    corrected_second = second_new / (1.0 - second_decay**ADAM_STEP)
    new_gains = norm_gains * (
        1.0 - gain_rate * weight_decay
    ) - gain_rate * debiased_first_moment / (jnp.sqrt(corrected_second) + adam_epsilon)
    return (
        result.reshape(tokens.shape),
        grad_inputs.reshape(tokens.shape),
        grad_shard,
        new_momentum,
        new_weights,
        first_new,
        second_new,
        new_gains,
    )


def solution(mesh):
    devices = mesh.devices
    count = devices.size
    context = mesh.shape["ctx"]
    split = Mesh(
        devices.reshape(4, count // (8 * context), 2, context), ("quarter", "rep", "half", "ctx")
    )
    rows = P(None, EVERY, None)
    flat = P(EVERY)
    placed = (rows, P(None, ("quarter", "rep", "half"), None), flat, flat, P(), P(), P(), rows)
    return jax.shard_map(
        per_device,
        mesh=split,
        in_specs=placed,
        out_specs=(rows, rows, flat, flat, flat, P(), P(), P()),
        check_vma=False,
    )
```

time: 1450 us -> 709 us (0.49)
  the two profiles are of different devices: /device:TPU:8 before, /device:TPU:26 now
where the time goes in v1:
time: 709 us; the launch traced here: 700 us
  waiting for transfers between devices  319 us (45%)
  matrix products  125 us (18%)
  local copies, waits for them, and re-layouts  97.1 us (14%)
  blocking collectives  47.6 us (7%)
  Pallas kernels  31 us (4%)
  other arithmetic  28.2 us (4%)
  between operations  28.2 us (4%)
  loops' own time  23.1 us (3%)
    unnamed x11, waiting for transfers between devices  89.4 us
    reduce_scatter x2, waiting for transfers between devices, per_device(): dkv = lax.psum_scatter(dkv, 'ctx', scatter_dimension=0, tiled=False)  70.1 us
    all_gather x1, waiting for transfers between devices, per_device(): lax.all_gather(weights.astype(jnp.bfloat16), EVERY, axis=0, tiled=True)  66.7 us
    psum x1, blocking collectives, per_device(): gain_grad = lax.psum(jnp.stack([gain_one_grad, gain_two_grad]), EVERY)  47.6 us
    dot_general x8, matrix products, dot32(): return jnp.dot(left, right, preferred_element_type=jnp.float32)  45.8 us
    reduce_scatter x1, waiting for transfers between devices, per_device(): late = lax.psum_scatter(late, PLANE, scatter_dimension=0, tiled=False)  41.3 us
    all_gather x1, waiting for transfers between devices, per_device(): lax.all_gather(momentum.astype(jnp.bfloat16), ('rep', 'half', 'ctx'), axi...  29.4 us
    reshape x8, local copies, waits for them, and re-layouts, cut(): shaped = matrix.reshape(ROW_CUT, D // ROW_CUT, COL_CUT, FF // COL_CUT)  27.3 us
  transfers between devices with their start and end apart: 10, of which 7 were waited for; matrix products, arithmetic and copies ran while one was open for 17% of the time, Pallas kernels for 2%

profile of v1, /device:TPU:26, one launch (start us, length us, event | category | flops | bytes accessed | tf_op | source)
XLA Modules:
  0.0 699.8 jit_solution(10438165502271458981)
XLA Ops:
  7.2 1.7 convert_element_type.413
  15.0 1.9 multiply_convert_fusion.4
  16.9 66.7 %all-gather.6.cloned.1.call-done = bf16[3538944]{0:T(1024)(128)(2,1)} async-done(((bf16[110592]{0:T(1024)(128)(2,1)}), bf16[3538944]{0:T(1024)(128)(2,1)}) %all-gather.6.cloned.1.call-update) | async-done | bytes 7077904 | tf_op jit(solution)/shard_map/all_gather | solution.py:428
  83.6 2.2 fusion.255
  105.6 2.5 copy.91
  108.3 2.2 fusion.231
  112.5 4.8 fusion.254
  117.2 2.4 slice.303
  119.6 4.5 slice.308
  124.2 4.4 slice.306
  128.6 2.8 slice.310
  134.0 6.3 attend_forward.2
  141.8 6.2 attend_forward.3
  149.5 2.1 copy-done.26
  151.6 2.7 fusion.264
  154.3 4.6 fusion.263
  158.9 9.2 %multiply_convert_fusion = (bf16[1024,1536]{1,0:T(8,128)(2,1)S(1)}, bf16[1024,1536]{1,0:T(8,128)(2,1)}, bf16[1024,1536]{1,0:T(8,128)(2,1)}) fusion(f32[1024,1536]{1,0:T(8,128)} %fusion.263, f32[1024,1536]{1,0:T(8,128)S(1)} %fusion.264, bf16[1024,576]{0,1:T(8,128)(2,1)S(1)} %bitcast.216, bf16[1536,576]{1,0:T(8,128)(2,1)S(1)} %copy-done.25), kind=kOutput, calls=%fused_computation.258 | convolution fusion | flops 1835532288 | bytes 24969216 | tf_op jit(solution)/shard_map/td,fd->tf/dot_general | solution.py:483
  168.1 5.0 fusion.265
  173.2 2.9 multiply_reduce_fusion.4
  179.5 9.1 %attend_back.2 = (bf16[3,3,64,512]{3,2,1,0:T(8,128)(2,1)S(1)}, bf16[4,384,512]{2,1,0:T(8,128)(2,1)}) custom-call(s32[7]{0:T(128)S(1)} %stack.83.info, bf16[3,3,64,512]{3,2,1,0:T(8,128)(2,1)S(1)} %bitcast.173, bf16[4,384,512]{2,1,0:T(8,128)(2,1)S(1)} %copy-done.1, s32[1,512]{1,0:T(1,128)S(1)} %bitcast.183, ...), custom_call_target="tpu_custom_call" | custom-call | flops 6039797760 | bytes 8000000 | tf_op jit(solution)/shard_map/attend_back/pallas_call | solution.py:288
  191.0 9.3 %attend_back.3 = (bf16[3,3,64,512]{3,2,1,0:T(8,128)(2,1)S(1)}, bf16[4,384,512]{2,1,0:T(8,128)(2,1)}) custom-call(s32[7]{0:T(128)S(1)} %stack.89.info, bf16[3,3,64,512]{3,2,1,0:T(8,128)(2,1)S(1)} %bitcast.171, bf16[4,384,512]{2,1,0:T(8,128)(2,1)S(1)} %copy-done.3, s32[1,512]{1,0:T(1,128)S(1)} %bitcast.181, ...), custom_call_target="tpu_custom_call" | custom-call | flops 6039797760 | bytes 8000000 | tf_op jit(solution)/shard_map/attend_back/pallas_call | solution.py:288
  200.4 5.5 convolution_convert_fusion.2
  205.9 4.8 reshape.655
  210.7 3.0 copy.70
  213.7 5.1 convolution_convert_fusion.1
  218.8 4.8 reshape.656
  223.7 3.0 copy.71
  226.7 5.1 fusion.228
  231.8 4.8 reshape.657
  236.7 1.8 copy.72
  239.2 3.0 pad_maximum_fusion
  242.2 3.7 convolution_convert_fusion.5
  245.9 35.5 %reduce-scatter.8.cloned.1.call-done = bf16[1,384,512]{2,1,0:T(8,128)(2,1)} async-done(((bf16[4,384,512]{2,1,0:T(8,128)(2,1)}), bf16[1,384,512]{2,1,0:T(8,128)(2,1)}) %reduce-scatter.8.cloned.1.call-update) | async-done | bytes 393232 | tf_op jit(solution)/shard_map/reduce_scatter | solution.py:524
  282.5 34.6 %reduce-scatter.10.cloned.1.call-done = bf16[1,384,512]{2,1,0:T(8,128)(2,1)} async-done(((bf16[4,384,512]{2,1,0:T(8,128)(2,1)}), bf16[1,384,512]{2,1,0:T(8,128)(2,1)}) %reduce-scatter.10.cloned.1.call-update) | async-done | bytes 393232 | tf_op jit(solution)/shard_map/reduce_scatter | solution.py:524
  319.0 9.6 %convolution_convert_fusion.3 = bf16[576,960]{1,0:T(8,128)(2,1)S(1)} fusion(bf16[1024,576]{0,1:T(8,128)(2,1)S(1)} %copy-done.33, bf16[192,512]{1,0:T(8,128)(2,1)S(1)} %get-tuple-element.258, bf16[192,512]{1,0:T(8,128)(2,1)S(1)} %bitcast.234, bf16[576,512]{1,0:T(8,128)(2,1)S(1)} %bitcast.186, bf16[192,512]{1,0:T(8,128)(2,1)S(1)} %get-tuple-element.256, ...), kind=kOutput, calls=%fused_computation.289 | convolution fusion | flops 1144811520 | bytes 4251648 | tf_op jit(solution)/shard_map/td,et->de/dot_general | solution.py:533
  329.0 2.0 reshape.653
  331.0 2.9 copy.69
  335.2 89.2 %all-reduce.3.cloned.1.call-done = bf16[8,3,144,768]{3,2,0,1:T(8,128)(2,1)} async-done(((bf16[8,3,144,768]{3,2,0,1:T(8,128)(2,1)}), bf16[8,3,144,768]{3,2,0,1:T(8,128)(2,1)}) %all-reduce.3.cloned.1.call-update) | async-done | bytes 5308432
  424.4 1.8 dynamic-slice_bitcast_fusion
  426.2 41.3 %reduce-scatter.12.cloned.1.call-done = bf16[1,144,768]{2,1,0:T(8,128)(2,1)} async-done(((bf16[8,144,768]{2,1,0:T(8,128)(2,1)}), bf16[1,144,768]{2,1,0:T(8,128)(2,1)}) %reduce-scatter.12.cloned.1.call-update) | async-done | bytes 221200 | tf_op jit(solution)/shard_map/reduce_scatter | solution.py:537
  467.6 2.0 pad_maximum_fusion.4
  470.4 22.4 %reduce-scatter.14.cloned.1.call-done = bf16[1,144,768]{2,1,0:T(8,128)(2,1)} async-done(((bf16[4,144,768]{2,1,0:T(8,128)(2,1)}), bf16[1,144,768]{2,1,0:T(8,128)(2,1)}) %reduce-scatter.14.cloned.1.call-update) | async-done | bytes 221200 | tf_op jit(solution)/shard_map/reduce_scatter | solution.py:542
  493.4 29.4 %all-gather.12.cloned.1.call-done = bf16[884736]{0:T(1024)(128)(2,1)} async-done(((bf16[110592]{0:T(1024)(128)(2,1)}), bf16[884736]{0:T(1024)(128)(2,1)}) %all-gather.12.cloned.1.call-update) | async-done | bytes 1769488 | tf_op jit(solution)/shard_map/all_gather | solution.py:548
  522.9 10.4 %conditional.4 = (f32[576,1536]{1,0:T(8,128)}) conditional(s32[]{:T(128)} %clamp.7, bf16[884736]{0:T(1024)(128)(2,1)} %all-gather.12.cloned.1.call-done, bf16[884736]{0:T(1024)(128)(2,1)} %all-gather.12.cloned.1.call-done, bf16[884736]{0:T(1024)(128)(2,1)} %all-gather.12.cloned.1.call-done, ...), branch_computations={%region_10.11_spmd, %region_11.12_spmd, %region_12.13_spmd, %regio... | conditional | flops 884736 | bytes 15925256 | solution.py:331
  522.9 4.5 reshape.667
  527.4 5.4 copy.61
  533.9 4.6 convolution_add_fusion.3
  541.6 1.7 multiply_reduce_fusion.5
  546.2 47.6 %psum.7 = f32[2,576]{1,0:T(2,128)S(1)} all-reduce(f32[2,576]{1,0:T(2,128)} %pad_maximum_fusion.11), channel_id=1, replica_groups=mesh['quarter'=4,'rep'=1,'half'=2,'ctx'=4] {'quarter','rep','half','ctx'}, use_global_device_ids=true, to_apply=%region_27.28 | all-reduce | flops 1152 | bytes 9216 | tf_op jit(solution)/shard_map/psum | solution.py:559
  595.1 93.7 %conditional.5 = (f32[110592]{0:T(1024)}, f32[110592]{0:T(1024)}) conditional(s32[]{:T(128)} %clamp.6, (f32[576,1536]{1,0:T(8,128)S(1)}, bf16[4,144,2,768]{3,1,2,0:T(8,128)(2,1)}, s32[]{:T(128)}) %tuple.170, (f32[576,1536]{1,0:T(8,128)S(1)}, bf16[4,144,2,768]{3,1,2,0:T(8,128)(2,1)}, s32[]{:T(128)}) %tuple.171, ...), branch_computations={%region_17.19_spmd, %region_19.21_spmd, %region_21.23_spmd, %regio... | conditional | flops 12142891008 | bytes 137355536
  616.9 2.8 copy.77
  623.5 5.0 fusion.189
  628.5 7.6 %multiply_add_fusion.13 = f32[576,1536]{1,0:T(8,128)} fusion(f32[576,576]{1,0:T(8,128)} %fusion.189, f32[]{:T(128)S(6)} %add.356, bf16[576,1536]{1,0:T(8,128)(2,1)} %bitcast.200, f32[576,1536]{1,0:T(8,128)S(1)} %get-tuple-element.111), kind=kOutput, calls=%fused_computation.201 | convolution fusion | flops 1412812800 | bytes 10174468 | tf_op jit(solution)/shard_map/cond/branch_3_fun/dot_general | solution.py:83
  636.1 6.0 fusion.186
  642.1 6.5 multiply_add_fusion.12
  648.6 6.0 fusion.183
  654.6 6.5 multiply_add_fusion.11
  661.1 6.0 fusion.180
  667.1 6.6 multiply_add_fusion.10
  673.8 2.8 fusion.177
  676.5 6.6 fusion.175
  683.2 1.8 fusion.212
  688.8 2.0 multiply_add_fusion.16
  690.8 2.0 multiply_subtract_fusion.2
  (207 shorter events, 47.3 us)
Async XLA Ops:
  7.2 76.5 %all-gather.6.cloned.1.call-start = ((), (), s32[]{:S(2)}) async-start(), calls=%async_computation.4 | async-start | bytes 7299072 | tf_op jit(solution)/shard_map/all_gather | solution.py:428
  9.0 123.6 %all-gather.8.cloned.1.call-start = ((), (), s32[]{:S(2)}) async-start(), calls=%async_computation.5 | async-start | bytes 1966080 | tf_op jit(solution)/shard_map/all_gather | solution.py:464
  11.6 1.7 copy-start.17
  11.7 2.0 copy-start.57
  11.7 2.0 copy-start.59
  16.9 72.0 %copy-start.31 = (bf16[1024,576]{0,1:T(8,128)(2,1)}, bf16[1024,576]{0,1:T(8,128)(2,1)S(1)}, u32[]{:S(2)}) copy-start(bf16[1024,576]{0,1:T(8,128)(2,1)S(1)} %multiply_convert_fusion.4) | copy-start | bytes 3538948
  87.4 2.3 copy-start.38
  88.7 19.5 %copy-start.40 = (bf16[576,192]{1,0:T(8,128)(2,1)}, bf16[576,192]{1,0:T(8,128)(2,1)S(1)}, u32[]{:S(2)}) copy-start(bf16[576,192]{1,0:T(8,128)(2,1)S(1)} %slice.279) | copy-start | bytes 663556
  91.2 17.1 %copy-start.32 = (bf16[1024,576]{0,1:T(8,128)(2,1)S(1)}, bf16[1024,576]{0,1:T(8,128)(2,1)}, u32[]{:S(2)}) copy-start(bf16[1024,576]{0,1:T(8,128)(2,1)} %copy-done.31) | copy-start | bytes 3538948
  91.2 17.1 %copy-start.43 = (bf16[576,192]{1,0:T(8,128)(2,1)S(1)}, bf16[576,192]{1,0:T(8,128)(2,1)}, u32[]{:S(2)}) copy-start(bf16[576,192]{1,0:T(8,128)(2,1)} %copy-done.42) | copy-start | bytes 663556
  92.0 48.4 %all-gather.10.cloned.1.call-start = ((), (), s32[]{:S(2)}) async-start(), calls=%async_computation.6 | async-start | bytes 1966080 | tf_op jit(solution)/shard_map/all_gather | solution.py:464
  110.8 0.7 copy-start.21
  112.4 169.0 %reduce-scatter.8.cloned.1.call-start = ((), (), s32[]{:S(2)}) async-start(), calls=%async_computation.7 | async-start | bytes 1966080 | tf_op jit(solution)/shard_map/reduce_scatter | solution.py:524
  131.4 1.0 copy-start.22
  132.6 1.4 copy-start
  140.4 1.4 copy-start.2
  141.8 6.2 copy-start.7
  141.8 6.3 copy-start.23
  149.2 26.9 %copy-start.9 = (f32[1024,576]{0,1:T(8,128)}, f32[1024,576]{0,1:T(8,128)S(1)}, u32[]{:S(2)}) copy-start(f32[1024,576]{0,1:T(8,128)S(1)} %get-tuple-element.283) | copy-start | bytes 7077892
  149.3 2.3 copy-start.26
  151.6 2.7 copy-start.34
  151.6 2.7 copy-start.27
  154.3 4.7 copy-start.18
  154.3 4.7 copy-start.25
  168.1 5.1 copy-start.61
  176.7 1.4 copy-start.11
  178.1 1.4 copy-start.1
  188.7 0.9 copy-start.4
  189.6 127.6 %reduce-scatter.10.cloned.1.call-start = ((), (), s32[]{:S(2)}) async-start(), calls=%async_computation.8 | async-start | bytes 1966080 | tf_op jit(solution)/shard_map/reduce_scatter | solution.py:524
  189.6 1.4 copy-start.3
  200.3 224.1 %all-reduce.3.cloned.1.call-start = ((), (), s32[]{:S(2)}) async-start(), calls=%async_computation.13 | async-start | bytes 10616832
  210.7 3.0 copy-start.35
  223.7 3.0 copy-start.19
  236.7 2.0 copy-start.15
  236.7 2.5 copy-start.16
  242.2 225.4 %reduce-scatter.12.cloned.1.call-start = ((), (), s32[]{:S(2)}) async-start(), calls=%async_computation.10 | async-start | bytes 1990656 | tf_op jit(solution)/shard_map/reduce_scatter | solution.py:537
  245.9 72.3 %copy-start.46 = (f32[32,512]{1,0:T(8,128)S(1)}, f32[32,512]{1,0:T(8,128)}, u32[]{:S(2)}) copy-start(f32[32,512]{1,0:T(8,128)} %get-tuple-element.261) | copy-start | bytes 196612
  245.9 72.5 %copy-start.45 = (f32[32,512]{1,0:T(8,128)S(1)}, f32[32,512]{1,0:T(8,128)}, u32[]{:S(2)}) copy-start(f32[32,512]{1,0:T(8,128)} %get-tuple-element.281) | copy-start | bytes 196612
  282.4 36.0 %copy-start.51 = (bf16[192,512]{1,0:T(8,128)(2,1)}, bf16[192,512]{1,0:T(8,128)(2,1)S(1)}, u32[]{:S(2)}) copy-start(bf16[192,512]{1,0:T(8,128)(2,1)S(1)} %get-tuple-element.256) | copy-start | bytes 589828
  282.5 36.5 %copy-start.5 = (bf16[3,3,64,512]{3,2,1,0:T(8,128)(2,1)S(1)}, bf16[3,3,64,512]{3,2,1,0:T(8,128)(2,1)}, u32[]{:S(2)}) copy-start(bf16[3,3,64,512]{3,2,1,0:T(8,128)(2,1)} %copy-done.4) | copy-start | bytes 1769476
  282.5 36.5 %copy-start.33 = (bf16[1024,576]{0,1:T(8,128)(2,1)S(1)}, bf16[1024,576]{0,1:T(8,128)(2,1)}, u32[]{:S(2)}) copy-start(bf16[1024,576]{0,1:T(8,128)(2,1)} %copy-done.31) | copy-start | bytes 3538948
  318.2 10.4 %copy-start.53 = (bf16[192,512]{1,0:T(8,128)(2,1)}, bf16[192,512]{1,0:T(8,128)(2,1)S(1)}, u32[]{:S(2)}) copy-start(bf16[192,512]{1,0:T(8,128)(2,1)S(1)} %get-tuple-element.258) | copy-start | bytes 589828
  318.5 10.1 %copy-start.49 = (bf16[3,2,32,512]{3,2,1,0:T(8,128)(2,1)}, bf16[3,2,32,512]{3,2,1,0:T(8,128)(2,1)S(1)}, u32[]{:S(2)}) copy-start(bf16[3,2,32,512]{3,2,1,0:T(8,128)(2,1)S(1)} %pad_maximum_fusion.10) | copy-start | bytes 589828
  319.0 9.6 %copy-start.37 = (bf16[576,576]{1,0:T(8,128)(2,1)S(1)}, bf16[576,576]{1,0:T(8,128)(2,1)}, u32[]{:S(2)}) copy-start(bf16[576,576]{1,0:T(8,128)(2,1)} %convolution_convert_fusion.5) | copy-start | bytes 1990660
  333.9 158.8 %reduce-scatter.14.cloned.1.call-start = ((), (), s32[]{:S(2)}) async-start(), calls=%async_computation.11 | async-start | bytes 1105920 | tf_op jit(solution)/shard_map/reduce_scatter | solution.py:542
  424.4 45.2 %copy-start.28 = (f32[110592]{0:T(1024)S(1)}, f32[110592]{0:T(1024)}, u32[]{:S(2)}) copy-start(f32[110592]{0:T(1024)} %param.19) | copy-start | bytes 1327108
  469.6 53.3 %all-gather.12.cloned.1.call-start = ((), (), s32[]{:S(2)}) async-start(), calls=%async_computation.9 | async-start | bytes 1990656 | tf_op jit(solution)/shard_map/all_gather | solution.py:548
  470.4 124.7 %all-gather.14.cloned.1.call-start = ((), (), s32[]{:S(2)}) async-start(), calls=%async_computation.12 | async-start | bytes 1990656 | tf_op jit(solution)/shard_map/all_gather | solution.py:547
  493.4 40.5 %copy-start.10 = (f32[1024,576]{0,1:T(8,128)S(1)}, f32[1024,576]{0,1:T(8,128)}, u32[]{:S(2)}) copy-start(f32[1024,576]{0,1:T(8,128)} %copy-done.9) | copy-start | bytes 7077892
  538.6 2.5 copy-start.8
  538.6 2.7 copy-start.39
  538.6 2.7 copy-start.41
  538.6 2.8 copy-start.44
  538.6 2.8 copy-start.48
  538.6 2.9 copy-start.50
  538.6 2.9 copy-start.52
  538.6 3.0 copy-start.54
  541.6 1.7 copy-start.12
  541.6 1.7 copy-start.58
  543.9 51.2 %copy-start.6 = (f32[576,1536]{1,0:T(8,128)S(1)}, f32[576,1536]{1,0:T(8,128)}, u32[]{:S(2)}) copy-start(f32[576,1536]{1,0:T(8,128)} %get-tuple-element.300) | copy-start | bytes 10616836
  620.0 1.2 copy-start.13
  636.1 6.0 copy-start.64
  648.6 6.0 copy-start.65
  673.8 2.8 copy-start.55
  (3 other events, 2.0 us)
Sparse Core Ops, SparseCore 0:
  11.5 72.1 all-gather.5
  92.1 19.6 all-gather.7
  114.0 19.6 all-gather.9
  189.7 91.6 reduce-scatter.7
  283.9 33.1 reduce-scatter.9
  320.3 104.0 all-reduce.2
  428.1 39.4 reduce-scatter.11
  470.0 22.7 reduce-scatter.13
  495.4 27.4 all-gather.11
  524.8 26.5 all-gather.13

commit v2 on v1

v2 whole, which is shorter than its diff:
```python
from functools import partial
import math

import jax
import jax.numpy as jnp
from jax import lax
from jax.experimental import pallas as pl
from jax.experimental.pallas import tpu as pltpu
from jax.sharding import Mesh, PartitionSpec as P

HEADS = 9
KV_HEADS = 3
HEAD_DIM = 64
FF = 1536
NS_STEPS = 5
ADAM_STEP = 10
D = 576
KV_WIDTH = 192
GROUPS = HEADS // KV_HEADS
TOK = 512
TILE = 256
COLS = GROUPS * TILE
ROW_CUT = 4
COL_CUT = 2
CHUNKS = ROW_CUT * COL_CUT
CHUNK_ROWS = D // ROW_CUT
CHUNK_COLS = FF // COL_CUT
PLANE = ("half", "ctx")
EVERY = ("quarter", "rep", "half", "ctx")


norm_epsilon = 1e-05
rope_base = 100000.0
masked_score = -1e30
newton_first = 3.4445
newton_second = -4.775
newton_third = 2.0315
momentum_decay = 0.95
matrix_rate = 0.2
weight_decay = 0.1
gain_rate = 0.2
first_decay = 0.9
second_decay = 0.95
adam_epsilon = 1e-08
frobenius_epsilon = 1e-07


def layout(lengths_row, places):
    finish = jnp.cumsum(lengths_row)
    firsts = finish - lengths_row
    begins = jnp.max(jnp.where(places[:, None] >= firsts[None, :], firsts[None, :], 0), axis=1)
    return (places - begins, begins)


def rope_tables(offsets):
    half_width = HEAD_DIM // 2
    inverse = jnp.exp(
        jnp.arange(half_width, dtype=jnp.float32) * (-2.0 * math.log(rope_base) / HEAD_DIM)
    )
    angles = inverse[:, None] * offsets.astype(jnp.float32)[None, :]
    return (jnp.cos(angles), jnp.sin(angles))


def rotate_columns(values, cosine, sine):
    shaped = values.reshape(-1, 2, HEAD_DIM // 2, values.shape[-1])
    former, latter = shaped[:, 0], shaped[:, 1]
    return jnp.stack(
        [former * cosine - latter * sine, latter * cosine + former * sine], axis=1
    ).reshape(values.shape)


def normalize(values, gain):
    scaling = lax.rsqrt(jnp.mean(values * values, axis=-1, keepdims=True) + norm_epsilon)
    return values * scaling * gain


def normalize_back(values, gain, upstream):
    scaling = lax.rsqrt(jnp.mean(values * values, axis=-1, keepdims=True) + norm_epsilon)
    weighted = upstream * gain
    gain_grad = jnp.sum(upstream * values * scaling, axis=0)
    inner_term = jnp.mean(weighted * values, axis=-1, keepdims=True)
    return (scaling * weighted - values * (scaling * scaling * scaling) * inner_term, gain_grad)


def dot32(left, right):
    return jnp.dot(left, right, preferred_element_type=jnp.float32)


def masked(scores, key_block, begins, places):
    keys = key_block * TILE + lax.broadcasted_iota(jnp.int32, scores.shape, 0)
    return jnp.where((keys >= begins) & (keys <= places), scores, masked_score)


def tile_row(row, tile):
    part = row[:, tile * TILE : (tile + 1) * TILE]
    return jnp.concatenate([part] * GROUPS, axis=1)


def tile_heads(ref, group, tile):
    return jnp.concatenate(
        [ref[group, head, :, tile * TILE : (tile + 1) * TILE] for head in range(GROUPS)], axis=1
    )


def key_loop(info, tile, step, carry):
    first, full, last = info[1 + 3 * tile], info[2 + 3 * tile], info[3 + 3 * tile]
    pairs = (last - full) // 2
    carry = lax.fori_loop(first, full, partial(step, True, 1), carry)
    carry = lax.fori_loop(
        0, pairs, lambda pair, held: step(False, 2, full + 2 * pair, held), carry
    )
    carry = lax.fori_loop(full + 2 * pairs, last, partial(step, False, 1), carry)
    return step(True, 1, last, carry)


def forward_kernel(backward_order, info, q_ref, kv_ref, begin_ref, o_ref, lse_ref, k_nat, v_ext):
    own = info[0]
    for block in range(4):

        @pl.when(block <= own)
        def _():
            for group in range(KV_HEADS):
                low = HEAD_DIM * group
                source = 3 - block if backward_order else block
                k_nat[group, TOK * block : TOK * (block + 1), :] = kv_ref[
                    source, low : low + HEAD_DIM, :
                ].T
                low = low + KV_WIDTH
                columns = slice(TOK * block, TOK * (block + 1))
                v_ext[group, :HEAD_DIM, columns] = kv_ref[source, low : low + HEAD_DIM, :]
                v_ext[group, HEAD_DIM:, columns] = jnp.ones((16, TOK), jnp.bfloat16)

    def one_group(group, unused):
        for tile in range(TOK // TILE):
            queries = tile_heads(q_ref, group, tile)
            begins = tile_row(begin_ref[...], tile)
            column = lax.broadcasted_iota(jnp.int32, (1, COLS), 1)
            places = own * TOK + tile * TILE + lax.rem(column, TILE)

            def step(is_masked, width, key_block, carry):
                top, total = carry
                keys = pl.ds(pl.multiple_of(key_block * TILE, TILE), width * TILE)
                scores = dot32(k_nat[group, keys, :], queries)
                if is_masked:
                    scores = masked(scores, key_block, begins, places)
                new_top = jnp.maximum(top, jnp.max(scores, axis=0, keepdims=True))
                probs = jnp.exp(scores - new_top).astype(jnp.bfloat16)
                total = total * jnp.exp(top - new_top) + dot32(v_ext[group, :, keys], probs)
                return (new_top, total)

            carry = (
                jnp.full((1, COLS), masked_score, jnp.float32),
                jnp.zeros((HEAD_DIM + 16, COLS), jnp.float32),
            )
            top, total = key_loop(info, tile, step, carry)
            weight = total[HEAD_DIM : HEAD_DIM + 1, :]
            mixed = (total[:HEAD_DIM, :] / weight).astype(jnp.bfloat16)
            log_total = top + jnp.log(weight)
            for head in range(GROUPS):
                o_ref[group, head, :, tile * TILE : (tile + 1) * TILE] = mixed[
                    :, head * TILE : (head + 1) * TILE
                ]
                lse_ref[group, head, :, tile * TILE : (tile + 1) * TILE] = log_total[
                    :, head * TILE : (head + 1) * TILE
                ]
        return unused

    lax.fori_loop(0, KV_HEADS, one_group, 0)


def backward_kernel(
    backward_order, info, q_ref, kv_ref, begin_ref, o_ref, lse_ref, do_ref, cos_ref, sin_ref,
    dq_ref, dkv_ref, k_nat, v_nat, k_tall, dk_ref, dv_ref,
):
    own = info[0]
    for block in range(4):

        @pl.when(block <= own)
        def _():
            rows = slice(TOK * block, TOK * (block + 1))
            for group in range(KV_HEADS):
                low = HEAD_DIM * group
                source = 3 - block if backward_order else block
                k_nat[group, rows, :] = kv_ref[source, low : low + HEAD_DIM, :].T
                k_tall[group, :, rows] = kv_ref[source, low : low + HEAD_DIM, :]
                low = low + KV_WIDTH
                v_nat[group, rows, :] = kv_ref[source, low : low + HEAD_DIM, :].T
                dk_ref[group, rows, :] = jnp.zeros((TOK, HEAD_DIM), jnp.float32)
                dv_ref[group, rows, :] = jnp.zeros((TOK, HEAD_DIM), jnp.float32)

    def one_group(group, unused):
        for tile in range(TOK // TILE):
            queries = tile_heads(q_ref, group, tile)
            upstream = tile_heads(do_ref, group, tile)
            mixed = tile_heads(o_ref, group, tile)
            log_total = tile_heads(lse_ref, group, tile)
            delta = jnp.sum(
                upstream.astype(jnp.float32) * mixed.astype(jnp.float32), axis=0, keepdims=True
            )
            queries_nat = queries.T
            upstream_nat = upstream.T
            begins = tile_row(begin_ref[...], tile)
            column = lax.broadcasted_iota(jnp.int32, (1, COLS), 1)
            places = own * TOK + tile * TILE + lax.rem(column, TILE)

            def step(is_masked, width, key_block, dq):
                rows = pl.ds(pl.multiple_of(key_block * TILE, TILE), width * TILE)
                scores = dot32(k_nat[group, rows, :], queries)
                if is_masked:
                    scores = masked(scores, key_block, begins, places)
                probs = jnp.exp(scores - log_total)
                grad_probs = dot32(v_nat[group, rows, :], upstream)
                grad_scores = (probs * (grad_probs - delta)).astype(jnp.bfloat16)
                dv_ref[group, rows, :] += dot32(probs.astype(jnp.bfloat16), upstream_nat)
                dk_ref[group, rows, :] += dot32(grad_scores, queries_nat)
                return dq + dot32(k_tall[group, :, rows], grad_scores)

            dq = jnp.zeros((HEAD_DIM, COLS), jnp.float32)
            dq = key_loop(info, tile, step, dq) * 0.125
            half_width = HEAD_DIM // 2
            cosine = tile_row(cos_ref[...], tile)
            sine = tile_row(sin_ref[...], tile)
            former, latter = dq[:half_width], dq[half_width:]
            turned = jnp.concatenate(
                [former * cosine + latter * sine, latter * cosine - former * sine], axis=0
            ).astype(jnp.bfloat16)
            for head in range(GROUPS):
                dq_ref[group, head, :, tile * TILE : (tile + 1) * TILE] = turned[
                    :, head * TILE : (head + 1) * TILE
                ]
        return unused

    lax.fori_loop(0, KV_HEADS, one_group, 0)
    for block in range(4):
        rows = slice(TOK * block, TOK * (block + 1))
        target = 3 - block if backward_order else block

        @pl.when(block <= own)
        def _():
            for group in range(KV_HEADS):
                low = HEAD_DIM * group
                dkv_ref[target, low : low + HEAD_DIM, :] = dk_ref[group, rows, :].T.astype(
                    jnp.bfloat16
                )
                low = low + KV_WIDTH
                dkv_ref[target, low : low + HEAD_DIM, :] = dv_ref[group, rows, :].T.astype(
                    jnp.bfloat16
                )

        @pl.when(block > own)
        def _():
            dkv_ref[target] = jnp.zeros((2 * KV_WIDTH, TOK), jnp.bfloat16)


def vmem():
    return pl.BlockSpec(memory_space=pltpu.VMEM)


def smem():
    return pl.BlockSpec(memory_space=pltpu.SMEM)


kernel_params = pltpu.CompilerParams(vmem_limit_bytes=56 * 1024 * 1024)
heads_shape = (KV_HEADS, GROUPS, HEAD_DIM, TOK)


def attend_forward(backward_order, info, queries, keyvals, begins):
    return pl.pallas_call(
        partial(forward_kernel, backward_order),
        out_shape=(
            jax.ShapeDtypeStruct(heads_shape, jnp.bfloat16),
            jax.ShapeDtypeStruct((KV_HEADS, GROUPS, 1, TOK), jnp.float32),
        ),
        in_specs=[smem(), vmem(), vmem(), vmem()],
        out_specs=(vmem(), vmem()),
        scratch_shapes=[
            pltpu.VMEM((KV_HEADS, 4 * TOK, HEAD_DIM), jnp.bfloat16),
            pltpu.VMEM((KV_HEADS, HEAD_DIM + 16, 4 * TOK), jnp.bfloat16),
        ],
        compiler_params=kernel_params,
        cost_estimate=pl.CostEstimate(
            flops=4 * 9 * 64 * TOK * 2048, bytes_accessed=4000000, transcendentals=9 * TOK * 2048
        ),
        name="attend_forward",
    )(info, queries, keyvals, begins)


def attend_back(
    backward_order, info, queries, keyvals, begins, mixed, log_total, grad_mixed, cosine, sine
):
    return pl.pallas_call(
        partial(backward_kernel, backward_order),
        out_shape=(
            jax.ShapeDtypeStruct(heads_shape, jnp.bfloat16),
            jax.ShapeDtypeStruct((4, 2 * KV_WIDTH, TOK), jnp.bfloat16),
        ),
        in_specs=[smem()] + [vmem()] * 8,
        out_specs=(vmem(), vmem()),
        scratch_shapes=[
            pltpu.VMEM((KV_HEADS, 4 * TOK, HEAD_DIM), jnp.bfloat16),
            pltpu.VMEM((KV_HEADS, 4 * TOK, HEAD_DIM), jnp.bfloat16),
            pltpu.VMEM((KV_HEADS, HEAD_DIM, 4 * TOK), jnp.bfloat16),
            pltpu.VMEM((KV_HEADS, 4 * TOK, HEAD_DIM), jnp.float32),
            pltpu.VMEM((KV_HEADS, 4 * TOK, HEAD_DIM), jnp.float32),
        ],
        compiler_params=kernel_params,
        cost_estimate=pl.CostEstimate(
            flops=10 * 9 * 64 * TOK * 2048, bytes_accessed=8000000, transcendentals=9 * TOK * 2048
        ),
        name="attend_back",
    )(info, queries, keyvals, begins, mixed, log_total, grad_mixed, cosine, sine)


def dot_with(left, right, left_side, right_side):
    return lax.dot_general(
        left, right, (((left_side,), (right_side,)), ((), ())), preferred_element_type=jnp.float32
    )


def norm_back(values, scaling, gain, upstream):
    weighted = upstream * gain
    inner = jnp.mean(weighted * values, axis=-1, keepdims=True)
    gain_grad = jnp.sum(upstream * values * scaling, axis=0, keepdims=True)
    return (scaling * weighted - values * (scaling * scaling * scaling) * inner, gain_grad)


def store_chunks(matrix, column, put):
    half, low = column // (FF // COL_CUT), column % (FF // COL_CUT)
    for row in range(ROW_CUT):
        part = matrix[row * CHUNK_ROWS : (row + 1) * CHUNK_ROWS].astype(jnp.bfloat16)
        put(row * COL_CUT + half, slice(low, low + matrix.shape[1]), part)


def mlp_kernel(
    x_ref, c_ref, o0_ref, o1_ref, wo_ref, wg_ref, wu_ref, wd_ref, gain_ref,
    out_ref, dh_ref, do0_ref, do1_ref, early_ref, gwo_ref, gg_ref,
    hid, dgate, dup, n2_tall, c_tall, dh_low,
):
    gain = gain_ref[...]
    gg_ref[...] = jnp.zeros((1, D), jnp.float32)
    block = 256
    for micro, (o_ref, do_ref) in enumerate(((o0_ref, do0_ref), (o1_ref, do1_ref))):
        rows = slice(micro * TOK, (micro + 1) * TOK)
        hidden_state = x_ref[micro].astype(jnp.float32) + dot32(o_ref[...].T, wo_ref[...])
        scaling = lax.rsqrt(
            jnp.mean(hidden_state * hidden_state, axis=-1, keepdims=True) + norm_epsilon
        )
        normed = (hidden_state * scaling * gain).astype(jnp.bfloat16)
        n2_tall[:, rows] = normed.T
        back = c_ref[micro]
        c_tall[:, rows] = back.T
        for column in range(0, FF, block):
            columns = slice(column, column + block)
            gate = dot32(normed, wg_ref[:, columns])
            upward = dot32(normed, wu_ref[:, columns])
            grad_hidden = dot_with(back, wd_ref[columns, :], 1, 1)
            sigmoid_gate = jax.nn.sigmoid(gate)
            activated = gate * sigmoid_gate
            hid[rows, columns] = (activated * upward).astype(jnp.bfloat16)
            dgate[rows, columns] = (
                grad_hidden * upward * sigmoid_gate * (1.0 + gate * (1.0 - sigmoid_gate))
            ).astype(jnp.bfloat16)
            dup[rows, columns] = (grad_hidden * activated).astype(jnp.bfloat16)
        out_ref[micro] = hidden_state + dot32(hid[rows, :], wd_ref[...])
        upstream = dot_with(dgate[rows, :], wg_ref[...], 1, 1) + dot_with(
            dup[rows, :], wu_ref[...], 1, 1
        )
        part, gain_grad = norm_back(hidden_state, scaling, gain, upstream)
        gg_ref[...] += gain_grad
        grad_state = back.astype(jnp.float32) + part
        dh_ref[micro] = grad_state
        low = grad_state.astype(jnp.bfloat16)
        dh_low[rows, :] = low
        do_ref[...] = dot_with(wo_ref[...], low, 1, 1).astype(jnp.bfloat16)
    for column in range(0, FF, block):
        columns = slice(column, column + block)
        for place, (left, right) in enumerate(((n2_tall, dgate), (n2_tall, dup), (c_tall, hid))):

            def put(spot, where, part):
                early_ref[spot, place, :, where] = part

            store_chunks(dot32(left[...], right[:, columns]), column, put)
    gwo_ref[...] = (
        dot32(o0_ref[...], dh_low[:TOK, :]) + dot32(o1_ref[...], dh_low[TOK:, :])
    ).astype(jnp.bfloat16)


def mlp(tokens, cotangent, mixed, w_out, w_gate, w_up, w_down, gain):
    rows = tokens.shape[0] * TOK
    low = jnp.bfloat16
    return pl.pallas_call(
        mlp_kernel,
        out_shape=(
            jax.ShapeDtypeStruct(tokens.shape, jnp.float32),
            jax.ShapeDtypeStruct(tokens.shape, jnp.float32),
            jax.ShapeDtypeStruct((D, TOK), low),
            jax.ShapeDtypeStruct((D, TOK), low),
            jax.ShapeDtypeStruct((CHUNKS, 3, CHUNK_ROWS, CHUNK_COLS), low),
            jax.ShapeDtypeStruct((D, D), low),
            jax.ShapeDtypeStruct((1, D), jnp.float32),
        ),
        in_specs=[vmem()] * 9,
        out_specs=(vmem(),) * 7,
        scratch_shapes=[
            pltpu.VMEM((rows, FF), low),
            pltpu.VMEM((rows, FF), low),
            pltpu.VMEM((rows, FF), low),
            pltpu.VMEM((D, rows), low),
            pltpu.VMEM((D, rows), low),
            pltpu.VMEM((rows, D), low),
        ],
        compiler_params=kernel_params,
        cost_estimate=pl.CostEstimate(
            flops=6 * rows * 3 * D * FF, bytes_accessed=25000000, transcendentals=rows * FF
        ),
        name="mlp",
    )(tokens, cotangent, mixed[0], mixed[1], w_out, w_gate, w_up, w_down, gain)


def projection_kernel(
    n_ref, dq0_ref, dq1_ref, dkv0_ref, dkv1_ref, cos0_ref, sin0_ref, cos1_ref, sin1_ref, gwo_ref,
    late_ref, all_ref, held,
):
    half_width = HEAD_DIM // 2
    parts = ((dq0_ref, dkv0_ref, cos0_ref, sin0_ref), (dq1_ref, dkv1_ref, cos1_ref, sin1_ref))
    for micro, (dq_ref, dkv_ref, cos_ref, sin_ref) in enumerate(parts):
        columns = slice(micro * TOK, (micro + 1) * TOK)
        all_ref[:D, columns] = dq_ref[...]
        cosine, sine = cos_ref[...], sin_ref[...]
        for head in range(KV_HEADS):
            low = head * HEAD_DIM
            former = dkv_ref[low : low + half_width, :].astype(jnp.float32)
            latter = dkv_ref[low + half_width : low + HEAD_DIM, :].astype(jnp.float32)
            all_ref[D + low : D + low + half_width, columns] = (
                former * cosine + latter * sine
            ).astype(jnp.bfloat16)
            all_ref[D + low + half_width : D + low + HEAD_DIM, columns] = (
                latter * cosine - former * sine
            ).astype(jnp.bfloat16)
        all_ref[D + KV_WIDTH :, columns] = dkv_ref[KV_WIDTH:, :]
    held[:, : D + 2 * KV_WIDTH] = dot_with(n_ref[...].T, all_ref[...], 1, 1)
    held[:, D + 2 * KV_WIDTH :] = gwo_ref[...].astype(jnp.float32)

    def put(spot, where, part):
        late_ref[spot, :, where] = part

    for column in range(0, FF, CHUNK_COLS):
        store_chunks(held[:, column : column + CHUNK_COLS], column, put)


def projection_grads(normed, dqs, dkvs, tables, gwo):
    rows = normed.shape[0]
    return pl.pallas_call(
        projection_kernel,
        out_shape=(
            jax.ShapeDtypeStruct((CHUNKS, CHUNK_ROWS, CHUNK_COLS), jnp.bfloat16),
            jax.ShapeDtypeStruct((D + 2 * KV_WIDTH, rows), jnp.bfloat16),
        ),
        in_specs=[vmem()] * 10,
        out_specs=(vmem(),) * 2,
        scratch_shapes=[pltpu.VMEM((D, FF), jnp.float32)],
        compiler_params=kernel_params,
        cost_estimate=pl.CostEstimate(
            flops=2 * rows * D * 960, bytes_accessed=8000000, transcendentals=0
        ),
        name="projection_grads",
    )(normed, *dqs, *dkvs, *tables[0], *tables[1], gwo)


def inputs_kernel(all_ref, w_ref, x_ref, dh_ref, gain_ref, out0_ref, out1_ref, gg_ref):
    gain = gain_ref[...]
    gg_ref[...] = jnp.zeros((1, D), jnp.float32)
    for micro, out_ref in enumerate((out0_ref, out1_ref)):
        columns = slice(micro * TOK, (micro + 1) * TOK)
        upstream = dot_with(all_ref[:, columns].T, w_ref[...], 1, 1)
        values = x_ref[micro].astype(jnp.float32)
        scaling = lax.rsqrt(jnp.mean(values * values, axis=-1, keepdims=True) + norm_epsilon)
        part, gain_grad = norm_back(values, scaling, gain, upstream)
        gg_ref[...] += gain_grad
        out_ref[...] = (dh_ref[micro] + part).astype(out_ref.dtype)


def input_grads(grad_qkv, w_qkv, tokens, grad_state, gain):
    rows = grad_qkv.shape[1]
    return pl.pallas_call(
        inputs_kernel,
        out_shape=(
            jax.ShapeDtypeStruct((TOK, D), jnp.float32),
            jax.ShapeDtypeStruct((TOK, D), jnp.bfloat16),
            jax.ShapeDtypeStruct((1, D), jnp.float32),
        ),
        in_specs=[vmem()] * 5,
        out_specs=(vmem(),) * 3,
        compiler_params=kernel_params,
        cost_estimate=pl.CostEstimate(
            flops=2 * rows * D * 960, bytes_accessed=8000000, transcendentals=0
        ),
        name="input_grads",
    )(grad_qkv, w_qkv, tokens, grad_state, gain)


def newton_loop(matrix, scale):
    current = matrix / (jnp.sqrt(jnp.sum(matrix * matrix)) + frobenius_epsilon)

    def iterate(unused, held):
        low = held.astype(jnp.bfloat16)
        square = dot_with(low, low, 1, 1)
        square_low = square.astype(jnp.bfloat16)
        mixer = newton_second * square + newton_third * dot32(square_low, square_low)
        return newton_first * held + dot32(mixer.astype(jnp.bfloat16), low)

    return lax.fori_loop(0, NS_STEPS, iterate, current) * (0.2 * math.sqrt(scale))


def newton_kernel(info, pieces_ref, old_ref, grad_ref, out_ref, total):
    spot, kind = info[0], info[1]
    for chunk in range(CHUNKS):
        row, column = chunk // COL_CUT * CHUNK_ROWS, chunk % COL_CUT * CHUNK_COLS
        rows, columns = slice(row, row + CHUNK_ROWS), slice(column, column + CHUNK_COLS)
        part = pieces_ref[chunk ^ spot]
        grad_ref[rows, columns] = part
        total[rows, columns] = momentum_decay * old_ref[rows, columns].astype(
            jnp.float32
        ) + part.astype(jnp.float32)

    @pl.when(kind == 0)
    def _():
        out_ref[...] = newton_loop(total[...], FF)

    for place, low in ((1, 0), (2, FF - D)):

        @pl.when(kind == place)
        def _():
            out_ref[:, low : low + D] = newton_loop(total[:, low : low + D], D)

    for place, low in ((3, D), (4, D + KV_WIDTH)):

        @pl.when(kind == place)
        def _():
            out_ref[:, low : low + KV_WIDTH] = newton_loop(total[:, low : low + KV_WIDTH].T, D).T


def newton(info, pieces, old):
    return pl.pallas_call(
        newton_kernel,
        out_shape=(
            jax.ShapeDtypeStruct((D, FF), jnp.bfloat16),
            jax.ShapeDtypeStruct((D, FF), jnp.float32),
        ),
        in_specs=[smem(), vmem(), vmem()],
        out_specs=(vmem(),) * 2,
        scratch_shapes=[pltpu.VMEM((D, FF), jnp.float32)],
        compiler_params=kernel_params,
        cost_estimate=pl.CostEstimate(
            flops=12000000000, bytes_accessed=9000000, transcendentals=0
        ),
        name="newton",
    )(info, pieces, old)


def quarter_matrix(quarter, flat):
    def mixed_case(flat):
        square = D * D
        narrow = D * KV_WIDTH
        return jnp.concatenate(
            [
                flat[:square].reshape(D, D),
                flat[square : square + narrow].reshape(D, KV_WIDTH),
                flat[square + narrow : square + 2 * narrow].reshape(D, KV_WIDTH),
                flat[square + 2 * narrow :].reshape(D, D),
            ],
            axis=1,
        )

    def wide_case(flat):
        return flat.reshape(D, FF)

    def tall_case(flat):
        return flat.reshape(FF, D).T

    return lax.switch(quarter, [mixed_case, wide_case, wide_case, tall_case], flat)


def own_kind(quarter, within):
    square = D * D
    narrow = D * KV_WIDTH
    edges = (square, square + narrow, square + 2 * narrow)
    passed = sum((within >= edge).astype(jnp.int32) for edge in edges)
    mixed = jnp.array([1, 3, 4, 2], jnp.int32)[passed]
    starts = jnp.array([0, square, square + narrow, square + 2 * narrow], jnp.int32)
    inside = within - jnp.where(quarter == 0, starts[passed], 0)
    return (jnp.where(quarter == 0, mixed, 0), inside)


def own_rows(quarter, kind, inside, shard_length, gradient, update):
    def block_case(low, width):
        def run(gradient, update):
            start = (inside // width, low)
            size = (shard_length // width, width)
            return tuple(
                lax.dynamic_slice(whole, start, size).reshape(-1) for whole in (gradient, update)
            )

        return run

    def tall_case(gradient, update):
        start = (0, inside // D)
        size = (D, shard_length // D)
        return tuple(
            lax.dynamic_slice(whole, start, size).T.reshape(-1) for whole in (gradient, update)
        )

    cases = [
        block_case(0, FF),
        block_case(0, D),
        block_case(FF - D, D),
        block_case(D, KV_WIDTH),
        block_case(D + KV_WIDTH, KV_WIDTH),
        tall_case,
    ]
    return lax.switch(jnp.where(quarter == 3, 5, kind), cases, gradient, update)


CORE_SWAP = [(0, 1), (1, 0), (2, 3), (3, 2)]
CHIP_SWAP = [(0, 2), (2, 0), (1, 3), (3, 1)]
SIDE_SWAP = [(0, 1), (1, 0)]
END_SWAP = [(0, 3), (3, 0), (1, 2), (2, 1)]


def plane_steps():
    ctx = lax.axis_index("ctx")
    return (
        ("ctx", CORE_SWAP, lax.rem(ctx, 2)),
        ("ctx", CHIP_SWAP, ctx // 2),
        ("half", SIDE_SWAP, lax.axis_index("half")),
    )


def plane_sum(chunks):
    for axis, swap, bit in plane_steps():
        halves = chunks.reshape(2, chunks.shape[0] // 2, *chunks.shape[1:])
        sent = lax.dynamic_index_in_dim(halves, 1 - bit, 0, keepdims=False)
        kept = lax.dynamic_index_in_dim(halves, bit, 0, keepdims=False)
        got = lax.ppermute(sent, axis, swap)
        chunks = (kept.astype(jnp.float32) + got.astype(jnp.float32)).astype(jnp.bfloat16)
    return chunks[0]


def plane_gather(piece):
    pieces = piece[None]
    for axis, swap, bit in reversed(plane_steps()):
        pieces = jnp.concatenate([pieces, lax.ppermute(pieces, axis, swap)], axis=0)
    return pieces


def depth_sum(late, early):
    quarter = lax.axis_index("quarter")
    pieces = jnp.concatenate([late[None], early], axis=0)
    total = lax.dynamic_index_in_dim(pieces, quarter, 0, keepdims=False).astype(jnp.float32)
    for shift in range(1, 4):
        target = lax.rem(quarter + shift, 4)
        sent = lax.dynamic_index_in_dim(pieces, target, 0, keepdims=False)
        got = lax.ppermute(sent, "quarter", [(place, (place + shift) % 4) for place in range(4)])
        total = total + got.astype(jnp.float32)
    return total.astype(jnp.bfloat16)


def attention_info(ctx, begins):
    fields = [ctx]
    for tile in range(TOK // TILE):
        last = ctx * (TOK // TILE) + tile
        first = begins[tile * TILE] // TILE
        full = jnp.minimum(last, (begins[(tile + 1) * TILE - 1] + TILE - 1) // TILE)
        fields = fields + [first, full, last]
    return jnp.stack(fields).astype(jnp.int32)


def per_device(tokens, lengths, weights, momentum, norm_gains, gain_first, gain_second, cotangent):
    micro_count = tokens.shape[0]
    ctx = lax.axis_index("ctx")
    quarter = lax.axis_index("quarter")
    reps = lax.axis_size("rep")
    shard_length = weights.shape[0]
    within = lax.axis_index(("rep", "half", "ctx")) * shard_length
    spot = lax.rem(ctx, 2) * 4 + ctx // 2 * 2 + lax.axis_index("half")

    full_weights = lax.all_gather(weights.astype(jnp.bfloat16), EVERY, axis=0, tiled=True)
    square, narrow, broad = D * D, D * KV_WIDTH, D * FF
    places_in = [0, square, square + narrow, square + 2 * narrow]
    w_qkv = jnp.concatenate(
        [
            full_weights[:square].reshape(D, D),
            full_weights[places_in[1] : places_in[2]].reshape(D, KV_WIDTH),
            full_weights[places_in[2] : places_in[3]].reshape(D, KV_WIDTH),
        ],
        axis=1,
    )
    w_out = full_weights[places_in[3] : places_in[3] + square].reshape(D, D)
    w_gate = full_weights[broad : 2 * broad].reshape(D, FF)
    w_up = full_weights[2 * broad : 3 * broad].reshape(D, FF)
    w_down = full_weights[3 * broad :].reshape(FF, D)

    swapped = lax.ppermute(jnp.stack([tokens[1], cotangent[1]]), "ctx", END_SWAP)
    tokens_here = jnp.stack([tokens[0], swapped[0]])
    back = jnp.stack([cotangent[0], swapped[1]])
    inputs = tokens_here.astype(jnp.float32).reshape(-1, D)
    normed = normalize(inputs, norm_gains[0]).astype(jnp.bfloat16)
    infos, begin_rows, tables = [], [], []
    for micro in range(micro_count):
        block = ctx if micro == 0 else 3 - ctx
        own_places = block * TOK + jnp.arange(TOK, dtype=jnp.int32)
        offsets, begins = layout(lengths[micro, 0], own_places)
        infos.append(attention_info(block, begins))
        begin_rows.append(begins.reshape(1, TOK))
        tables.append(rope_tables(offsets))

    queries, keyvals, mixed, log_totals = [], [], [], []
    for micro in range(micro_count):
        rows = normed[micro * TOK : (micro + 1) * TOK]
        linear = jnp.einsum("de,td->et", w_qkv, rows, preferred_element_type=jnp.float32)
        turned = rotate_columns(linear[: D + KV_WIDTH], *tables[micro])
        scaled = turned[:D].astype(jnp.bfloat16) * jnp.bfloat16(0.125)
        queries.append(scaled.reshape(heads_shape))
        own_keyvals = jnp.concatenate([turned[D:], linear[D + KV_WIDTH :]], axis=0)
        keyvals.append(own_keyvals.astype(jnp.bfloat16))
    gathered = lax.all_gather(jnp.stack(keyvals), "ctx", axis=1, tiled=False)
    keyvals = [gathered[micro] for micro in range(micro_count)]
    for micro in range(micro_count):
        mixed_one, log_total = attend_forward(
            micro == 1, infos[micro], queries[micro], keyvals[micro], begin_rows[micro]
        )
        mixed.append(mixed_one)
        log_totals.append(log_total)
    result, grad_state, grad_mixed_0, grad_mixed_1, early, grad_w_out, gain_two_grad = mlp(
        tokens_here,
        back,
        [part.reshape(D, TOK) for part in mixed],
        w_out,
        w_gate,
        w_up,
        w_down,
        norm_gains[1:2],
    )
    returned = lax.ppermute(result[1].astype(jnp.bfloat16), "ctx", END_SWAP)
    result = jnp.stack([result[0], returned.astype(jnp.float32)])
    early = plane_sum(early)
    old = lax.all_gather(
        momentum.astype(jnp.bfloat16), ("rep", "half", "ctx"), axis=0, tiled=True
    )

    grad_queries, grad_keyvals = [], []
    for micro, grad_mixed in enumerate((grad_mixed_0, grad_mixed_1)):
        dq, dkv = attend_back(
            micro == 1,
            infos[micro],
            queries[micro],
            keyvals[micro],
            begin_rows[micro],
            mixed[micro],
            log_totals[micro],
            grad_mixed.reshape(heads_shape),
            *tables[micro],
        )
        for step, (swap, bit) in enumerate(((CORE_SWAP, lax.rem(ctx, 2)), (CHIP_SWAP, ctx // 2))):
            shaped = dkv.reshape(2, 2, 2 * KV_WIDTH, TOK) if step == 0 else dkv
            axis = 1 if step == 0 else 0
            sent = lax.dynamic_index_in_dim(shaped, 1 - bit, axis, keepdims=False)
            kept = lax.dynamic_index_in_dim(shaped, bit, axis, keepdims=False)
            got = lax.ppermute(sent, "ctx", swap)
            dkv = (kept.astype(jnp.float32) + got.astype(jnp.float32)).astype(jnp.bfloat16)
        grad_queries.append(dq.reshape(D, TOK))
        grad_keyvals.append(dkv)
    late, grad_qkv = projection_grads(normed, grad_queries, grad_keyvals, tables, grad_w_out)
    late = plane_sum(late)
    grad_inputs_0, grad_inputs_1, gain_one_grad = input_grads(
        grad_qkv, w_qkv, tokens_here, grad_state, norm_gains[0:1]
    )
    returned = lax.ppermute(grad_inputs_1, "ctx", END_SWAP)
    grad_inputs = jnp.stack([grad_inputs_0, returned.astype(jnp.float32)])
    gain_parts = lax.all_gather(
        jnp.concatenate([gain_one_grad, gain_two_grad], axis=0), EVERY, axis=0, tiled=False
    )
    gain_grad = jnp.sum(gain_parts, axis=0)

    piece = depth_sum(late, early)
    if reps > 1:
        piece = lax.psum(piece, "rep")
    pieces = plane_gather(piece)
    kind, inside = own_kind(quarter, within)
    gradient, update = newton(
        jnp.stack([spot, kind]).astype(jnp.int32), pieces, quarter_matrix(quarter, old)
    )
    grad_shard, update_shard = own_rows(quarter, kind, inside, shard_length, gradient, update)
    grad_shard = grad_shard.astype(jnp.float32)
    new_momentum = momentum_decay * momentum + grad_shard
    new_weights = weights * (1.0 - matrix_rate * weight_decay) - matrix_rate * update_shard

    first_new = first_decay * gain_first + (1.0 - first_decay) * gain_grad
    second_new = second_decay * gain_second + (1.0 - second_decay) * gain_grad * gain_grad
    debiased_first_moment = first_new / (1.0 - first_decay**ADAM_STEP)
    corrected_second = second_new / (1.0 - second_decay**ADAM_STEP)
    new_gains = norm_gains * (
        1.0 - gain_rate * weight_decay
    ) - gain_rate * debiased_first_moment / (jnp.sqrt(corrected_second) + adam_epsilon)
    return (
        result,
        grad_inputs,
        grad_shard,
        new_momentum,
        new_weights,
        first_new,
        second_new,
        new_gains,
    )


def solution(mesh):
    devices = mesh.devices
    count = devices.size
    context = mesh.shape["ctx"]
    split = Mesh(
        devices.reshape(4, count // (8 * context), 2, context), ("quarter", "rep", "half", "ctx")
    )
    rows = P(None, EVERY, None)
    flat = P(EVERY)
    placed = (rows, P(None, ("quarter", "rep", "half"), None), flat, flat, P(), P(), P(), rows)
    return jax.shard_map(
        per_device,
        mesh=split,
        in_specs=placed,
        out_specs=(rows, rows, flat, flat, flat, P(), P(), P()),
        check_vma=False,
    )
```

time: 709 us -> 510 us (0.72)
  the two profiles are of different devices: /device:TPU:26 before, /device:TPU:31 now
where the time goes in v2:
time: 510 us; the launch traced here: 501 us
  Pallas kernels  135 us (26%)
  waiting for transfers between devices  119 us (23%)
  local copies, waits for them, and re-layouts  77.1 us (15%)
  starting transfers between devices  57.2 us (11%)
  other arithmetic  41.4 us (8%)
  blocking collectives  37.8 us (7%)
  between operations  30.4 us (6%)
    all_gather x1, blocking collectives, per_device(): lax.all_gather(jnp.concatenate([gain_one_grad, gain_two_grad], axis=0), E...  37.8 us
    pallas_call x2, Pallas kernels, attend_back(): pl.pallas_call(partial(backward_kernel, backward_order), out_shape=(jax.S...  35.5 us
    ppermute x6, waiting for transfers between devices, plane_sum(): got = lax.ppermute(sent, axis, swap)  35.4 us
    all_gather x1, waiting for transfers between devices, per_device(): lax.all_gather(weights.astype(jnp.bfloat16), EVERY, axis=0, tiled=True)  35.1 us
    pallas_call x1, Pallas kernels, mlp(): pl.pallas_call(mlp_kernel, out_shape=(jax.ShapeDtypeStruct(tokens.shape,...  33.9 us
    ppermute x6, starting transfers between devices, plane_sum(): got = lax.ppermute(sent, axis, swap)  31 us
    pallas_call x1, Pallas kernels, newton(): pl.pallas_call(newton_kernel, out_shape=(jax.ShapeDtypeStruct((D, FF), jn...  27.5 us
    pallas_call x2, Pallas kernels, attend_forward(): pl.pallas_call(partial(forward_kernel, backward_order), out_shape=(jax.Sh...  26.6 us
  transfers between devices with their start and end apart: 22, of which 11 were waited for; matrix products, arithmetic and copies ran while one was open for 15% of the time, Pallas kernels for 9%

profile of v2, /device:TPU:31, one launch (start us, length us, event | category | flops | bytes accessed | tf_op | source)
XLA Modules:
  0.0 501.0 jit_solution(10653576372557931802)
XLA Ops:
  8.0 1.7 convert_element_type.223
  9.8 1.8 fusion.40
  32.2 12.0 %collective-permute-done = bf16[2,512,576]{1,2,0:T(8,128)(2,1)S(1)} collective-permute-done((bf16[2,512,576]{1,2,0:T(8,128)(2,1)}, bf16[2,512,576]{1,2,0:T(8,128)(2,1)S(1)}, u32[]{:S(2)}, u32[]{:S(2)}) %collective-permute-start) | collective-permute-done | bytes 1179680 | tf_op jit(solution)/shard_map/ppermute | solution.py:703
  45.8 1.4 copy.76
  47.1 1.3 pad_maximum_fusion.3.x_ref
  48.4 1.3 pad_maximum_fusion.4.c_ref
  50.1 35.1 %all-gather.7.cloned.1.call-done = bf16[3538944]{0:T(1024)(128)(2,1)} async-done(((bf16[110592]{0:T(1024)(128)(2,1)}), bf16[3538944]{0:T(1024)(128)(2,1)}) %all-gather.7.cloned.1.call-update) | async-done | bytes 7077904 | tf_op jit(solution)/shard_map/all_gather | solution.py:687
  85.2 2.2 fusion.37
  98.6 4.1 fusion.36
  102.7 2.8 slice.317.wd_ref
  105.4 4.5 slice.313.wg_ref
  109.9 3.0 slice.315.wu_ref
  112.9 2.5 slice.311.wo_ref
  117.3 9.9 %all-gather.11.cloned.1.call-done = bf16[2,1536,512]{2,1,0:T(8,128)(2,1)} async-done(((bf16[2,384,512]{2,1,0:T(8,128)(2,1)}), bf16[2,1536,512]{2,1,0:T(8,128)(2,1)}) %all-gather.11.cloned.1.call-update) | async-done | bytes 3145744 | tf_op jit(solution)/shard_map/all_gather | solution.py:726
  127.2 3.8 fusion.39
  131.0 8.1 %attend_forward.3 = (bf16[3,3,64,512]{3,2,1,0:T(8,128)(2,1)}, f32[3,3,1,512]{3,2,1,0:T(1,128)}) custom-call(s32[7]{0:T(128)} %stack.123.info, bf16[3,3,64,512]{3,2,1,0:T(8,128)(2,1)} %bitcast.179, bf16[4,384,512]{2,1,0:T(8,128)(2,1)} %bitcast.170, s32[1,512]{1,0:T(1,128)} %bitcast.183), custom_call_target="tpu_custom_call" | custom-call | flops 2415919104 | bytes 4000000 | tf_op jit(solution)/shard_map/attend_forward/pallas_call | solution.py:268
  139.1 18.4 %attend_forward.2 = (bf16[3,3,64,512]{3,2,1,0:T(8,128)(2,1)}, f32[3,3,1,512]{3,2,1,0:T(1,128)}) custom-call(s32[7]{0:T(128)} %stack.112.info, bf16[3,3,64,512]{3,2,1,0:T(8,128)(2,1)} %bitcast.175, bf16[4,384,512]{2,1,0:T(8,128)(2,1)} %bitcast.168, s32[1,512]{1,0:T(1,128)} %bitcast.181), custom_call_target="tpu_custom_call" | custom-call | flops 2415919104 | bytes 4000000 | tf_op jit(solution)/shard_map/attend_forward/pallas_call | solution.py:268
  157.6 33.9 %mlp.1 = (f32[2,512,576]{2,1,0:T(8,128)}, f32[2,512,576]{2,1,0:T(8,128)}, bf16[576,512]{1,0:T(8,128)(2,1)}, bf16[576,512]{1,0:T(8,128)(2,1)}, bf16[8,3,144,768]{...) custom-call(bf16[2,512,576]{2,1,0:T(8,128)(2,1)} %pad_maximum_fusion.3.x_ref, ...), custom_call_target="tpu_custom_call" | custom-call | flops 16307453952 | bytes 25000000 | tf_op jit(solution)/shard_map/mlp/pallas_call | solution.py:391
  191.4 3.5 dynamic-slice_bitcast_fusion.1
  194.9 5.9 %collective-permute-start.10 = (bf16[4,3,144,768]{3,2,1,0:T(8,128)(2,1)}, bf16[4,3,144,768]{3,2,1,0:T(8,128)(2,1)}, u32[]{:S(2)}, u32[]{:S(2)}) collective-permute-start(bf16[4,3,144,768]{3,2,1,0:T(8,128)(2,1)} %dynamic-slice_bitcast_fusion.1), channel_id=1, source_target_pairs={{0,1},{1,0},{2,3},{3,2},{4,5},{5,4},{6,7},{7,6},{8,9},{9,8},{10,11... | collective-permute-start | bytes 7962632 | tf_op jit(solution)/shard_map/ppermute | solution.py:644
  200.8 10.7 %attend_back.3 = (bf16[3,3,64,512]{3,2,1,0:T(8,128)(2,1)}, bf16[4,384,512]{2,1,0:T(8,128)(2,1)}) custom-call(s32[7]{0:T(128)} %stack.123.info, bf16[3,3,64,512]{3,2,1,0:T(8,128)(2,1)} %bitcast.180, bf16[4,384,512]{2,1,0:T(8,128)(2,1)} %bitcast.171, s32[1,512]{1,0:T(1,128)} %bitcast.184, bf16[3,3,64,512]{3,2,1,0:T(8,128)(2,1)} %get-tuple-element.164.o_ref, ...), custom_call_target="tpu_custom_call" | custom-call | flops 6039797760 | bytes 8000000 | tf_op jit(solution)/shard_map/attend_back/pallas_call | solution.py:291
  212.7 7.8 %collective-permute-start.4 = (bf16[2,384,512]{2,1,0:T(8,128)(2,1)S(1)}, bf16[2,384,512]{2,1,0:T(8,128)(2,1)S(1)}, u32[]{:S(2)}, u32[]{:S(2)}) collective-permute-start(bf16[2,384,512]{2,1,0:T(8,128)(2,1)S(1)} %dynamic-slice_bitcast_fusion.4), channel_id=1, source_target_pairs={{0,1},{1,0},{2,3},{3,2},{4,5},{5,4},{6,7},{7,6},{8,9},{9,8},{10,11... | collective-permute-start | bytes 2359304 | tf_op jit(solution)/shard_map/ppermute | solution.py:769
  220.5 24.8 %attend_back.2 = (bf16[3,3,64,512]{3,2,1,0:T(8,128)(2,1)}, bf16[4,384,512]{2,1,0:T(8,128)(2,1)}) custom-call(s32[7]{0:T(128)} %stack.112.info, bf16[3,3,64,512]{3,2,1,0:T(8,128)(2,1)} %bitcast.176, bf16[4,384,512]{2,1,0:T(8,128)(2,1)} %bitcast.169, s32[1,512]{1,0:T(1,128)} %bitcast.182, bf16[3,3,64,512]{3,2,1,0:T(8,128)(2,1)} %get-tuple-element.163.o_ref, ...), custom_call_target="tpu_custom_call" | custom-call | flops 6039797760 | bytes 8000000 | tf_op jit(solution)/shard_map/attend_back/pallas_call | solution.py:291
  245.3 2.2 dynamic-slice_bitcast_fusion.5
  250.6 1.6 fusion.6
  252.2 1.4 collective-permute-start.3
  253.6 5.8 %collective-permute-done.5 = bf16[384,512]{1,0:T(8,128)(2,1)S(1)} collective-permute-done((bf16[384,512]{1,0:T(8,128)(2,1)S(1)}, bf16[384,512]{1,0:T(8,128)(2,1)S(1)}, u32[]{:S(2)}, u32[]{:S(2)}) %collective-permute-start.5) | collective-permute-done | bytes 393248 | tf_op jit(solution)/shard_map/ppermute | solution.py:769
  260.2 7.6 %collective-permute-done.3 = bf16[384,512]{1,0:T(8,128)(2,1)S(1)} collective-permute-done((bf16[384,512]{1,0:T(8,128)(2,1)S(1)}, bf16[384,512]{1,0:T(8,128)(2,1)S(1)}, u32[]{:S(2)}, u32[]{:S(2)}) %collective-permute-start.3) | collective-permute-done | bytes 393248 | tf_op jit(solution)/shard_map/ppermute | solution.py:769
  268.6 5.1 %projection_grads.1 = (bf16[8,144,768]{2,1,0:T(8,128)(2,1)}, bf16[960,1024]{1,0:T(8,128)(2,1)}) custom-call(bf16[1024,576]{1,0:T(8,128)(2,1)} %copy-done.1, bf16[576,512]{1,0:T(8,128)(2,1)} %bitcast.178, bf16[576,512]{1,0:T(8,128)(2,1)} %bitcast.177, bf16[384,512]{1,0:T(8,128)(2,1)} %fusion.10.dkv0_ref, bf16[384,512]{1,0:T(8,128)(2,1)} %fusion.9.dkv1_ref, ...), custom_call_target="tpu_custom_call" | custom-call | flops 1132462080 | bytes 8000000 | tf_op jit(solution)/shard_map/projection_grads/pallas_call | solution.py:453
  273.8 3.2 fusion
  279.0 1.4 collective-permute-start.7
  281.1 1.4 collective-permute-done.7
  282.6 1.6 fusion.4
  285.5 25.3 %collective-permute-done.11 = bf16[2,3,144,768]{3,2,1,0:T(8,128)(2,1)} collective-permute-done((bf16[2,3,144,768]{3,2,1,0:T(8,128)(2,1)}, bf16[2,3,144,768]{3,2,1,0:T(8,128)(2,1)}, u32[]{:S(2)}, u32[]{:S(2)}) %collective-permute-start.11) | collective-permute-done | bytes 1327136 | tf_op jit(solution)/shard_map/ppermute | solution.py:644
  310.8 1.6 fusion.1
  313.6 16.1 %collective-permute-start.12 = (bf16[1,3,144,768]{3,2,1,0:T(8,128)(2,1)S(1)}, bf16[1,3,144,768]{3,2,1,0:T(8,128)(2,1)}, u32[]{:S(2)}, u32[]{:S(2)}) collective-permute-start(bf16[1,3,144,768]{3,2,1,0:T(8,128)(2,1)S(1)} %constant_dynamic-slice_fusion.3), channel_id=1, source_target_pairs={{0,4},{4,0},{1,5},{5,1},{2,6},{6,2},{3,7},{7,3},{8,12},{12,8},{9,1... | collective-permute-start | bytes 1990664 | tf_op jit(solution)/shard_map/ppermute | solution.py:644
  330.8 6.7 %collective-permute-start.9 = (bf16[1,144,768]{2,1,0:T(8,128)(2,1)S(1)}, bf16[1,144,768]{2,1,0:T(8,128)(2,1)S(1)}, u32[]{:S(2)}, u32[]{:S(2)}) collective-permute-start(bf16[1,144,768]{2,1,0:T(8,128)(2,1)S(1)} %constant_dynamic-slice_fusion.4), channel_id=1, source_target_pairs={{0,4},{4,0},{1,5},{5,1},{2,6},{6,2},{3,7},{7,3},{8,12},{12,8},{9,1... | collective-permute-start | bytes 663560 | tf_op jit(solution)/shard_map/ppermute | solution.py:644
  337.5 8.7 %collective-permute-done.9 = bf16[1,144,768]{2,1,0:T(8,128)(2,1)S(1)} collective-permute-done((bf16[1,144,768]{2,1,0:T(8,128)(2,1)S(1)}, bf16[1,144,768]{2,1,0:T(8,128)(2,1)S(1)}, u32[]{:S(2)}, u32[]{:S(2)}) %collective-permute-start.9) | collective-permute-done | bytes 221216 | tf_op jit(solution)/shard_map/ppermute | solution.py:644
  348.2 2.0 collective-permute-start.14
  350.6 1.4 fusion.12
  353.1 5.8 %collective-permute-start.1 = (bf16[512,576]{0,1:T(8,128)(2,1)}, bf16[512,576]{0,1:T(8,128)(2,1)}, u32[]{:S(2)}, u32[]{:S(2)}) collective-permute-start(bf16[512,576]{0,1:T(8,128)(2,1)} %copy.63), channel_id=1, source_target_pairs={{0,3},{3,0},{1,2},{2,1},{4,7},{7,4},{5,6},{6,5},{8,11},{11,8},{9,1... | collective-permute-start | bytes 1769480 | tf_op jit(solution)/shard_map/ppermute | solution.py:744
  359.0 8.7 %collective-permute-done.14 = bf16[144,768]{1,0:T(8,128)(2,1)S(1)} collective-permute-done((bf16[144,768]{1,0:T(8,128)(2,1)S(1)}, bf16[144,768]{1,0:T(8,128)(2,1)S(1)}, u32[]{:S(2)}, u32[]{:S(2)}) %collective-permute-start.14) | collective-permute-done | bytes 221216 | tf_op jit(solution)/shard_map/ppermute | solution.py:663
  369.2 3.9 collective-permute-done.16
  374.6 5.6 %conditional.4 = (bf16[576,1536]{1,0:T(8,128)(2,1)}) conditional(s32[]{:T(128)} %clamp.7, bf16[884736]{0:T(1024)(128)(2,1)} %all-gather.9.cloned.1.call-done, bf16[884736]{0:T(1024)(128)(2,1)} %all-gather.9.cloned.1.call-done, bf16[884736]{0:T(1024)(128)(2,1)} %all-gather.9.cloned.1.call-done, ...), branch_computations={%region_5.6_spmd, %region_6.7_spmd, %region_7.8_spmd, %region_8.9_... | conditional | bytes 10616840 | solution.py:581
  374.6 3.3 reshape.524
  377.9 2.3 copy.58
  380.2 2.5 slice.319
  382.7 1.4 copy.64
  385.2 6.3 %input_grads.1 = (f32[512,576]{1,0:T(8,128)}, bf16[512,576]{1,0:T(8,128)(2,1)}, f32[1,576]{1,0:T(1,128)}) custom-call(bf16[960,1024]{1,0:T(8,128)(2,1)} %get-tuple-element.175.all_ref, bf16[576,960]{1,0:T(8,128)(2,1)} %copy-done, bf16[2,512,576]{2,1,0:T(8,128)(2,1)} %pad_maximum_fusion.3.x_ref, f32[2,512,576]{2,1,0:T(8,128)} %get-tuple-element.176.dh_ref, ...), custom_call_target="tpu_custom_call" | custom-call | flops 1132462080 | bytes 8000000 | tf_op jit(solution)/shard_map/input_grads/pallas_call | solution.py:485
  391.5 2.1 copy.67
  393.7 5.4 %collective-permute-start.6 = (bf16[512,576]{0,1:T(8,128)(2,1)}, bf16[512,576]{0,1:T(8,128)(2,1)}, u32[]{:S(2)}, u32[]{:S(2)}) collective-permute-start(bf16[512,576]{0,1:T(8,128)(2,1)} %copy.67), channel_id=1, source_target_pairs={{0,3},{3,0},{1,2},{2,1},{4,7},{7,4},{5,6},{6,5},{8,11},{11,8},{9,1... | collective-permute-start | bytes 1769480 | tf_op jit(solution)/shard_map/ppermute | solution.py:778
  400.1 1.9 pad_maximum_fusion
  402.0 2.0 copy.71
  404.1 37.8 %all-gather.2 = f32[32,2,576]{2,1,0:T(2,128)S(1)} all-gather(f32[1,2,576]{2,1,0:T(2,128)S(1)} %maximum_bitcast_fusion), channel_id=3, replica_groups=mesh['quarter'=4,'rep'=1,'half'=2,'ctx'=4] {'quarter','rep','half','ctx'}, dimensions={0}, use_global_device_ids=true | all-gather | bytes 152064 | tf_op jit(solution)/shard_map/all_gather | solution.py:780
  442.6 1.4 copy.68
  444.0 1.5 pad_maximum_fusion.1
  445.5 2.0 copy.72
  447.5 2.7 pad_maximum_fusion.2.pieces_ref
  450.3 27.5 %newton.1 = (bf16[576,1536]{1,0:T(8,128)(2,1)}, f32[576,1536]{1,0:T(8,128)S(1)}) custom-call(s32[2]{0:T(128)} %pad_add_fusion.info, bf16[8,144,768]{2,1,0:T(8,128)(2,1)} %pad_maximum_fusion.2.pieces_ref, bf16[576,1536]{1,0:T(8,128)(2,1)S(1)} %copy-done.15), custom_call_target="tpu_custom_call" | custom-call | flops 12000000000 | bytes 9000000 | tf_op jit(solution)/shard_map/newton/pallas_call | solution.py:544
  477.7 11.5 %conditional.5 = (f32[110592]{0:T(1024)}, f32[110592]{0:T(1024)}) conditional(s32[]{:T(128)} %clamp.6, (s32[]{:T(128)}, pred[]{:T(512)}, s32[]{:T(128)}, f32[576,1536]{1,0:T(8,128)S(1)}, bf16[576,1536]{1,0:T(8,128)(2,1)}) %tuple.85, (s32[]{:T(128)}, pred[]{:T(512)}, s32[]{:T(128)}, f32[576,1536]{1,0:T(8,128)S(1)}, ...), branch_computations={%region_9.10_spmd.clone, %region_10.11_spmd.clone, %region_11.12_s... | conditional | flops 110605 | bytes 21012680
  479.7 3.1 copy.69
  485.0 2.3 copy.70
  489.2 2.0 multiply_add_fusion.2
  491.2 2.0 multiply_subtract_fusion.2
  (167 shorter events, 48.6 us)
Async XLA Ops:
  8.0 77.2 %all-gather.7.cloned.1.call-start = ((), (), s32[]{:S(2)}) async-start(), calls=%async_computation | async-start | bytes 7299072 | tf_op jit(solution)/shard_map/all_gather | solution.py:687
  9.8 117.4 %all-gather.11.cloned.1.call-start = ((), (), s32[]{:S(2)}) async-start(), calls=%async_computation.2 | async-start | bytes 3932160 | tf_op jit(solution)/shard_map/all_gather | solution.py:726
  11.6 1.9 copy-start.27
  12.8 17.6 %copy-start.22 = (f32[2,576]{1,0:T(2,128)S(1)}, f32[2,576]{1,0:T(2,128)}, u32[]{:S(2)}) copy-start(f32[2,576]{1,0:T(2,128)} %param.24) | copy-start | bytes 13828
  12.8 31.4 %collective-permute-start = (bf16[2,512,576]{1,2,0:T(8,128)(2,1)}, bf16[2,512,576]{1,2,0:T(8,128)(2,1)S(1)}, u32[]{:S(2)}, u32[]{:S(2)}) collective-permute-start(bf16[2,512,576]{1,2,0:T(8,128)(2,1)} %pad_maximum_fusion.6), channel_id=1, source_target_pairs={{0,3},{3,0},{1,2},{2,1},{4,7},{7,4},{5,6},{6,5},{8,11},{11,8},{9,1... | collective-permute-start | bytes 3538952 | tf_op jit(solution)/shard_map/ppermute | solution.py:703
  14.0 31.0 %copy-start.23 = (s32[512]{0:T(512)}, s32[512]{0:T(512)S(1)}, u32[]{:S(2)}) copy-start(s32[512]{0:T(512)S(1)} %get-tuple-element.334) | copy-start | bytes 6148
  14.0 31.0 %copy-start.24 = (s32[512]{0:T(512)}, s32[512]{0:T(512)S(1)}, u32[]{:S(2)}) copy-start(s32[512]{0:T(512)S(1)} %get-tuple-element.333) | copy-start | bytes 6148
  50.1 42.4 %copy-start.1 = (bf16[1024,576]{1,0:T(8,128)(2,1)}, bf16[1024,576]{1,0:T(8,128)(2,1)S(1)}, u32[]{:S(2)}) copy-start(bf16[1024,576]{1,0:T(8,128)(2,1)S(1)} %fusion.3.n_ref) | copy-start | bytes 3538948
  91.5 1.1 copy-start
  93.6 1.3 copy-start.2
  94.8 0.8 copy-start.20
  94.8 0.9 copy-start.21
  95.0 1.4 slice-start
  95.0 1.4 copy-start.18
  95.0 1.4 copy-start.19
  96.0 0.8 copy-start.6
  96.0 0.9 copy-start.8
  96.7 0.7 copy-start.10
  96.7 0.9 copy-start.12
  98.5 276.1 %all-gather.9.cloned.1.call-start = ((), (), s32[]{:S(2)}) async-start(), calls=%async_computation.1 | async-start | bytes 1990656 | tf_op jit(solution)/shard_map/all_gather | solution.py:747
  109.9 5.4 %copy-start.11 = (bf16[12,1,32,512]{3,2,1,0:T(8,128)(2,1)S(1)}, bf16[12,1,32,512]{3,2,1,0:T(8,128)(2,1)}, u32[]{:S(2)}) copy-start(bf16[12,1,32,512]{3,2,1,0:T(8,128)(2,1)} %copy-done.10) | copy-start | bytes 1179652
  109.9 5.4 %copy-start.13 = (bf16[12,1,32,512]{3,2,1,0:T(8,128)(2,1)S(1)}, bf16[12,1,32,512]{3,2,1,0:T(8,128)(2,1)}, u32[]{:S(2)}) copy-start(bf16[12,1,32,512]{3,2,1,0:T(8,128)(2,1)} %copy-done.12) | copy-start | bytes 1179652
  112.9 3.4 copy-start.7
  112.9 3.4 copy-start.9
  194.9 78.9 %collective-permute-start.10 = (bf16[4,3,144,768]{3,2,1,0:T(8,128)(2,1)}, bf16[4,3,144,768]{3,2,1,0:T(8,128)(2,1)}, u32[]{:S(2)}, u32[]{:S(2)}) collective-permute-start(bf16[4,3,144,768]{3,2,1,0:T(8,128)(2,1)} %dynamic-slice_bitcast_fusion.1), channel_id=1, source_target_pairs={{0,1},{1,0},{2,3},{3,2},{4,5},{5,4},{6,7},{7,6},{8,9},{9,8},{10,11... | collective-permute-start | bytes 7962632 | tf_op jit(solution)/shard_map/ppermute | solution.py:644
  212.7 35.6 %collective-permute-start.4 = (bf16[2,384,512]{2,1,0:T(8,128)(2,1)S(1)}, bf16[2,384,512]{2,1,0:T(8,128)(2,1)S(1)}, u32[]{:S(2)}, u32[]{:S(2)}) collective-permute-start(bf16[2,384,512]{2,1,0:T(8,128)(2,1)S(1)} %dynamic-slice_bitcast_fusion.4), channel_id=1, source_target_pairs={{0,1},{1,0},{2,3},{3,2},{4,5},{5,4},{6,7},{7,6},{8,9},{9,8},{10,11... | collective-permute-start | bytes 2359304 | tf_op jit(solution)/shard_map/ppermute | solution.py:769
  245.3 3.0 copy-start.17
  247.5 3.1 collective-permute-start.2
  248.6 10.8 %collective-permute-start.5 = (bf16[384,512]{1,0:T(8,128)(2,1)S(1)}, bf16[384,512]{1,0:T(8,128)(2,1)S(1)}, u32[]{:S(2)}, u32[]{:S(2)}) collective-permute-start(bf16[384,512]{1,0:T(8,128)(2,1)S(1)} %dynamic-slice_bitcast_fusion.7), channel_id=1, source_target_pairs={{0,2},{2,0},{1,3},{3,1},{4,6},{6,4},{5,7},{7,5},{8,10},{10,8},{9,1... | collective-permute-start | bytes 1179656 | tf_op jit(solution)/shard_map/ppermute | solution.py:769
  252.2 15.6 %collective-permute-start.3 = (bf16[384,512]{1,0:T(8,128)(2,1)S(1)}, bf16[384,512]{1,0:T(8,128)(2,1)S(1)}, u32[]{:S(2)}, u32[]{:S(2)}) collective-permute-start(bf16[384,512]{1,0:T(8,128)(2,1)S(1)} %dynamic-slice_bitcast_fusion.8), channel_id=1, source_target_pairs={{0,2},{2,0},{1,3},{3,1},{4,6},{6,4},{5,7},{7,5},{8,10},{10,8},{9,1... | collective-permute-start | bytes 1179656 | tf_op jit(solution)/shard_map/ppermute | solution.py:769
  277.0 2.0 copy-start.14
  277.0 3.4 copy-start.16
  278.2 32.6 %collective-permute-start.11 = (bf16[2,3,144,768]{3,2,1,0:T(8,128)(2,1)}, bf16[2,3,144,768]{3,2,1,0:T(8,128)(2,1)}, u32[]{:S(2)}, u32[]{:S(2)}) collective-permute-start(bf16[2,3,144,768]{3,2,1,0:T(8,128)(2,1)} %dynamic-slice_bitcast_fusion.2), channel_id=1, source_target_pairs={{0,2},{2,0},{1,3},{3,1},{4,6},{6,4},{5,7},{7,5},{8,10},{10,8},{9,1... | collective-permute-start | bytes 3981320 | tf_op jit(solution)/shard_map/ppermute | solution.py:644
  279.0 3.5 collective-permute-start.7
  285.0 44.7 %collective-permute-start.8 = (bf16[2,144,768]{2,1,0:T(8,128)(2,1)}, bf16[2,144,768]{2,1,0:T(8,128)(2,1)}, u32[]{:S(2)}, u32[]{:S(2)}) collective-permute-start(bf16[2,144,768]{2,1,0:T(8,128)(2,1)} %dynamic-slice_bitcast_fusion.6), channel_id=1, source_target_pairs={{0,2},{2,0},{1,3},{3,1},{4,6},{6,4},{5,7},{7,5},{8,10},{10,8},{9,1... | collective-permute-start | bytes 1327112 | tf_op jit(solution)/shard_map/ppermute | solution.py:644
  312.4 1.1 copy-start.4
  313.6 32.8 %copy-start.5 = (bf16[2,3,144,768]{3,2,1,0:T(8,128)(2,1)S(1)}, bf16[2,3,144,768]{3,2,1,0:T(8,128)(2,1)}, u32[]{:S(2)}) copy-start(bf16[2,3,144,768]{3,2,1,0:T(8,128)(2,1)} %copy-done.4) | copy-start | bytes 3981316
  313.6 32.7 %collective-permute-start.12 = (bf16[1,3,144,768]{3,2,1,0:T(8,128)(2,1)S(1)}, bf16[1,3,144,768]{3,2,1,0:T(8,128)(2,1)}, u32[]{:S(2)}, u32[]{:S(2)}) collective-permute-start(bf16[1,3,144,768]{3,2,1,0:T(8,128)(2,1)S(1)} %constant_dynamic-slice_fusion.3), channel_id=1, source_target_pairs={{0,4},{4,0},{1,5},{5,1},{2,6},{6,2},{3,7},{7,3},{8,12},{12,8},{9,1... | collective-permute-start | bytes 1990664 | tf_op jit(solution)/shard_map/ppermute | solution.py:644
  330.8 15.4 %collective-permute-start.9 = (bf16[1,144,768]{2,1,0:T(8,128)(2,1)S(1)}, bf16[1,144,768]{2,1,0:T(8,128)(2,1)S(1)}, u32[]{:S(2)}, u32[]{:S(2)}) collective-permute-start(bf16[1,144,768]{2,1,0:T(8,128)(2,1)S(1)} %constant_dynamic-slice_fusion.4), channel_id=1, source_target_pairs={{0,4},{4,0},{1,5},{5,1},{2,6},{6,2},{3,7},{7,3},{8,12},{12,8},{9,1... | collective-permute-start | bytes 663560 | tf_op jit(solution)/shard_map/ppermute | solution.py:644
  347.8 11.1 %collective-permute-start.13 = (bf16[144,768]{1,0:T(8,128)(2,1)S(1)}, bf16[144,768]{1,0:T(8,128)(2,1)S(1)}, u32[]{:S(2)}, u32[]{:S(2)}) collective-permute-start(bf16[144,768]{1,0:T(8,128)(2,1)S(1)} %get-tuple-element.309), channel_id=1, source_target_pairs={{0,8},{8,16},{16,24},{24,0},{1,9},{9,17},{17,25},{25,1},{2,10},{10... | collective-permute-start | bytes 663560 | tf_op jit(solution)/shard_map/ppermute | solution.py:663
  348.2 19.4 %collective-permute-start.14 = (bf16[144,768]{1,0:T(8,128)(2,1)S(1)}, bf16[144,768]{1,0:T(8,128)(2,1)S(1)}, u32[]{:S(2)}, u32[]{:S(2)}) collective-permute-start(bf16[144,768]{1,0:T(8,128)(2,1)S(1)} %get-tuple-element.310), channel_id=1, source_target_pairs={{0,16},{8,24},{16,0},{24,8},{1,17},{9,25},{17,1},{25,9},{2,18},{10... | collective-permute-start | bytes 663560 | tf_op jit(solution)/shard_map/ppermute | solution.py:663
  350.2 17.4 %collective-permute-start.15 = (bf16[144,768]{1,0:T(8,128)(2,1)S(1)}, bf16[144,768]{1,0:T(8,128)(2,1)S(1)}, u32[]{:S(2)}, u32[]{:S(2)}) collective-permute-start(bf16[144,768]{1,0:T(8,128)(2,1)S(1)} %get-tuple-element.311), channel_id=1, source_target_pairs={{0,24},{8,0},{16,8},{24,16},{1,25},{9,1},{17,9},{25,17},{2,26},{10... | collective-permute-start | bytes 663560 | tf_op jit(solution)/shard_map/ppermute | solution.py:663
  352.0 15.9 %copy-start.30 = (s32[4]{0:T(128)S(1)}, s32[4]{0:T(128)}, u32[]{:S(2)}) copy-start(s32[4]{0:T(128)} %constant.315.clone) | copy-start | bytes 52
  353.1 29.6 %collective-permute-start.1 = (bf16[512,576]{0,1:T(8,128)(2,1)}, bf16[512,576]{0,1:T(8,128)(2,1)}, u32[]{:S(2)}, u32[]{:S(2)}) collective-permute-start(bf16[512,576]{0,1:T(8,128)(2,1)} %copy.63), channel_id=1, source_target_pairs={{0,3},{3,0},{1,2},{2,1},{4,7},{7,4},{5,6},{6,5},{8,11},{11,8},{9,1... | collective-permute-start | bytes 1769480 | tf_op jit(solution)/shard_map/ppermute | solution.py:744
  367.8 5.2 %collective-permute-start.16 = (bf16[1,144,768]{2,1,0:T(8,128)(2,1)S(1)}, bf16[1,144,768]{2,1,0:T(8,128)(2,1)S(1)}, u32[]{:S(2)}, u32[]{:S(2)}) collective-permute-start(bf16[1,144,768]{2,1,0:T(8,128)(2,1)S(1)} %fusion.21), channel_id=1, source_target_pairs={{0,4},{4,0},{1,5},{5,1},{2,6},{6,2},{3,7},{7,3},{8,12},{12,8},{9,1... | collective-permute-start | bytes 663560 | tf_op jit(solution)/shard_map/ppermute | solution.py:652
  373.9 25.2 %collective-permute-start.17 = (bf16[2,144,768]{2,1,0:T(8,128)(2,1)}, bf16[2,144,768]{2,1,0:T(8,128)(2,1)S(1)}, u32[]{:S(2)}, u32[]{:S(2)}) collective-permute-start(bf16[2,144,768]{2,1,0:T(8,128)(2,1)} %pad_maximum_fusion.9), channel_id=1, source_target_pairs={{0,2},{2,0},{1,3},{3,1},{4,6},{6,4},{5,7},{7,5},{8,10},{10,8},{9,1... | collective-permute-start | bytes 1327112 | tf_op jit(solution)/shard_map/ppermute | solution.py:652
  393.7 48.9 %collective-permute-start.6 = (bf16[512,576]{0,1:T(8,128)(2,1)}, bf16[512,576]{0,1:T(8,128)(2,1)}, u32[]{:S(2)}, u32[]{:S(2)}) collective-permute-start(bf16[512,576]{0,1:T(8,128)(2,1)} %copy.67), channel_id=1, source_target_pairs={{0,3},{3,0},{1,2},{2,1},{4,7},{7,4},{5,6},{6,5},{8,11},{11,8},{9,1... | collective-permute-start | bytes 1769480 | tf_op jit(solution)/shard_map/ppermute | solution.py:778
  400.1 47.4 %collective-permute-start.18 = (bf16[4,144,768]{2,1,0:T(8,128)(2,1)}, bf16[4,144,768]{2,1,0:T(8,128)(2,1)}, u32[]{:S(2)}, u32[]{:S(2)}) collective-permute-start(bf16[4,144,768]{2,1,0:T(8,128)(2,1)} %pad_maximum_fusion.8), channel_id=1, source_target_pairs={{0,1},{1,0},{2,3},{3,2},{4,5},{5,4},{6,7},{7,6},{8,9},{9,8},{10,11... | collective-permute-start | bytes 2654216 | tf_op jit(solution)/shard_map/ppermute | solution.py:652
  402.0 2.0 copy-start.28
  402.0 2.0 copy-start.29
  402.0 39.9 %copy-start.25 = (f32[2,576]{1,0:T(2,128)S(1)}, f32[2,576]{1,0:T(2,128)}, u32[]{:S(2)}) copy-start(f32[2,576]{1,0:T(2,128)} %param.26) | copy-start | bytes 13828
  402.0 39.9 %copy-start.26 = (f32[2,576]{1,0:T(2,128)S(1)}, f32[2,576]{1,0:T(2,128)}, u32[]{:S(2)}) copy-start(f32[2,576]{1,0:T(2,128)} %param.25) | copy-start | bytes 13828
  447.5 2.7 copy-start.15
  482.8 2.2 copy-start.3
Sparse Core Ops, SparseCore 0:
  12.3 72.8 all-gather.6
  98.6 28.4 all-gather.10
Sparse Core Ops, SparseCore 1:
  281.2 44.7 all-gather.8

commit v3 on v2

--- a/solution.py
+++ b/solution.py
@@ -61,27 +61,6 @@
     return (jnp.cos(angles), jnp.sin(angles))
 
 
-def rotate_columns(values, cosine, sine):
-    shaped = values.reshape(-1, 2, HEAD_DIM // 2, values.shape[-1])
-    former, latter = shaped[:, 0], shaped[:, 1]
-    return jnp.stack(
-        [former * cosine - latter * sine, latter * cosine + former * sine], axis=1
-    ).reshape(values.shape)
-
-
-def normalize(values, gain):
-    scaling = lax.rsqrt(jnp.mean(values * values, axis=-1, keepdims=True) + norm_epsilon)
-    return values * scaling * gain
-
-
-def normalize_back(values, gain, upstream):
-    scaling = lax.rsqrt(jnp.mean(values * values, axis=-1, keepdims=True) + norm_epsilon)
-    weighted = upstream * gain
-    gain_grad = jnp.sum(upstream * values * scaling, axis=0)
-    inner_term = jnp.mean(weighted * values, axis=-1, keepdims=True)
-    return (scaling * weighted - values * (scaling * scaling * scaling) * inner_term, gain_grad)
-
-
 def dot32(left, right):
     return jnp.dot(left, right, preferred_element_type=jnp.float32)
 
@@ -113,22 +92,31 @@
     return step(True, 1, last, carry)
 
 
-def forward_kernel(backward_order, info, q_ref, kv_ref, begin_ref, o_ref, lse_ref, k_nat, v_ext):
+def key_slots(own, micro, kv_ref, other_ref, far_ref, far_other_ref):
+    refs = (kv_ref.at[micro], other_ref.at[micro], far_ref, far_other_ref)
+    return [(own ^ place, ref) for place, ref in enumerate(refs)]
+
+
+def block_rows(block):
+    return pl.ds(pl.multiple_of(block * TOK, TOK), TOK)
+
+
+def forward_kernel(
+    micro, info, q_ref, kv_ref, other_ref, far_ref, far_other_ref, begin_ref, tie_ref,
+    o_ref, lse_ref, k_nat, v_ext,
+):
     own = info[0]
-    for block in range(4):
+    for block, source in key_slots(own, micro, kv_ref, other_ref, far_ref, far_other_ref):
 
         @pl.when(block <= own)
         def _():
+            rows = block_rows(block)
             for group in range(KV_HEADS):
                 low = HEAD_DIM * group
-                source = 3 - block if backward_order else block
-                k_nat[group, TOK * block : TOK * (block + 1), :] = kv_ref[
-                    source, low : low + HEAD_DIM, :
-                ].T
+                k_nat[group, rows, :] = source[low : low + HEAD_DIM, :].T
                 low = low + KV_WIDTH
-                columns = slice(TOK * block, TOK * (block + 1))
-                v_ext[group, :HEAD_DIM, columns] = kv_ref[source, low : low + HEAD_DIM, :]
-                v_ext[group, HEAD_DIM:, columns] = jnp.ones((16, TOK), jnp.bfloat16)
+                v_ext[group, :HEAD_DIM, rows] = source[low : low + HEAD_DIM, :]
+                v_ext[group, HEAD_DIM:, rows] = jnp.ones((16, TOK), jnp.bfloat16)
 
     def one_group(group, unused):
         for tile in range(TOK // TILE):
@@ -169,22 +157,23 @@
 
 
 def backward_kernel(
-    backward_order, info, q_ref, kv_ref, begin_ref, o_ref, lse_ref, do_ref, cos_ref, sin_ref,
-    dq_ref, dkv_ref, k_nat, v_nat, k_tall, dk_ref, dv_ref,
+    micro, info, q_ref, kv_ref, other_ref, far_ref, far_other_ref, begin_ref, o_ref, lse_ref,
+    do_ref, cos_ref, sin_ref, tie_ref,
+    dq_ref, keep_ref, send_ref, k_nat, v_nat, k_tall, dk_ref, dv_ref,
 ):
     own = info[0]
-    for block in range(4):
+    slots = key_slots(own, micro, kv_ref, other_ref, far_ref, far_other_ref)
+    for block, source in slots:
 
         @pl.when(block <= own)
         def _():
-            rows = slice(TOK * block, TOK * (block + 1))
+            rows = block_rows(block)
             for group in range(KV_HEADS):
                 low = HEAD_DIM * group
-                source = 3 - block if backward_order else block
-                k_nat[group, rows, :] = kv_ref[source, low : low + HEAD_DIM, :].T
-                k_tall[group, :, rows] = kv_ref[source, low : low + HEAD_DIM, :]
+                k_nat[group, rows, :] = source[low : low + HEAD_DIM, :].T
+                k_tall[group, :, rows] = source[low : low + HEAD_DIM, :]
                 low = low + KV_WIDTH
-                v_nat[group, rows, :] = kv_ref[source, low : low + HEAD_DIM, :].T
+                v_nat[group, rows, :] = source[low : low + HEAD_DIM, :].T
                 dk_ref[group, rows, :] = jnp.zeros((TOK, HEAD_DIM), jnp.float32)
                 dv_ref[group, rows, :] = jnp.zeros((TOK, HEAD_DIM), jnp.float32)
 
@@ -231,25 +220,25 @@
         return unused
 
     lax.fori_loop(0, KV_HEADS, one_group, 0)
-    for block in range(4):
-        rows = slice(TOK * block, TOK * (block + 1))
-        target = 3 - block if backward_order else block
+    for place, (block, _) in enumerate(slots):
+        out_ref = (keep_ref, send_ref)[place % 2]
 
         @pl.when(block <= own)
         def _():
+            rows = block_rows(block)
             for group in range(KV_HEADS):
                 low = HEAD_DIM * group
-                dkv_ref[target, low : low + HEAD_DIM, :] = dk_ref[group, rows, :].T.astype(
+                out_ref[place // 2, low : low + HEAD_DIM, :] = dk_ref[group, rows, :].T.astype(
                     jnp.bfloat16
                 )
                 low = low + KV_WIDTH
-                dkv_ref[target, low : low + HEAD_DIM, :] = dv_ref[group, rows, :].T.astype(
+                out_ref[place // 2, low : low + HEAD_DIM, :] = dv_ref[group, rows, :].T.astype(
                     jnp.bfloat16
                 )
 
         @pl.when(block > own)
         def _():
-            dkv_ref[target] = jnp.zeros((2 * KV_WIDTH, TOK), jnp.bfloat16)
+            out_ref[place // 2] = jnp.zeros((2 * KV_WIDTH, TOK), jnp.bfloat16)
 
 
 def vmem():
@@ -260,18 +249,22 @@
     return pl.BlockSpec(memory_space=pltpu.SMEM)
 
 
+def anywhere():
+    return pl.BlockSpec(memory_space=pl.ANY)
+
+
 kernel_params = pltpu.CompilerParams(vmem_limit_bytes=56 * 1024 * 1024)
 heads_shape = (KV_HEADS, GROUPS, HEAD_DIM, TOK)
 
 
-def attend_forward(backward_order, info, queries, keyvals, begins):
+def attend_forward(micro, info, queries, keyvals, begins, tie):
     return pl.pallas_call(
-        partial(forward_kernel, backward_order),
+        partial(forward_kernel, micro),
         out_shape=(
             jax.ShapeDtypeStruct(heads_shape, jnp.bfloat16),
             jax.ShapeDtypeStruct((KV_HEADS, GROUPS, 1, TOK), jnp.float32),
         ),
-        in_specs=[smem(), vmem(), vmem(), vmem()],
+        in_specs=[smem()] + [vmem()] * 6 + [anywhere()],
         out_specs=(vmem(), vmem()),
         scratch_shapes=[
             pltpu.VMEM((KV_HEADS, 4 * TOK, HEAD_DIM), jnp.bfloat16),
@@ -282,20 +275,22 @@
             flops=4 * 9 * 64 * TOK * 2048, bytes_accessed=4000000, transcendentals=9 * TOK * 2048
         ),
         name="attend_forward",
-    )(info, queries, keyvals, begins)
+    )(info, queries, *keyvals, begins, tie)
 
 
 def attend_back(
-    backward_order, info, queries, keyvals, begins, mixed, log_total, grad_mixed, cosine, sine
+    micro, info, queries, keyvals, begins, mixed, log_total, grad_mixed, cosine, sine, tie
 ):
+    half_shape = (2, 2 * KV_WIDTH, TOK)
     return pl.pallas_call(
-        partial(backward_kernel, backward_order),
+        partial(backward_kernel, micro),
         out_shape=(
             jax.ShapeDtypeStruct(heads_shape, jnp.bfloat16),
-            jax.ShapeDtypeStruct((4, 2 * KV_WIDTH, TOK), jnp.bfloat16),
-        ),
-        in_specs=[smem()] + [vmem()] * 8,
-        out_specs=(vmem(), vmem()),
+            jax.ShapeDtypeStruct(half_shape, jnp.bfloat16),
+            jax.ShapeDtypeStruct(half_shape, jnp.bfloat16),
+        ),
+        in_specs=[smem()] + [vmem()] * 11 + [anywhere()],
+        out_specs=(vmem(),) * 3,
         scratch_shapes=[
             pltpu.VMEM((KV_HEADS, 4 * TOK, HEAD_DIM), jnp.bfloat16),
             pltpu.VMEM((KV_HEADS, 4 * TOK, HEAD_DIM), jnp.bfloat16),
@@ -308,7 +303,7 @@
             flops=10 * 9 * 64 * TOK * 2048, bytes_accessed=8000000, transcendentals=9 * TOK * 2048
         ),
         name="attend_back",
-    )(info, queries, keyvals, begins, mixed, log_total, grad_mixed, cosine, sine)
+    )(info, queries, *keyvals, begins, mixed, log_total, grad_mixed, cosine, sine, tie)
 
 
 def dot_with(left, right, left_side, right_side):
@@ -324,17 +319,17 @@
     return (scaling * weighted - values * (scaling * scaling * scaling) * inner, gain_grad)
 
 
-def store_chunks(matrix, column, put):
-    half, low = column // (FF // COL_CUT), column % (FF // COL_CUT)
-    for row in range(ROW_CUT):
-        part = matrix[row * CHUNK_ROWS : (row + 1) * CHUNK_ROWS].astype(jnp.bfloat16)
-        put(row * COL_CUT + half, slice(low, low + matrix.shape[1]), part)
+def row_parts(held, spot, side):
+    for turn in range(ROW_CUT):
+        start = (turn ^ (spot // COL_CUT)) * CHUNK_ROWS
+        part = held[pl.ds(pl.multiple_of(start, CHUNK_ROWS), CHUNK_ROWS), :]
+        yield (turn * COL_CUT + side, part.astype(jnp.bfloat16))
 
 
 def mlp_kernel(
-    x_ref, c_ref, o0_ref, o1_ref, wo_ref, wg_ref, wu_ref, wd_ref, gain_ref,
-    out_ref, dh_ref, do0_ref, do1_ref, early_ref, gwo_ref, gg_ref,
-    hid, dgate, dup, n2_tall, c_tall, dh_low,
+    info, x_ref, c_ref, o0_ref, o1_ref, wo_ref, wg_ref, wu_ref, wd_ref, gain_ref,
+    out_ref, dh_ref, do0_ref, do1_ref, keep_ref, send_ref, gwo_ref, gg_ref,
+    hid, dgate, dup, n2_tall, c_tall, dh_low, held,
 ):
     gain = gain_ref[...]
     gg_ref[...] = jnp.zeros((1, D), jnp.float32)
@@ -372,20 +367,21 @@
         low = grad_state.astype(jnp.bfloat16)
         dh_low[rows, :] = low
         do_ref[...] = dot_with(wo_ref[...], low, 1, 1).astype(jnp.bfloat16)
-    for column in range(0, FF, block):
-        columns = slice(column, column + block)
-        for place, (left, right) in enumerate(((n2_tall, dgate), (n2_tall, dup), (c_tall, hid))):
-
-            def put(spot, where, part):
-                early_ref[spot, place, :, where] = part
-
-            store_chunks(dot32(left[...], right[:, columns]), column, put)
+    for place, (left, right) in enumerate(((n2_tall, dgate), (n2_tall, dup), (c_tall, hid))):
+        for side in range(COL_CUT):
+            start = (side ^ (info[0] % COL_CUT)) * CHUNK_COLS
+            for column in range(0, CHUNK_COLS, block):
+                columns = pl.ds(pl.multiple_of(start + column, block), block)
+                held[...] = dot32(left[...], right[:, columns])
+                for index, part in row_parts(held, info[0], side):
+                    out = (keep_ref, send_ref)[index // 4]
+                    out[index % 4, place, :, column : column + block] = part
     gwo_ref[...] = (
         dot32(o0_ref[...], dh_low[:TOK, :]) + dot32(o1_ref[...], dh_low[TOK:, :])
     ).astype(jnp.bfloat16)
 
 
-def mlp(tokens, cotangent, mixed, w_out, w_gate, w_up, w_down, gain):
+def mlp(info, tokens, cotangent, mixed, w_out, w_gate, w_up, w_down, gain):
     rows = tokens.shape[0] * TOK
     low = jnp.bfloat16
     return pl.pallas_call(
@@ -395,12 +391,13 @@
             jax.ShapeDtypeStruct(tokens.shape, jnp.float32),
             jax.ShapeDtypeStruct((D, TOK), low),
             jax.ShapeDtypeStruct((D, TOK), low),
-            jax.ShapeDtypeStruct((CHUNKS, 3, CHUNK_ROWS, CHUNK_COLS), low),
+            jax.ShapeDtypeStruct((CHUNKS // 2, 3, CHUNK_ROWS, CHUNK_COLS), low),
+            jax.ShapeDtypeStruct((CHUNKS // 2, 3, CHUNK_ROWS, CHUNK_COLS), low),
             jax.ShapeDtypeStruct((D, D), low),
             jax.ShapeDtypeStruct((1, D), jnp.float32),
         ),
-        in_specs=[vmem()] * 9,
-        out_specs=(vmem(),) * 7,
+        in_specs=[smem()] + [vmem()] * 9,
+        out_specs=(vmem(),) * 8,
         scratch_shapes=[
             pltpu.VMEM((rows, FF), low),
             pltpu.VMEM((rows, FF), low),
@@ -408,63 +405,202 @@
             pltpu.VMEM((D, rows), low),
             pltpu.VMEM((D, rows), low),
             pltpu.VMEM((rows, D), low),
+            pltpu.VMEM((D, 256), jnp.float32),
         ],
         compiler_params=kernel_params,
         cost_estimate=pl.CostEstimate(
             flops=6 * rows * 3 * D * FF, bytes_accessed=25000000, transcendentals=rows * FF
         ),
         name="mlp",
-    )(tokens, cotangent, mixed[0], mixed[1], w_out, w_gate, w_up, w_down, gain)
+    )(info, tokens, cotangent, mixed[0], mixed[1], w_out, w_gate, w_up, w_down, gain)
+
+
+def natural_tiles(flat, base, rows, width):
+    pairs, step, whole = rows // 2, width * 2 // 128, width // 128
+    parts = [flat[pl.ds(base + place, pairs, stride=step), :] for place in range(step)]
+    even = parts[:whole] + [parts[whole][:, :HEAD_DIM]]
+    odd = jnp.concatenate([parts[whole][:, HEAD_DIM:]] + parts[whole + 1 :], axis=1)
+    return even, [odd[:, low : low + 128] for low in range(0, width, 128)]
+
+
+def unflatten(flat, base, rows, width, tiles):
+    even, odd = natural_tiles(flat, base, rows, width)
+    for place, (first, second) in enumerate(zip(even, odd)):
+        breadth = first.shape[1]
+        if breadth < 128:
+            blank = jnp.zeros((rows // 2, 128 - breadth), jnp.float32)
+            first = jnp.concatenate([first, blank], axis=1)
+            second = jnp.concatenate([second, blank], axis=1)
+        tiles[place, pl.ds(0, rows // 2, stride=2), :] = first
+        tiles[place, pl.ds(1, rows // 2, stride=2), :] = second
+
+
+def tile_widths(width):
+    return [(place, low, min(128, width - low)) for place, low in enumerate(range(0, width, 128))]
+
+
+MIXED = ((0, 0, D), (2592, D, KV_WIDTH), (3456, D + KV_WIDTH, KV_WIDTH), (4320, FF - D, D))
+
+
+def project_kernel(
+    info, pieces_ref, x_ref, gain_ref, cos0_ref, sin0_ref, cos1_ref, sin1_ref,
+    q0_ref, q1_ref, kv_ref, w_ref, wo_ref, n_ref, flat, tiles,
+):
+    spot = info[0]
+    length = flat.shape[0] // CHUNKS
+    for place in range(CHUNKS):
+        half, chip, core = place // 4, place // 2 % 2, place % 2
+        chunk = core * 4 + half * 2 + chip
+        flat[place * length : (place + 1) * length, :] = pieces_ref[chunk ^ spot].astype(
+            jnp.float32
+        )
+    for base, start, width in MIXED:
+        unflatten(flat, base, D, width, tiles)
+        for place, low, breadth in tile_widths(width):
+            part = tiles[place][:D, :breadth].astype(jnp.bfloat16)
+            if start < FF - D:
+                w_ref[:, start + low : start + low + breadth] = part
+            else:
+                wo_ref[:, low : low + breadth] = part
+    tall = w_ref[...].T
+    half_width = HEAD_DIM // 2
+    tables = ((q0_ref, cos0_ref, sin0_ref), (q1_ref, cos1_ref, sin1_ref))
+    for micro, (q_ref, cos_ref, sin_ref) in enumerate(tables):
+        values = x_ref[micro].astype(jnp.float32)
+        scaling = lax.rsqrt(jnp.mean(values * values, axis=-1, keepdims=True) + norm_epsilon)
+        normed = (values * scaling * gain_ref[...]).astype(jnp.bfloat16)
+        n_ref[micro * TOK : (micro + 1) * TOK, :] = normed
+        linear = dot_with(tall, normed, 1, 1)
+        cosine, sine = cos_ref[...], sin_ref[...]
+        for head in range(HEADS + KV_HEADS):
+            low = head * HEAD_DIM
+            former = linear[low : low + half_width]
+            latter = linear[low + half_width : low + HEAD_DIM]
+            turned = jnp.concatenate(
+                [former * cosine - latter * sine, latter * cosine + former * sine], axis=0
+            ).astype(jnp.bfloat16)
+            if head < HEADS:
+                scaled = turned.astype(jnp.float32) * 0.125
+                q_ref[head // GROUPS, head % GROUPS] = scaled.astype(jnp.bfloat16)
+            else:
+                low = low - D
+                kv_ref[micro, low : low + HEAD_DIM, :] = turned
+        kv_ref[micro, KV_WIDTH:, :] = linear[D + KV_WIDTH :].astype(jnp.bfloat16)
+
+
+def project(info, pieces, tokens, gain, tables):
+    low = jnp.bfloat16
+    return pl.pallas_call(
+        project_kernel,
+        out_shape=(
+            jax.ShapeDtypeStruct(heads_shape, low),
+            jax.ShapeDtypeStruct(heads_shape, low),
+            jax.ShapeDtypeStruct((2, 2 * KV_WIDTH, TOK), low),
+            jax.ShapeDtypeStruct((D, D + 2 * KV_WIDTH), low),
+            jax.ShapeDtypeStruct((D, D), low),
+            jax.ShapeDtypeStruct((2 * TOK, D), low),
+        ),
+        in_specs=[smem()] + [vmem()] * 7,
+        out_specs=(vmem(),) * 6,
+        scratch_shapes=[
+            pltpu.VMEM((D * FF // 128, 128), jnp.float32),
+            pltpu.VMEM((5, D, 128), jnp.float32),
+        ],
+        compiler_params=kernel_params,
+        cost_estimate=pl.CostEstimate(
+            flops=4 * TOK * D * 960, bytes_accessed=8000000, transcendentals=0
+        ),
+        name="project",
+    )(info, pieces, tokens, gain, *tables[0], *tables[1])
 
 
 def projection_kernel(
-    n_ref, dq0_ref, dq1_ref, dkv0_ref, dkv1_ref, cos0_ref, sin0_ref, cos1_ref, sin1_ref, gwo_ref,
-    late_ref, all_ref, held,
+    info, n_ref, dq0_ref, dq1_ref, kept0_ref, kept1_ref, got_ref, far_ref,
+    cos0_ref, sin0_ref, cos1_ref, sin1_ref, gwo_ref, tie_ref,
+    keep_ref, send_ref, all_ref, held, cut,
 ):
+    spot, chip = info[0], info[1]
     half_width = HEAD_DIM // 2
-    parts = ((dq0_ref, dkv0_ref, cos0_ref, sin0_ref), (dq1_ref, dkv1_ref, cos1_ref, sin1_ref))
-    for micro, (dq_ref, dkv_ref, cos_ref, sin_ref) in enumerate(parts):
+    parts = ((dq0_ref, kept0_ref, cos0_ref, sin0_ref), (dq1_ref, kept1_ref, cos1_ref, sin1_ref))
+    for micro, (dq_ref, kept_ref, cos_ref, sin_ref) in enumerate(parts):
         columns = slice(micro * TOK, (micro + 1) * TOK)
         all_ref[:D, columns] = dq_ref[...]
         cosine, sine = cos_ref[...], sin_ref[...]
+        summed = kept_ref[0].astype(jnp.float32) + got_ref[2 * micro].astype(jnp.float32)
+        summed = summed + jnp.where(chip == micro, far_ref[...].astype(jnp.float32), 0.0)
         for head in range(KV_HEADS):
             low = head * HEAD_DIM
-            former = dkv_ref[low : low + half_width, :].astype(jnp.float32)
-            latter = dkv_ref[low + half_width : low + HEAD_DIM, :].astype(jnp.float32)
+            former = summed[low : low + half_width, :]
+            latter = summed[low + half_width : low + HEAD_DIM, :]
             all_ref[D + low : D + low + half_width, columns] = (
                 former * cosine + latter * sine
             ).astype(jnp.bfloat16)
             all_ref[D + low + half_width : D + low + HEAD_DIM, columns] = (
                 latter * cosine - former * sine
             ).astype(jnp.bfloat16)
-        all_ref[D + KV_WIDTH :, columns] = dkv_ref[KV_WIDTH:, :]
+        all_ref[D + KV_WIDTH :, columns] = summed[KV_WIDTH:, :].astype(jnp.bfloat16)
     held[:, : D + 2 * KV_WIDTH] = dot_with(n_ref[...].T, all_ref[...], 1, 1)
     held[:, D + 2 * KV_WIDTH :] = gwo_ref[...].astype(jnp.float32)
-
-    def put(spot, where, part):
-        late_ref[spot, :, where] = part
-
-    for column in range(0, FF, CHUNK_COLS):
-        store_chunks(held[:, column : column + CHUNK_COLS], column, put)
-
-
-def projection_grads(normed, dqs, dkvs, tables, gwo):
+    for side in range(COL_CUT):
+        start = (side ^ (spot % COL_CUT)) * CHUNK_COLS
+        cut[...] = held[:, pl.ds(pl.multiple_of(start, CHUNK_COLS), CHUNK_COLS)]
+        for index, part in row_parts(cut, spot, side):
+            (keep_ref, send_ref)[index // 4][index % 4] = part
+
+
+def projection_grads(info, normed, dqs, kept, got, far, tables, gwo, tie):
     rows = normed.shape[0]
+    chunk_shape = (CHUNKS // 2, CHUNK_ROWS, CHUNK_COLS)
     return pl.pallas_call(
         projection_kernel,
         out_shape=(
-            jax.ShapeDtypeStruct((CHUNKS, CHUNK_ROWS, CHUNK_COLS), jnp.bfloat16),
+            jax.ShapeDtypeStruct(chunk_shape, jnp.bfloat16),
+            jax.ShapeDtypeStruct(chunk_shape, jnp.bfloat16),
             jax.ShapeDtypeStruct((D + 2 * KV_WIDTH, rows), jnp.bfloat16),
         ),
-        in_specs=[vmem()] * 10,
-        out_specs=(vmem(),) * 2,
-        scratch_shapes=[pltpu.VMEM((D, FF), jnp.float32)],
+        in_specs=[smem()] + [vmem()] * 12 + [anywhere()],
+        out_specs=(vmem(),) * 3,
+        scratch_shapes=[
+            pltpu.VMEM((D, FF), jnp.float32),
+            pltpu.VMEM((D, CHUNK_COLS), jnp.float32),
+        ],
         compiler_params=kernel_params,
         cost_estimate=pl.CostEstimate(
             flops=2 * rows * D * 960, bytes_accessed=8000000, transcendentals=0
         ),
         name="projection_grads",
-    )(normed, *dqs, *dkvs, *tables[0], *tables[1], gwo)
+    )(info, normed, *dqs, *kept, got, far, *tables[0], *tables[1], gwo, tie)
+
+
+def add_kernel(left_ref, right_ref, tie_ref, out_ref):
+    total = left_ref[...].astype(jnp.float32) + right_ref[...].astype(jnp.float32)
+    out_ref[...] = total.astype(out_ref.dtype)
+
+
+def tied_add(left, right, tie):
+    return pl.pallas_call(
+        add_kernel,
+        out_shape=jax.ShapeDtypeStruct(left.shape, left.dtype),
+        in_specs=[vmem(), vmem(), anywhere()],
+        out_specs=vmem(),
+        compiler_params=kernel_params,
+        name="tied_add",
+    )(left, right, tie)
+
+
+def cast_kernel(value_ref, tie_ref, out_ref):
+    out_ref[...] = value_ref[...].astype(out_ref.dtype)
+
+
+def tied_cast(value, tie):
+    return pl.pallas_call(
+        cast_kernel,
+        out_shape=jax.ShapeDtypeStruct(value.shape, jnp.bfloat16),
+        in_specs=[vmem(), anywhere()],
+        out_specs=vmem(),
+        compiler_params=kernel_params,
+        name="tied_cast",
+    )(value, tie)
 
 
 def inputs_kernel(all_ref, w_ref, x_ref, dh_ref, gain_ref, out0_ref, out1_ref, gg_ref):
@@ -512,73 +648,126 @@
     return lax.fori_loop(0, NS_STEPS, iterate, current) * (0.2 * math.sqrt(scale))
 
 
-def newton_kernel(info, pieces_ref, old_ref, grad_ref, out_ref, total):
-    spot, kind = info[0], info[1]
+def flatten_rows(tiles, start, rows, width, out):
+    pairs, step, whole = rows // 2, width * 2 // 128, width // 128
+    spans = range(whole + 1)
+    even = [tiles[place, pl.ds(start, pairs, stride=2), :] for place in spans]
+    odd = [tiles[place, pl.ds(start + 1, pairs, stride=2), :] for place in spans]
+    for place in range(whole):
+        out[pl.ds(place, pairs, stride=step), :] = even[place]
+    rest = width - whole * 128
+    joined = jnp.concatenate([even[whole][:, :rest]] + odd[:whole] + [odd[whole][:, :rest]], axis=1)
+    for place in range(whole, step):
+        low = (place - whole) * 128
+        out[pl.ds(place, pairs, stride=step), :] = joined[:, low : low + 128]
+
+
+def shard_rows(kind, start, matrix, tiles, out):
+    length = out.shape[0] * 128
+
+    @pl.when(kind == 0)
+    def _():
+        rows = length // FF
+        for place in range(FF // 128):
+            out[pl.ds(place, rows, stride=FF // 128), :] = matrix[
+                pl.ds(pl.multiple_of(start, 8), rows), place * 128 : (place + 1) * 128
+            ]
+
+    @pl.when(kind == 5)
+    def _():
+        for place, low, breadth in tile_widths(D):
+            tiles[place, :, :breadth] = matrix[low : low + breadth, :].T
+        flatten_rows(tiles, start, length // D, D, out)
+
+    for place, (base, low, width) in zip((1, 3, 4, 2), MIXED):
+
+        @pl.when(kind == place)
+        def _():
+            for tile, column, breadth in tile_widths(width):
+                tiles[tile, :D, :breadth] = matrix[:, low + column : low + column + breadth]
+            flatten_rows(tiles, start, length // width, width, out)
+
+
+def newton_kernel(local, info, pieces_ref, old_ref, *refs):
+    spot, kind, start = info[0], info[1], info[2]
+    grad, total, tiles = refs[-3:]
     for chunk in range(CHUNKS):
         row, column = chunk // COL_CUT * CHUNK_ROWS, chunk % COL_CUT * CHUNK_COLS
         rows, columns = slice(row, row + CHUNK_ROWS), slice(column, column + CHUNK_COLS)
-        part = pieces_ref[chunk ^ spot]
-        grad_ref[rows, columns] = part
-        total[rows, columns] = momentum_decay * old_ref[rows, columns].astype(
-            jnp.float32
-        ) + part.astype(jnp.float32)
-
-    @pl.when(kind == 0)
-    def _():
-        out_ref[...] = newton_loop(total[...], FF)
-
-    for place, low in ((1, 0), (2, FF - D)):
-
-        @pl.when(kind == place)
+        grad[rows, columns] = pieces_ref[chunk ^ spot].astype(jnp.float32)
+
+    def newton_body(flat):
+        flat[...] = old_ref[...].astype(jnp.float32) * momentum_decay
+
+        @pl.when(kind == 0)
         def _():
-            out_ref[:, low : low + D] = newton_loop(total[:, low : low + D], D)
-
-    for place, low in ((3, D), (4, D + KV_WIDTH)):
-
-        @pl.when(kind == place)
+            for place in range(FF // 128):
+                columns = slice(place * 128, (place + 1) * 128)
+                total[:, columns] = flat[pl.ds(place, D, stride=FF // 128), :] + grad[:, columns]
+
+        @pl.when(kind == 5)
         def _():
-            out_ref[:, low : low + KV_WIDTH] = newton_loop(total[:, low : low + KV_WIDTH].T, D).T
-
-
-def newton(info, pieces, old):
+            unflatten(flat, 0, FF, D, tiles)
+            for place, low, breadth in tile_widths(D):
+                rows = slice(low, low + breadth)
+                total[rows, :] = tiles[place].T[:breadth] + grad[rows, :]
+
+        @pl.when((kind == 0) | (kind == 5))
+        def _():
+            total[...] = newton_loop(total[...], FF)
+
+        for place, (base, low, width) in zip((1, 3, 4, 2), MIXED):
+
+            @pl.when(kind == place)
+            def _():
+                unflatten(flat, base, D, width, tiles)
+                part = jnp.concatenate(
+                    [tiles[tile][:D, :breadth] for tile, _, breadth in tile_widths(width)], axis=1
+                )
+                columns = slice(low, low + width)
+                part = part + grad[:, columns]
+                if width == D:
+                    total[:, columns] = newton_loop(part, D)
+                else:
+                    total[:, columns] = newton_loop(part.T, D).T
+
+    pl.run_scoped(newton_body, pltpu.VMEM((D * FF // 128, 128), jnp.float32))
+    if local:
+        weights_ref, momentum_ref, grad_ref, new_momentum_ref, new_weights_ref = refs[:5]
+        shard_rows(kind, start, grad, tiles, grad_ref)
+        shard_rows(kind, start, total, tiles, new_weights_ref)
+        new_momentum_ref[...] = momentum_decay * momentum_ref[...] + grad_ref[...]
+        new_weights_ref[...] = (
+            weights_ref[...] * (1.0 - matrix_rate * weight_decay)
+            - matrix_rate * new_weights_ref[...]
+        )
+    else:
+        refs[0][...] = grad[...]
+        refs[1][...] = total[...]
+
+
+def newton(info, pieces, old, *shards):
+    local = len(shards) > 0
+    if local:
+        outs = (jax.ShapeDtypeStruct(shards[0].shape, jnp.float32),) * 3
+    else:
+        outs = (jax.ShapeDtypeStruct((D, FF), jnp.float32),) * 2
     return pl.pallas_call(
-        newton_kernel,
-        out_shape=(
-            jax.ShapeDtypeStruct((D, FF), jnp.bfloat16),
-            jax.ShapeDtypeStruct((D, FF), jnp.float32),
-        ),
-        in_specs=[smem(), vmem(), vmem()],
-        out_specs=(vmem(),) * 2,
-        scratch_shapes=[pltpu.VMEM((D, FF), jnp.float32)],
+        partial(newton_kernel, local),
+        out_shape=outs,
+        in_specs=[smem()] + [vmem()] * (2 + len(shards)),
+        out_specs=(vmem(),) * len(outs),
+        scratch_shapes=[
+            pltpu.VMEM((D, FF), jnp.float32),
+            pltpu.VMEM((D, FF), jnp.float32),
+            pltpu.VMEM((5, FF, 128), jnp.float32),
+        ],
         compiler_params=kernel_params,
         cost_estimate=pl.CostEstimate(
             flops=12000000000, bytes_accessed=9000000, transcendentals=0
         ),
         name="newton",
-    )(info, pieces, old)
-
-
-def quarter_matrix(quarter, flat):
-    def mixed_case(flat):
-        square = D * D
-        narrow = D * KV_WIDTH
-        return jnp.concatenate(
-            [
-                flat[:square].reshape(D, D),
-                flat[square : square + narrow].reshape(D, KV_WIDTH),
-                flat[square + narrow : square + 2 * narrow].reshape(D, KV_WIDTH),
-                flat[square + 2 * narrow :].reshape(D, D),
-            ],
-            axis=1,
-        )
-
-    def wide_case(flat):
-        return flat.reshape(D, FF)
-
-    def tall_case(flat):
-        return flat.reshape(FF, D).T
-
-    return lax.switch(quarter, [mixed_case, wide_case, wide_case, tall_case], flat)
+    )(info, pieces, old, *shards)
 
 
 def own_kind(quarter, within):
@@ -589,10 +778,10 @@
     mixed = jnp.array([1, 3, 4, 2], jnp.int32)[passed]
     starts = jnp.array([0, square, square + narrow, square + 2 * narrow], jnp.int32)
     inside = within - jnp.where(quarter == 0, starts[passed], 0)
-    return (jnp.where(quarter == 0, mixed, 0), inside)
-
-
-def own_rows(quarter, kind, inside, shard_length, gradient, update):
+    return (jnp.where(quarter == 0, mixed, jnp.where(quarter == 3, 5, 0)), inside)
+
+
+def own_rows(kind, inside, shard_length, gradient, update):
     def block_case(low, width):
         def run(gradient, update):
             start = (inside // width, low)
@@ -618,7 +807,7 @@
         block_case(D + KV_WIDTH, KV_WIDTH),
         tall_case,
     ]
-    return lax.switch(jnp.where(quarter == 3, 5, kind), cases, gradient, update)
+    return lax.switch(kind, cases, gradient, update)
 
 
 CORE_SWAP = [(0, 1), (1, 0), (2, 3), (3, 2)]
@@ -627,29 +816,19 @@
 END_SWAP = [(0, 3), (3, 0), (1, 2), (2, 1)]
 
 
-def plane_steps():
-    ctx = lax.axis_index("ctx")
-    return (
-        ("ctx", CORE_SWAP, lax.rem(ctx, 2)),
-        ("ctx", CHIP_SWAP, ctx // 2),
-        ("half", SIDE_SWAP, lax.axis_index("half")),
-    )
-
-
-def plane_sum(chunks):
-    for axis, swap, bit in plane_steps():
-        halves = chunks.reshape(2, chunks.shape[0] // 2, *chunks.shape[1:])
-        sent = lax.dynamic_index_in_dim(halves, 1 - bit, 0, keepdims=False)
-        kept = lax.dynamic_index_in_dim(halves, bit, 0, keepdims=False)
-        got = lax.ppermute(sent, axis, swap)
-        chunks = (kept.astype(jnp.float32) + got.astype(jnp.float32)).astype(jnp.bfloat16)
-    return chunks[0]
+def plane_swap(value, bit):
+    axis, swap = (("ctx", CHIP_SWAP), ("half", SIDE_SWAP), ("ctx", CORE_SWAP))[bit]
+    return lax.ppermute(value, axis, swap)
+
+
+def low_sum(left, right):
+    return (left.astype(jnp.float32) + right.astype(jnp.float32)).astype(jnp.bfloat16)
 
 
 def plane_gather(piece):
     pieces = piece[None]
-    for axis, swap, bit in reversed(plane_steps()):
-        pieces = jnp.concatenate([pieces, lax.ppermute(pieces, axis, swap)], axis=0)
+    for bit in range(3):
+        pieces = jnp.concatenate([pieces, plane_swap(pieces, bit)], axis=0)
     return pieces
 
 
@@ -675,38 +854,47 @@
     return jnp.stack(fields).astype(jnp.int32)
 
 
+def gather_weights(low, spot):
+    rows = low.shape[0]
+    if lax.axis_size("rep") > 1:
+        full = lax.all_gather(low, EVERY, axis=0, tiled=True).reshape(4, D * FF)
+        order = [4 * (place // 2 % 2) + 2 * (place % 2) + place // 4 for place in range(CHUNKS)]
+        mixed = full[0].reshape(CHUNKS, -1, 128)
+        mixed = jnp.stack([mixed[place] for place in order])
+        return (mixed, jnp.zeros_like(spot)), [
+            full[1].reshape(D, FF),
+            full[2].reshape(D, FF),
+            full[3].reshape(FF, D),
+        ]
+    depth = lax.all_gather(low, "quarter", axis=0, tiled=False)
+    mixed = plane_gather(depth[0])
+    shapes = ((D // CHUNKS, FF), (D // CHUNKS, FF), (FF // CHUNKS, D))
+    rest = [
+        lax.all_gather(depth[place + 1].reshape(shape), PLANE, axis=0, tiled=True)
+        for place, shape in enumerate(shapes)
+    ]
+    return (mixed, spot), rest
+
+
 def per_device(tokens, lengths, weights, momentum, norm_gains, gain_first, gain_second, cotangent):
-    micro_count = tokens.shape[0]
     ctx = lax.axis_index("ctx")
+    core, chip = lax.rem(ctx, 2), ctx // 2
     quarter = lax.axis_index("quarter")
     reps = lax.axis_size("rep")
     shard_length = weights.shape[0]
+    flat_shape = (shard_length // 128, 128)
     within = lax.axis_index(("rep", "half", "ctx")) * shard_length
-    spot = lax.rem(ctx, 2) * 4 + ctx // 2 * 2 + lax.axis_index("half")
-
-    full_weights = lax.all_gather(weights.astype(jnp.bfloat16), EVERY, axis=0, tiled=True)
-    square, narrow, broad = D * D, D * KV_WIDTH, D * FF
-    places_in = [0, square, square + narrow, square + 2 * narrow]
-    w_qkv = jnp.concatenate(
-        [
-            full_weights[:square].reshape(D, D),
-            full_weights[places_in[1] : places_in[2]].reshape(D, KV_WIDTH),
-            full_weights[places_in[2] : places_in[3]].reshape(D, KV_WIDTH),
-        ],
-        axis=1,
-    )
-    w_out = full_weights[places_in[3] : places_in[3] + square].reshape(D, D)
-    w_gate = full_weights[broad : 2 * broad].reshape(D, FF)
-    w_up = full_weights[2 * broad : 3 * broad].reshape(D, FF)
-    w_down = full_weights[3 * broad :].reshape(FF, D)
-
+    spot = core * 4 + lax.axis_index("half") * 2 + chip
+    place_info = jnp.stack([spot, chip]).astype(jnp.int32)
+
+    (mixed_weights, mixed_spot), (w_gate, w_up, w_down) = gather_weights(
+        weights.reshape(flat_shape).astype(jnp.bfloat16), spot
+    )
     swapped = lax.ppermute(jnp.stack([tokens[1], cotangent[1]]), "ctx", END_SWAP)
     tokens_here = jnp.stack([tokens[0], swapped[0]])
     back = jnp.stack([cotangent[0], swapped[1]])
-    inputs = tokens_here.astype(jnp.float32).reshape(-1, D)
-    normed = normalize(inputs, norm_gains[0]).astype(jnp.bfloat16)
     infos, begin_rows, tables = [], [], []
-    for micro in range(micro_count):
+    for micro in range(2):
         block = ctx if micro == 0 else 3 - ctx
         own_places = block * TOK + jnp.arange(TOK, dtype=jnp.int32)
         offsets, begins = layout(lengths[micro, 0], own_places)
@@ -714,24 +902,35 @@
         begin_rows.append(begins.reshape(1, TOK))
         tables.append(rope_tables(offsets))
 
-    queries, keyvals, mixed, log_totals = [], [], [], []
-    for micro in range(micro_count):
-        rows = normed[micro * TOK : (micro + 1) * TOK]
-        linear = jnp.einsum("de,td->et", w_qkv, rows, preferred_element_type=jnp.float32)
-        turned = rotate_columns(linear[: D + KV_WIDTH], *tables[micro])
-        scaled = turned[:D].astype(jnp.bfloat16) * jnp.bfloat16(0.125)
-        queries.append(scaled.reshape(heads_shape))
-        own_keyvals = jnp.concatenate([turned[D:], linear[D + KV_WIDTH :]], axis=0)
-        keyvals.append(own_keyvals.astype(jnp.bfloat16))
-    gathered = lax.all_gather(jnp.stack(keyvals), "ctx", axis=1, tiled=False)
-    keyvals = [gathered[micro] for micro in range(micro_count)]
-    for micro in range(micro_count):
+    q0, q1, keyvals, w_qkv, w_out, normed = project(
+        mixed_spot.reshape(1).astype(jnp.int32), mixed_weights, tokens_here, norm_gains[0:1], tables
+    )
+    queries = (q0, q1)
+    far = lax.ppermute(
+        lax.dynamic_index_in_dim(keyvals, chip, 0, keepdims=False), "ctx", CHIP_SWAP
+    )
+    keyvals = (
+        keyvals,
+        lax.ppermute(keyvals, "ctx", CORE_SWAP),
+        far,
+        lax.ppermute(far, "ctx", CORE_SWAP),
+    )
+    mixed, log_totals = [], []
+    tie = norm_gains
+    for micro in range(2):
         mixed_one, log_total = attend_forward(
-            micro == 1, infos[micro], queries[micro], keyvals[micro], begin_rows[micro]
+            micro, infos[micro], queries[micro], keyvals, begin_rows[micro], tie
         )
         mixed.append(mixed_one)
         log_totals.append(log_total)
-    result, grad_state, grad_mixed_0, grad_mixed_1, early, grad_w_out, gain_two_grad = mlp(
+    old = lax.all_gather(
+        tied_cast(momentum.reshape(flat_shape), mixed[0]),
+        ("rep", "half", "ctx"),
+        axis=0,
+        tiled=True,
+    )
+    result, grad_state, grad_mixed_0, grad_mixed_1, keep, send, grad_w_out, gain_two_grad = mlp(
+        place_info,
         tokens_here,
         back,
         [part.reshape(D, TOK) for part in mixed],
@@ -743,57 +942,83 @@
     )
     returned = lax.ppermute(result[1].astype(jnp.bfloat16), "ctx", END_SWAP)
     result = jnp.stack([result[0], returned.astype(jnp.float32)])
-    early = plane_sum(early)
-    old = lax.all_gather(
-        momentum.astype(jnp.bfloat16), ("rep", "half", "ctx"), axis=0, tiled=True
-    )
-
-    grad_queries, grad_keyvals = [], []
-    for micro, grad_mixed in enumerate((grad_mixed_0, grad_mixed_1)):
-        dq, dkv = attend_back(
-            micro == 1,
+
+    def back_pass(micro, grad_mixed, tie):
+        return attend_back(
+            micro,
             infos[micro],
             queries[micro],
-            keyvals[micro],
+            keyvals,
             begin_rows[micro],
             mixed[micro],
             log_totals[micro],
             grad_mixed.reshape(heads_shape),
             *tables[micro],
+            tie,
         )
-        for step, (swap, bit) in enumerate(((CORE_SWAP, lax.rem(ctx, 2)), (CHIP_SWAP, ctx // 2))):
-            shaped = dkv.reshape(2, 2, 2 * KV_WIDTH, TOK) if step == 0 else dkv
-            axis = 1 if step == 0 else 0
-            sent = lax.dynamic_index_in_dim(shaped, 1 - bit, axis, keepdims=False)
-            kept = lax.dynamic_index_in_dim(shaped, bit, axis, keepdims=False)
-            got = lax.ppermute(sent, "ctx", swap)
-            dkv = (kept.astype(jnp.float32) + got.astype(jnp.float32)).astype(jnp.bfloat16)
-        grad_queries.append(dq.reshape(D, TOK))
-        grad_keyvals.append(dkv)
-    late, grad_qkv = projection_grads(normed, grad_queries, grad_keyvals, tables, grad_w_out)
-    late = plane_sum(late)
+
+    got = plane_swap(send, 2)
+    dq0, kept0, sent0 = back_pass(0, grad_mixed_0, old)
+    early = low_sum(keep, got)
+    got = plane_swap(early[2:], 1)
+    dq1, kept1, sent1 = back_pass(1, grad_mixed_1, early)
+    traded = lax.ppermute(jnp.concatenate([sent0, sent1], axis=0), "ctx", CORE_SWAP)
+    heavy = chip == 0
+    crossing = low_sum(
+        jnp.where(heavy, kept1[1], kept0[1]), jnp.where(heavy, traded[3], traded[1])
+    )
+    crossed = lax.ppermute(crossing, "ctx", CHIP_SWAP)
+    early = low_sum(early[:2], got)
+    late_keep, late_send, grad_qkv = projection_grads(
+        place_info,
+        normed,
+        (dq0.reshape(D, TOK), dq1.reshape(D, TOK)),
+        (kept0, kept1),
+        traded,
+        crossed,
+        tables,
+        grad_w_out,
+        early,
+    )
+    early = low_sum(early[0], plane_swap(early[1], 0))
+    late = low_sum(late_keep, plane_swap(late_send, 2))
+    late = low_sum(late[:2], plane_swap(late[2:], 1))
     grad_inputs_0, grad_inputs_1, gain_one_grad = input_grads(
         grad_qkv, w_qkv, tokens_here, grad_state, norm_gains[0:1]
     )
+    late = tied_add(late[0], plane_swap(late[1], 0), gain_one_grad)
     returned = lax.ppermute(grad_inputs_1, "ctx", END_SWAP)
     grad_inputs = jnp.stack([grad_inputs_0, returned.astype(jnp.float32)])
-    gain_parts = lax.all_gather(
-        jnp.concatenate([gain_one_grad, gain_two_grad], axis=0), EVERY, axis=0, tiled=False
-    )
-    gain_grad = jnp.sum(gain_parts, axis=0)
+    gain_grad = jnp.concatenate([gain_one_grad, gain_two_grad], axis=0)
+    for bit in range(3):
+        gain_grad = gain_grad + plane_swap(gain_grad, bit)
+    gain_grad = gain_grad + sum(
+        lax.ppermute(gain_grad, "quarter", [(place, (place + shift) % 4) for place in range(4)])
+        for shift in range(1, 4)
+    )
 
     piece = depth_sum(late, early)
     if reps > 1:
         piece = lax.psum(piece, "rep")
+        gain_grad = lax.psum(gain_grad, "rep")
     pieces = plane_gather(piece)
     kind, inside = own_kind(quarter, within)
-    gradient, update = newton(
-        jnp.stack([spot, kind]).astype(jnp.int32), pieces, quarter_matrix(quarter, old)
-    )
-    grad_shard, update_shard = own_rows(quarter, kind, inside, shard_length, gradient, update)
-    grad_shard = grad_shard.astype(jnp.float32)
-    new_momentum = momentum_decay * momentum + grad_shard
-    new_weights = weights * (1.0 - matrix_rate * weight_decay) - matrix_rate * update_shard
+    if flat_shape[0] % 8 == 0:
+        width = jnp.array([FF, D, D, KV_WIDTH, KV_WIDTH, D], jnp.int32)[kind]
+        grad_shard, new_momentum, new_weights = newton(
+            jnp.stack([spot, kind, inside // width]).astype(jnp.int32),
+            pieces,
+            old,
+            weights.reshape(flat_shape),
+            momentum.reshape(flat_shape),
+        )
+    else:
+        gradient, update = newton(
+            jnp.stack([spot, kind, kind]).astype(jnp.int32), pieces, old
+        )
+        grad_shard, update_shard = own_rows(kind, inside, shard_length, gradient, update)
+        new_momentum = momentum_decay * momentum + grad_shard
+        new_weights = weights * (1.0 - matrix_rate * weight_decay) - matrix_rate * update_shard
 
     first_new = first_decay * gain_first + (1.0 - first_decay) * gain_grad
     second_new = second_decay * gain_second + (1.0 - second_decay) * gain_grad * gain_grad
@@ -805,9 +1030,9 @@
     return (
         result,
         grad_inputs,
-        grad_shard,
-        new_momentum,
-        new_weights,
+        grad_shard.reshape(weights.shape),
+        new_momentum.reshape(weights.shape),
+        new_weights.reshape(weights.shape),
         first_new,
         second_new,
         new_gains,

time: 510 us -> 432 us (0.85)
  the two profiles are of different devices: /device:TPU:31 before, /device:TPU:8 now
where the time goes in v3:
time: 432 us; the launch traced here: 425 us
  Pallas kernels  154 us (36%)
  waiting for transfers between devices  109 us (25%)
  starting transfers between devices  51.7 us (12%)
  local copies, waits for them, and re-layouts  31.3 us (7%)
  between operations  30.4 us (7%)
  other arithmetic  29.5 us (7%)
  blocking collectives  19 us (4%)
    ppermute x15, waiting for transfers between devices, plane_swap(): return lax.ppermute(value, axis, swap)  53.6 us
    pallas_call x1, Pallas kernels, mlp(): pl.pallas_call(mlp_kernel, out_shape=(jax.ShapeDtypeStruct(tokens.shape,...  37 us
    pallas_call x2, Pallas kernels, attend_back(): pl.pallas_call(partial(backward_kernel, micro), out_shape=(jax.ShapeDtype...  36.1 us
    ppermute x15, starting transfers between devices, plane_swap(): return lax.ppermute(value, axis, swap)  28.7 us
    pallas_call x1, Pallas kernels, newton(): pl.pallas_call(partial(newton_kernel, local), out_shape=outs, in_specs=[s...  28.6 us
    pallas_call x2, Pallas kernels, attend_forward(): pl.pallas_call(partial(forward_kernel, micro), out_shape=(jax.ShapeDtypeS...  27.1 us
    all_gather x1, blocking collectives, gather_weights(): depth = lax.all_gather(low, 'quarter', axis=0, tiled=False)  19 us
    ppermute x3, waiting for transfers between devices, depth_sum(): lax.ppermute(sent, 'quarter', [(place, (place + shift) % 4) for place in...  17.1 us
  transfers between devices with their start and end apart: 33, of which 15 were waited for; matrix products, arithmetic and copies ran while one was open for 10% of the time, Pallas kernels for 21%

profile of v3, /device:TPU:8, one launch (start us, length us, event | category | flops | bytes accessed | tf_op | source)
XLA Modules:
  0.0 424.9 jit_solution(16782729740279581988)
XLA Ops:
  7.2 1.0 convert_bitcast_fusion
  8.3 19.0 %all_gather.16 = bf16[4,864,128]{2,1,0:T(8,128)(2,1)S(1)} all-gather(bf16[1,864,128]{2,1,0:T(8,128)(2,1)S(1)} %convert_bitcast_fusion), channel_id=1, replica_groups=mesh['quarter'=4,'rep'=1,'half'=2,'ctx'=4] {'quarter'}, dimensions={0}, use_global_device_ids=true | all-gather | bytes 1105920 | tf_op jit(solution)/shard_map/all_gather | solution.py:869
  30.0 1.6 collective-permute-start.1
  31.6 1.4 fusion.18
  36.1 1.6 collective-permute-start.2
  37.7 12.6 %collective-permute-done.2 = bf16[2,864,128]{2,1,0:T(8,128)(2,1)S(1)} collective-permute-done((bf16[2,864,128]{2,1,0:T(8,128)(2,1)S(1)}, bf16[2,864,128]{2,1,0:T(8,128)(2,1)S(1)}, u32[]{:S(2)}, u32[]{:S(2)}) %collective-permute-start.2) | collective-permute-done | bytes 442400 | tf_op jit(solution)/shard_map/ppermute | solution.py:821
  50.3 1.1 pad_maximum_fusion.8
  52.3 1.2 multiply_sine_fusion
  53.5 15.8 %collective-permute-done = bf16[2,512,576]{1,2,0:T(8,128)(2,1)} collective-permute-done((bf16[2,512,576]{1,2,0:T(8,128)(2,1)S(1)}, bf16[2,512,576]{1,2,0:T(8,128)(2,1)}, u32[]{:S(2)}, u32[]{:S(2)}) %collective-permute-start) | collective-permute-done | bytes 1179680 | tf_op jit(solution)/shard_map/ppermute | solution.py:893
  69.3 1.3 fusion.19
  71.0 1.3 pad_maximum_fusion.5.x_ref
  72.2 2.5 pad_maximum_fusion.2.pieces_ref
  74.8 8.0 %project.1 = (bf16[3,3,64,512]{3,2,1,0:T(8,128)(2,1)}, bf16[3,3,64,512]{3,2,1,0:T(8,128)(2,1)}, bf16[2,384,512]{2,1,0:T(8,128)(2,1)}, bf16[576,960]{1,0:T(8,128)...) custom-call(s32[1]{0:T(128)} %bitcast.info, bf16[8,864,128]{2,1,0:T(8,128)(2,1)} %pad_maximum_fusion.2.pieces_ref, ...), custom_call_target="tpu_custom_call" | custom-call | flops 1132462080 | bytes 8000000 | tf_op jit(solution)/shard_map/project/pallas_call | solution.py:493
  84.9 14.6 %collective-permute-done.5.far_ref = bf16[384,512]{1,0:T(8,128)(2,1)} collective-permute-done((bf16[384,512]{1,0:T(8,128)(2,1)S(1)}, bf16[384,512]{1,0:T(8,128)(2,1)}, u32[]{:S(2)}, u32[]{:S(2)}) %collective-permute-start.5) | collective-permute-done | bytes 393248 | tf_op jit(solution)/shard_map/ppermute | solution.py:909
  116.0 1.3 pad_maximum_fusion.6.c_ref
  118.2 8.6 %attend_forward.2 = (bf16[3,3,64,512]{3,2,1,0:T(8,128)(2,1)}, f32[3,3,1,512]{3,2,1,0:T(1,128)}) custom-call(s32[7]{0:T(128)} %stack.110.info, bf16[3,3,64,512]{3,2,1,0:T(8,128)(2,1)} %get-tuple-element.41.q_ref, bf16[2,384,512]{2,1,0:T(8,128)(2,1)} %get-tuple-element.42.kv_ref, bf16[2,384,512]{2,1,0:T(8,128)(2,1)} %copy-done.23, ...), custom_call_target="tpu_custom_call" | custom-call | flops 2415919104 | bytes 4000000 | tf_op jit(solution)/shard_map/attend_forward/pallas_call | solution.py:261
  126.8 1.7 tied_cast.1
  128.5 18.5 %attend_forward.3 = (bf16[3,3,64,512]{3,2,1,0:T(8,128)(2,1)}, f32[3,3,1,512]{3,2,1,0:T(1,128)}) custom-call(s32[7]{0:T(128)} %stack.118.info, bf16[3,3,64,512]{3,2,1,0:T(8,128)(2,1)} %get-tuple-element.44.q_ref, bf16[2,384,512]{2,1,0:T(8,128)(2,1)} %get-tuple-element.42.kv_ref, bf16[2,384,512]{2,1,0:T(8,128)(2,1)} %copy-done.23, ...), custom_call_target="tpu_custom_call" | custom-call | flops 2415919104 | bytes 4000000 | tf_op jit(solution)/shard_map/attend_forward/pallas_call | solution.py:261
  147.0 37.0 %mlp.1 = (f32[2,512,576]{2,1,0:T(8,128)}, f32[2,512,576]{2,1,0:T(8,128)}, bf16[576,512]{1,0:T(8,128)(2,1)}, bf16[576,512]{1,0:T(8,128)(2,1)}, bf16[4,3,144,768]{...) custom-call(s32[2]{0:T(128)} %pad_add_fusion.info, ...), custom_call_target="tpu_custom_call" | custom-call | flops 16307453952 | bytes 25000000 | tf_op jit(solution)/shard_map/mlp/pallas_call | solution.py:387
  184.0 6.5 %collective-permute-start.8 = (bf16[4,3,144,768]{3,2,1,0:T(8,128)(2,1)}, bf16[4,3,144,768]{3,2,1,0:T(8,128)(2,1)S(1)}, u32[]{:S(2)}, u32[]{:S(2)}) collective-permute-start(bf16[4,3,144,768]{3,2,1,0:T(8,128)(2,1)} %get-tuple-element.55), channel_id=1, source_target_pairs={{0,1},{1,0},{2,3},{3,2},{4,5},{5,4},{6,7},{7,6},{8,9},{9,8},{10,11... | collective-permute-start | bytes 7962632 | tf_op jit(solution)/shard_map/ppermute | solution.py:821
  190.5 11.0 %attend_back.2 = (bf16[3,3,64,512]{3,2,1,0:T(8,128)(2,1)}, bf16[2,384,512]{2,1,0:T(8,128)(2,1)}, bf16[2,384,512]{2,1,0:T(8,128)(2,1)}) custom-call(s32[7]{0:T(128)} %stack.110.info, bf16[3,3,64,512]{3,2,1,0:T(8,128)(2,1)} %get-tuple-element.41.q_ref, bf16[2,384,512]{2,1,0:T(8,128)(2,1)} %get-tuple-element.42.kv_ref, bf16[2,384,512]{2,1,0:T(8,128)(2,1)} %copy-done.23, ...), custom_call_target="tpu_custom_call" | custom-call | flops 6039797760 | bytes 8000000 | tf_op jit(solution)/shard_map/attend_back/pallas_call | solution.py:285
  201.5 2.1 add_convert_fusion.tie_ref
  203.7 25.0 %attend_back.3 = (bf16[3,3,64,512]{3,2,1,0:T(8,128)(2,1)}, bf16[2,384,512]{2,1,0:T(8,128)(2,1)}, bf16[2,384,512]{2,1,0:T(8,128)(2,1)}) custom-call(s32[7]{0:T(128)} %stack.118.info, bf16[3,3,64,512]{3,2,1,0:T(8,128)(2,1)} %get-tuple-element.44.q_ref, bf16[2,384,512]{2,1,0:T(8,128)(2,1)} %get-tuple-element.42.kv_ref, bf16[2,384,512]{2,1,0:T(8,128)(2,1)} %copy-done.23, ...), custom_call_target="tpu_custom_call" | custom-call | flops 6039797760 | bytes 8000000 | tf_op jit(solution)/shard_map/attend_back/pallas_call | solution.py:285
  228.7 2.6 pad_maximum_fusion.4
  231.3 8.5 %collective-permute-start.9 = (bf16[4,384,512]{2,1,0:T(8,128)(2,1)}, bf16[4,384,512]{2,1,0:T(8,128)(2,1)}, u32[]{:S(2)}, u32[]{:S(2)}) collective-permute-start(bf16[4,384,512]{2,1,0:T(8,128)(2,1)} %pad_maximum_fusion.4), channel_id=1, source_target_pairs={{0,1},{1,0},{2,3},{3,2},{4,5},{5,4},{6,7},{7,6},{8,9},{9,8},{10,11... | collective-permute-start | bytes 4718600 | tf_op jit(solution)/shard_map/ppermute | solution.py:965
  239.8 1.1 slice.156
  241.0 1.5 collective-permute-start.11
  243.2 1.4 fusion.5
  244.7 5.6 %collective-permute-start.10 = (bf16[384,512]{1,0:T(8,128)(2,1)S(1)}, bf16[384,512]{1,0:T(8,128)(2,1)S(1)}, u32[]{:S(2)}, u32[]{:S(2)}) collective-permute-start(bf16[384,512]{1,0:T(8,128)(2,1)S(1)} %fusion.5), channel_id=1, source_target_pairs={{0,2},{2,0},{1,3},{3,1},{4,6},{6,4},{5,7},{7,5},{8,10},{10,8},{9,1... | collective-permute-start | bytes 1179656 | tf_op jit(solution)/shard_map/ppermute | solution.py:970
  250.3 22.1 %collective-permute-done.11 = bf16[2,3,144,768]{3,2,1,0:T(8,128)(2,1)} collective-permute-done((bf16[2,3,144,768]{3,2,1,0:T(8,128)(2,1)}, bf16[2,3,144,768]{3,2,1,0:T(8,128)(2,1)}, u32[]{:S(2)}, u32[]{:S(2)}) %collective-permute-start.11) | collective-permute-done | bytes 1327136 | tf_op jit(solution)/shard_map/ppermute | solution.py:821
  272.4 2.7 add_convert_fusion.1.tie_ref
  275.8 7.2 %projection_grads.1 = (bf16[4,144,768]{2,1,0:T(8,128)(2,1)}, bf16[4,144,768]{2,1,0:T(8,128)(2,1)}, bf16[960,1024]{1,0:T(8,128)(2,1)}) custom-call(s32[2]{0:T(128)} %pad_add_fusion.info, bf16[1024,576]{1,0:T(8,128)(2,1)} %get-tuple-element.48.n_ref, bf16[576,512]{1,0:T(8,128)(2,1)} %bitcast.97, bf16[576,512]{1,0:T(8,128)(2,1)} %bitcast.98, ...), custom_call_target="tpu_custom_call" | custom-call | flops 1132462080 | bytes 8000000 | tf_op jit(solution)/shard_map/projection_grads/pallas_call | solution.py:554
  283.0 2.6 collective-permute-done.13
  285.6 1.5 add_convert_fusion.2
  287.9 1.5 collective-permute-start.14
  289.5 5.7 %collective-permute-start.16 = (bf16[3,144,768]{2,1,0:T(8,128)(2,1)S(1)}, bf16[3,144,768]{2,1,0:T(8,128)(2,1)S(1)}, u32[]{:S(2)}, u32[]{:S(2)}) collective-permute-start(bf16[3,144,768]{2,1,0:T(8,128)(2,1)S(1)} %slice_bitcast_fusion), channel_id=1, source_target_pairs={{0,2},{2,0},{1,3},{3,1},{4,6},{6,4},{5,7},{7,5},{8,10},{10,8},{9,1... | collective-permute-start | bytes 1990664 | tf_op jit(solution)/shard_map/ppermute | solution.py:821
  295.1 6.3 %input_grads.1 = (f32[512,576]{1,0:T(8,128)}, bf16[512,576]{1,0:T(8,128)(2,1)}, f32[1,576]{1,0:T(1,128)}) custom-call(bf16[960,1024]{1,0:T(8,128)(2,1)} %get-tuple-element.62.all_ref, bf16[576,960]{1,0:T(8,128)(2,1)} %get-tuple-element.63.w_ref, bf16[2,512,576]{2,1,0:T(8,128)(2,1)} %pad_maximum_fusion.5.x_ref, f32[2,512,576]{2,1,0:T(8,128)} %get-tuple-element.64.dh_ref, ...), custom_call_target="tpu_custom_call" | custom-call | flops 1132462080 | bytes 8000000 | tf_op jit(solution)/shard_map/input_grads/pallas_call | solution.py:621
  301.5 1.1 add_convert_fusion.3
  303.3 4.5 %collective-permute-start.15 = (bf16[144,768]{1,0:T(8,128)(2,1)S(1)}, bf16[144,768]{1,0:T(8,128)(2,1)S(1)}, u32[]{:S(2)}, u32[]{:S(2)}) collective-permute-start(bf16[144,768]{1,0:T(8,128)(2,1)S(1)} %get-tuple-element.114), channel_id=1, source_target_pairs={{0,2},{2,0},{1,3},{3,1},{4,6},{6,4},{5,7},{7,5},{8,10},{10,8},{9,1... | collective-permute-start | bytes 663560 | tf_op jit(solution)/shard_map/ppermute | solution.py:821
  307.8 3.0 collective-permute-done.16
  311.0 3.8 collective-permute-done.15.right_ref
  315.5 1.8 tied_add.1
  317.3 1.2 fusion.12
  319.2 2.9 collective-permute-start.18
  322.1 1.4 collective-permute-start.19
  323.5 11.1 %collective-permute-done.17 = bf16[144,768]{1,0:T(8,128)(2,1)S(1)} collective-permute-done((bf16[144,768]{1,0:T(8,128)(2,1)S(1)}, bf16[144,768]{1,0:T(8,128)(2,1)S(1)}, u32[]{:S(2)}, u32[]{:S(2)}) %collective-permute-start.17) | collective-permute-done | bytes 221216 | tf_op jit(solution)/shard_map/ppermute | solution.py:842
  334.6 2.9 collective-permute-done.18
  337.5 3.2 collective-permute-done.19
  340.8 1.4 collective-permute-start.20
  342.3 1.4 fusion.1
  349.1 1.4 collective-permute-start.23
  352.0 9.0 %collective-permute-done.23 = f32[2,576]{1,0:T(2,128)S(1)} collective-permute-done((f32[2,576]{1,0:T(2,128)S(1)}, f32[2,576]{1,0:T(2,128)S(1)}, u32[]{:S(2)}, u32[]{:S(2)}) %collective-permute-start.23) | collective-permute-done | bytes 4640 | tf_op jit(solution)/shard_map/ppermute | solution.py:821
  362.4 2.5 slice.132
  365.2 1.1 copy.41
  366.3 1.5 collective-permute-start.25
  369.2 2.3 collective-permute-start.28
  371.7 2.0 copy.43
  374.7 1.3 divide_subtract_fusion
  376.0 6.2 %collective-permute-done.12 = bf16[512,576]{0,1:T(8,128)(2,1)} collective-permute-done((bf16[512,576]{0,1:T(8,128)(2,1)}, bf16[512,576]{0,1:T(8,128)(2,1)}, u32[]{:S(2)}, u32[]{:S(2)}) %collective-permute-start.12) | collective-permute-done | bytes 589856 | tf_op jit(solution)/shard_map/ppermute | solution.py:990
  382.1 1.4 copy.42
  383.6 1.2 copy-done.7
  385.0 2.0 copy.44
  387.0 2.6 pad_maximum_fusion.3.pieces_ref
  389.6 28.6 %newton.1 = (f32[864,128]{1,0:T(8,128)}, f32[864,128]{1,0:T(8,128)}, f32[864,128]{1,0:T(8,128)}) custom-call(s32[3]{0:T(128)} %pad_add_fusion.1.info, bf16[8,144,768]{2,1,0:T(8,128)(2,1)} %pad_maximum_fusion.3.pieces_ref, bf16[6912,128]{1,0:T(8,128)(2,1)} %all-gather.11.cloned.1.call-done.tie_ref.old_ref, f32[864,128]{1,0:T(8,128)} %bitcast.102, ...), custom_call_target="tpu_custom_call" | custom-call | flops 12000000000 | bytes 9000000 | tf_op jit(solution)/shard_map/newton/pallas_call | solution.py:755
  (144 shorter events, 26.5 us)
Async XLA Ops:
  7.2 139.8 %all-gather.9.cloned.1.call-start = ((), (), s32[]{:S(2)}) async-start(), calls=%async_computation.2 | async-start | bytes 2211840 | tf_op jit(solution)/shard_map/all_gather | solution.py:873
  27.3 4.4 %copy-start.8 = (bf16[2,512,576]{1,2,0:T(8,128)(2,1)S(1)}, bf16[2,512,576]{1,2,0:T(8,128)(2,1)}, u32[]{:S(2)}) copy-start(bf16[2,512,576]{1,2,0:T(8,128)(2,1)} %param.18) | copy-start | bytes 3538948
  29.0 118.0 %all-gather.5.cloned.1.call-start = ((), (), s32[]{:S(2)}) async-start(), calls=%async_computation | async-start | bytes 1990656 | tf_op jit(solution)/shard_map/all_gather | solution.py:873
  30.0 117.0 %all-gather.7.cloned.1.call-start = ((), (), s32[]{:S(2)}) async-start(), calls=%async_computation.1 | async-start | bytes 1990656 | tf_op jit(solution)/shard_map/all_gather | solution.py:873
  30.0 6.0 %collective-permute-start.1 = (bf16[1,864,128]{2,1,0:T(8,128)(2,1)S(1)}, bf16[1,864,128]{2,1,0:T(8,128)(2,1)S(1)}, u32[]{:S(2)}, u32[]{:S(2)}) collective-permute-start(bf16[1,864,128]{2,1,0:T(8,128)(2,1)S(1)} %get-tuple-element.113), channel_id=1, source_target_pairs={{0,2},{2,0},{1,3},{3,1},{4,6},{6,4},{5,7},{7,5},{8,10},{10,8},{9,1... | collective-permute-start | bytes 663560 | tf_op jit(solution)/shard_map/ppermute | solution.py:821
  33.1 0.9 copy-start.9
  33.1 2.0 copy-start.22
  33.2 36.1 %collective-permute-start = (bf16[2,512,576]{1,2,0:T(8,128)(2,1)S(1)}, bf16[2,512,576]{1,2,0:T(8,128)(2,1)}, u32[]{:S(2)}, u32[]{:S(2)}) collective-permute-start(bf16[2,512,576]{1,2,0:T(8,128)(2,1)S(1)} %pad_maximum_fusion.7), channel_id=1, source_target_pairs={{0,3},{3,0},{1,2},{2,1},{4,7},{7,4},{5,6},{6,5},{8,11},{11,8},{9,1... | collective-permute-start | bytes 3538952 | tf_op jit(solution)/shard_map/ppermute | solution.py:893
  35.0 155.5 %all-gather.11.cloned.1.call-start = ((), (), s32[]{:S(2)}) async-start(), calls=%async_computation.3 | async-start | bytes 1990656 | tf_op jit(solution)/shard_map/all_gather | solution.py:926
  35.5 64.1 %copy-start.18 = (s32[512]{0:T(512)}, s32[512]{0:T(512)S(1)}, u32[]{:S(2)}) copy-start(s32[512]{0:T(512)S(1)} %get-tuple-element.136) | copy-start | bytes 6148
  35.5 71.0 %copy-start.19 = (s32[512]{0:T(512)}, s32[512]{0:T(512)S(1)}, u32[]{:S(2)}) copy-start(s32[512]{0:T(512)S(1)} %get-tuple-element.137) | copy-start | bytes 6148
  35.5 16.1 %copy-start.16 = (f32[2,576]{1,0:T(2,128)S(1)}, f32[2,576]{1,0:T(2,128)}, u32[]{:S(2)}) copy-start(f32[2,576]{1,0:T(2,128)} %tie_ref.3) | copy-start | bytes 13828
  36.1 14.2 %collective-permute-start.2 = (bf16[2,864,128]{2,1,0:T(8,128)(2,1)S(1)}, bf16[2,864,128]{2,1,0:T(8,128)(2,1)S(1)}, u32[]{:S(2)}, u32[]{:S(2)}) collective-permute-start(bf16[2,864,128]{2,1,0:T(8,128)(2,1)S(1)} %pad_maximum_fusion.10), channel_id=1, source_target_pairs={{0,4},{4,0},{1,5},{5,1},{2,6},{6,2},{3,7},{7,3},{8,12},{12,8},{9,1... | collective-permute-start | bytes 1327112 | tf_op jit(solution)/shard_map/ppermute | solution.py:821
  50.3 1.1 copy-start.4
  51.3 20.9 %collective-permute-start.3 = (bf16[4,864,128]{2,1,0:T(8,128)(2,1)}, bf16[4,864,128]{2,1,0:T(8,128)(2,1)}, u32[]{:S(2)}, u32[]{:S(2)}) collective-permute-start(bf16[4,864,128]{2,1,0:T(8,128)(2,1)} %pad_maximum_fusion.8), channel_id=1, source_target_pairs={{0,1},{1,0},{2,3},{3,2},{4,5},{5,4},{6,7},{7,6},{8,9},{9,8},{10,11... | collective-permute-start | bytes 2654216 | tf_op jit(solution)/shard_map/ppermute | solution.py:821
  70.9 1.3 copy-start.5
  83.8 15.8 %collective-permute-start.5 = (bf16[384,512]{1,0:T(8,128)(2,1)S(1)}, bf16[384,512]{1,0:T(8,128)(2,1)}, u32[]{:S(2)}, u32[]{:S(2)}) collective-permute-start(bf16[384,512]{1,0:T(8,128)(2,1)S(1)} %dynamic-slice_bitcast_fusion), channel_id=1, source_target_pairs={{0,2},{2,0},{1,3},{3,1},{4,6},{6,4},{5,7},{7,5},{8,10},{10,8},{9,1... | collective-permute-start | bytes 1179656 | tf_op jit(solution)/shard_map/ppermute | solution.py:909
  84.7 32.6 %collective-permute-start.4 = (bf16[2,384,512]{2,1,0:T(8,128)(2,1)}, bf16[2,384,512]{2,1,0:T(8,128)(2,1)S(1)}, u32[]{:S(2)}, u32[]{:S(2)}) collective-permute-start(bf16[2,384,512]{2,1,0:T(8,128)(2,1)} %get-tuple-element.42.kv_ref), channel_id=1, source_target_pairs={{0,1},{1,0},{2,3},{3,2},{4,5},{5,4},{6,7},{7,6},{8,9},{9,8},{10,11... | collective-permute-start | bytes 2359304 | tf_op jit(solution)/shard_map/ppermute | solution.py:914
  99.6 17.7 %collective-permute-start.6 = (bf16[384,512]{1,0:T(8,128)(2,1)}, bf16[384,512]{1,0:T(8,128)(2,1)}, u32[]{:S(2)}, u32[]{:S(2)}) collective-permute-start(bf16[384,512]{1,0:T(8,128)(2,1)} %collective-permute-done.5.far_ref), channel_id=1, source_target_pairs={{0,1},{1,0},{2,3},{3,2},{4,5},{5,4},{6,7},{7,6},{8,9},{9,8},{10,11... | collective-permute-start | bytes 1179656 | tf_op jit(solution)/shard_map/ppermute | solution.py:916
  117.2 0.9 copy-start.23
  184.0 17.5 %collective-permute-start.8 = (bf16[4,3,144,768]{3,2,1,0:T(8,128)(2,1)}, bf16[4,3,144,768]{3,2,1,0:T(8,128)(2,1)S(1)}, u32[]{:S(2)}, u32[]{:S(2)}) collective-permute-start(bf16[4,3,144,768]{3,2,1,0:T(8,128)(2,1)} %get-tuple-element.55), channel_id=1, source_target_pairs={{0,1},{1,0},{2,3},{3,2},{4,5},{5,4},{6,7},{7,6},{8,9},{9,8},{10,11... | collective-permute-start | bytes 7962632 | tf_op jit(solution)/shard_map/ppermute | solution.py:821
  190.5 11.1 %copy-start.3 = (bf16[4,3,144,768]{3,2,1,0:T(8,128)(2,1)S(1)}, bf16[4,3,144,768]{3,2,1,0:T(8,128)(2,1)}, u32[]{:S(2)}) copy-start(bf16[4,3,144,768]{3,2,1,0:T(8,128)(2,1)} %get-tuple-element.54) | copy-start | bytes 7962628
  203.7 25.1 %copy-start.10 = (bf16[2,384,512]{2,1,0:T(8,128)(2,1)S(1)}, bf16[2,384,512]{2,1,0:T(8,128)(2,1)}, u32[]{:S(2)}) copy-start(bf16[2,384,512]{2,1,0:T(8,128)(2,1)} %get-tuple-element.59) | copy-start | bytes 2359300
  228.7 11.1 %copy-start.1 = (bf16[4,3,144,768]{3,2,1,0:T(8,128)(2,1)S(1)}, bf16[4,3,144,768]{3,2,1,0:T(8,128)(2,1)}, u32[]{:S(2)}) copy-start(bf16[4,3,144,768]{3,2,1,0:T(8,128)(2,1)} %add_convert_fusion.tie_ref) | copy-start | bytes 7962628
  231.3 11.9 %copy-start.6 = (bf16[2,384,512]{2,1,0:T(8,128)(2,1)S(1)}, bf16[2,384,512]{2,1,0:T(8,128)(2,1)}, u32[]{:S(2)}) copy-start(bf16[2,384,512]{2,1,0:T(8,128)(2,1)} %get-tuple-element.57.kept0_ref) | copy-start | bytes 2359300
  231.3 11.9 %collective-permute-start.9 = (bf16[4,384,512]{2,1,0:T(8,128)(2,1)}, bf16[4,384,512]{2,1,0:T(8,128)(2,1)}, u32[]{:S(2)}, u32[]{:S(2)}) collective-permute-start(bf16[4,384,512]{2,1,0:T(8,128)(2,1)} %pad_maximum_fusion.4), channel_id=1, source_target_pairs={{0,1},{1,0},{2,3},{3,2},{4,5},{5,4},{6,7},{7,6},{8,9},{9,8},{10,11... | collective-permute-start | bytes 4718600 | tf_op jit(solution)/shard_map/ppermute | solution.py:965
  241.0 31.4 %collective-permute-start.11 = (bf16[2,3,144,768]{3,2,1,0:T(8,128)(2,1)}, bf16[2,3,144,768]{3,2,1,0:T(8,128)(2,1)}, u32[]{:S(2)}, u32[]{:S(2)}) collective-permute-start(bf16[2,3,144,768]{3,2,1,0:T(8,128)(2,1)} %slice.156), channel_id=1, source_target_pairs={{0,4},{4,0},{1,5},{5,1},{2,6},{6,2},{3,7},{7,3},{8,12},{12,8},{9,1... | collective-permute-start | bytes 3981320 | tf_op jit(solution)/shard_map/ppermute | solution.py:821
  244.7 30.4 %collective-permute-start.10 = (bf16[384,512]{1,0:T(8,128)(2,1)S(1)}, bf16[384,512]{1,0:T(8,128)(2,1)S(1)}, u32[]{:S(2)}, u32[]{:S(2)}) collective-permute-start(bf16[384,512]{1,0:T(8,128)(2,1)S(1)} %fusion.5), channel_id=1, source_target_pairs={{0,2},{2,0},{1,3},{3,1},{4,6},{6,4},{5,7},{7,5},{8,10},{10,8},{9,1... | collective-permute-start | bytes 1179656 | tf_op jit(solution)/shard_map/ppermute | solution.py:970
  275.1 0.7 copy-start.12
  283.0 2.6 collective-permute-start.13
  285.6 3.8 copy-start
  287.9 13.5 %collective-permute-start.14 = (bf16[2,144,768]{2,1,0:T(8,128)(2,1)}, bf16[2,144,768]{2,1,0:T(8,128)(2,1)}, u32[]{:S(2)}, u32[]{:S(2)}) collective-permute-start(bf16[2,144,768]{2,1,0:T(8,128)(2,1)} %slice.158), channel_id=1, source_target_pairs={{0,4},{4,0},{1,5},{5,1},{2,6},{6,2},{3,7},{7,3},{8,12},{12,8},{9,1... | collective-permute-start | bytes 1327112 | tf_op jit(solution)/shard_map/ppermute | solution.py:821
  289.5 21.4 %collective-permute-start.16 = (bf16[3,144,768]{2,1,0:T(8,128)(2,1)S(1)}, bf16[3,144,768]{2,1,0:T(8,128)(2,1)S(1)}, u32[]{:S(2)}, u32[]{:S(2)}) collective-permute-start(bf16[3,144,768]{2,1,0:T(8,128)(2,1)S(1)} %slice_bitcast_fusion), channel_id=1, source_target_pairs={{0,2},{2,0},{1,3},{3,1},{4,6},{6,4},{5,7},{7,5},{8,10},{10,8},{9,1... | collective-permute-start | bytes 1990664 | tf_op jit(solution)/shard_map/ppermute | solution.py:821
  303.3 11.5 %collective-permute-start.15 = (bf16[144,768]{1,0:T(8,128)(2,1)S(1)}, bf16[144,768]{1,0:T(8,128)(2,1)S(1)}, u32[]{:S(2)}, u32[]{:S(2)}) collective-permute-start(bf16[144,768]{1,0:T(8,128)(2,1)S(1)} %get-tuple-element.114), channel_id=1, source_target_pairs={{0,2},{2,0},{1,3},{3,1},{4,6},{6,4},{5,7},{7,5},{8,10},{10,8},{9,1... | collective-permute-start | bytes 663560 | tf_op jit(solution)/shard_map/ppermute | solution.py:821
  314.8 0.7 copy-start.13
  318.5 16.1 %collective-permute-start.17 = (bf16[144,768]{1,0:T(8,128)(2,1)S(1)}, bf16[144,768]{1,0:T(8,128)(2,1)S(1)}, u32[]{:S(2)}, u32[]{:S(2)}) collective-permute-start(bf16[144,768]{1,0:T(8,128)(2,1)S(1)} %get-tuple-element.107), channel_id=1, source_target_pairs={{0,8},{8,16},{16,24},{24,0},{1,9},{9,17},{17,25},{25,1},{2,10},{10... | collective-permute-start | bytes 663560 | tf_op jit(solution)/shard_map/ppermute | solution.py:842
  319.2 18.3 %collective-permute-start.18 = (bf16[144,768]{1,0:T(8,128)(2,1)S(1)}, bf16[144,768]{1,0:T(8,128)(2,1)S(1)}, u32[]{:S(2)}, u32[]{:S(2)}) collective-permute-start(bf16[144,768]{1,0:T(8,128)(2,1)S(1)} %get-tuple-element.108), channel_id=1, source_target_pairs={{0,16},{8,24},{16,0},{24,8},{1,17},{9,25},{17,1},{25,9},{2,18},{10... | collective-permute-start | bytes 663560 | tf_op jit(solution)/shard_map/ppermute | solution.py:842
  322.1 18.5 %collective-permute-start.19 = (bf16[144,768]{1,0:T(8,128)(2,1)S(1)}, bf16[144,768]{1,0:T(8,128)(2,1)S(1)}, u32[]{:S(2)}, u32[]{:S(2)}) collective-permute-start(bf16[144,768]{1,0:T(8,128)(2,1)S(1)} %get-tuple-element.109), channel_id=1, source_target_pairs={{0,24},{8,0},{16,8},{24,16},{1,25},{9,1},{17,9},{25,17},{2,26},{10... | collective-permute-start | bytes 663560 | tf_op jit(solution)/shard_map/ppermute | solution.py:842
  323.5 20.5 %copy-start.26 = (s32[4]{0:T(128)S(1)}, s32[4]{0:T(128)}, u32[]{:S(2)}) copy-start(s32[4]{0:T(128)} %constant.183.clone) | copy-start | bytes 52
  323.5 21.8 %copy-start.25 = (s32[6]{0:T(128)S(1)}, s32[6]{0:T(128)}, u32[]{:S(2)}) copy-start(s32[6]{0:T(128)} %constant.185.clone) | copy-start | bytes 76
  323.5 23.0 %copy-start.24 = (s32[4]{0:T(128)S(1)}, s32[4]{0:T(128)}, u32[]{:S(2)}) copy-start(s32[4]{0:T(128)} %constant.184.clone) | copy-start | bytes 52
  323.5 25.6 %copy-start.14 = (f32[1,576]{1,0:T(1,128)S(1)}, f32[1,576]{1,0:T(1,128)}, u32[]{:S(2)}) copy-start(f32[1,576]{1,0:T(1,128)} %get-tuple-element.69.tie_ref) | copy-start | bytes 6916
  323.5 25.6 %copy-start.15 = (f32[1,576]{1,0:T(1,128)S(1)}, f32[1,576]{1,0:T(1,128)}, u32[]{:S(2)}) copy-start(f32[1,576]{1,0:T(1,128)} %get-tuple-element.73) | copy-start | bytes 6916
  340.8 9.7 %collective-permute-start.20 = (bf16[1,144,768]{2,1,0:T(8,128)(2,1)S(1)}, bf16[1,144,768]{2,1,0:T(8,128)(2,1)S(1)}, u32[]{:S(2)}, u32[]{:S(2)}) collective-permute-start(bf16[1,144,768]{2,1,0:T(8,128)(2,1)S(1)} %fusion.6), channel_id=1, source_target_pairs={{0,2},{2,0},{1,3},{3,1},{4,6},{6,4},{5,7},{7,5},{8,10},{10,8},{9,1... | collective-permute-start | bytes 663560 | tf_op jit(solution)/shard_map/ppermute | solution.py:821
  343.9 21.0 %collective-permute-start.7 = (bf16[512,576]{0,1:T(8,128)(2,1)S(1)}, bf16[512,576]{0,1:T(8,128)(2,1)S(1)}, u32[]{:S(2)}, u32[]{:S(2)}) collective-permute-start(bf16[512,576]{0,1:T(8,128)(2,1)S(1)} %copy.39), channel_id=1, source_target_pairs={{0,3},{3,0},{1,2},{2,1},{4,7},{7,4},{5,6},{6,5},{8,11},{11,8},{9,1... | collective-permute-start | bytes 1769480 | tf_op jit(solution)/shard_map/ppermute | solution.py:943
  349.1 11.9 %collective-permute-start.23 = (f32[2,576]{1,0:T(2,128)S(1)}, f32[2,576]{1,0:T(2,128)S(1)}, u32[]{:S(2)}, u32[]{:S(2)}) collective-permute-start(f32[2,576]{1,0:T(2,128)S(1)} %pad_maximum_fusion.12), channel_id=1, source_target_pairs={{0,2},{2,0},{1,3},{3,1},{4,6},{6,4},{5,7},{7,5},{8,10},{10,8},{9,1... | collective-permute-start | bytes 13832 | tf_op jit(solution)/shard_map/ppermute | solution.py:821
  351.3 16.6 %collective-permute-start.21 = (bf16[2,144,768]{2,1,0:T(8,128)(2,1)}, bf16[2,144,768]{2,1,0:T(8,128)(2,1)S(1)}, u32[]{:S(2)}, u32[]{:S(2)}) collective-permute-start(bf16[2,144,768]{2,1,0:T(8,128)(2,1)} %pad_maximum_fusion.11), channel_id=1, source_target_pairs={{0,4},{4,0},{1,5},{5,1},{2,6},{6,2},{3,7},{7,3},{8,12},{12,8},{9,1... | collective-permute-start | bytes 1327112 | tf_op jit(solution)/shard_map/ppermute | solution.py:821
  361.0 5.3 %collective-permute-start.24 = (f32[2,576]{1,0:T(2,128)S(1)}, f32[2,576]{1,0:T(2,128)S(1)}, u32[]{:S(2)}, u32[]{:S(2)}) collective-permute-start(f32[2,576]{1,0:T(2,128)S(1)} %fusion.16), channel_id=1, source_target_pairs={{0,4},{4,0},{1,5},{5,1},{2,6},{6,2},{3,7},{7,3},{8,12},{12,8},{9,1... | collective-permute-start | bytes 13832 | tf_op jit(solution)/shard_map/ppermute | solution.py:821
  362.4 2.8 copy-start.11
  366.3 15.8 %collective-permute-start.12 = (bf16[512,576]{0,1:T(8,128)(2,1)}, bf16[512,576]{0,1:T(8,128)(2,1)}, u32[]{:S(2)}, u32[]{:S(2)}) collective-permute-start(bf16[512,576]{0,1:T(8,128)(2,1)} %copy.41), channel_id=1, source_target_pairs={{0,3},{3,0},{1,2},{2,1},{4,7},{7,4},{5,6},{6,5},{8,11},{11,8},{9,1... | collective-permute-start | bytes 1769480 | tf_op jit(solution)/shard_map/ppermute | solution.py:990
  366.3 5.2 %copy-start.2 = (f32[1,512,576]{2,1,0:T(8,128)S(1)}, f32[1,512,576]{2,1,0:T(8,128)}, u32[]{:S(2)}) copy-start(f32[1,512,576]{2,1,0:T(8,128)} %slice.132) | copy-start | bytes 3538948
  366.3 2.7 collective-permute-start.25
  368.9 18.1 %collective-permute-start.22 = (bf16[4,144,768]{2,1,0:T(8,128)(2,1)}, bf16[4,144,768]{2,1,0:T(8,128)(2,1)}, u32[]{:S(2)}, u32[]{:S(2)}) collective-permute-start(bf16[4,144,768]{2,1,0:T(8,128)(2,1)} %pad_maximum_fusion.9), channel_id=1, source_target_pairs={{0,1},{1,0},{2,3},{3,2},{4,5},{5,4},{6,7},{7,6},{8,9},{9,8},{10,11... | collective-permute-start | bytes 2654216 | tf_op jit(solution)/shard_map/ppermute | solution.py:821
  369.0 4.7 %collective-permute-start.26 = (f32[2,576]{1,0:T(2,128)S(1)}, f32[2,576]{1,0:T(2,128)S(1)}, u32[]{:S(2)}, u32[]{:S(2)}) collective-permute-start(f32[2,576]{1,0:T(2,128)S(1)} %add.203), channel_id=1, source_target_pairs={{0,8},{8,16},{16,24},{24,0},{1,9},{9,17},{17,25},{25,1},{2,10},{10... | collective-permute-start | bytes 13832 | tf_op jit(solution)/shard_map/ppermute | solution.py:996
  369.1 4.6 %collective-permute-start.27 = (f32[2,576]{1,0:T(2,128)S(1)}, f32[2,576]{1,0:T(2,128)S(1)}, u32[]{:S(2)}, u32[]{:S(2)}) collective-permute-start(f32[2,576]{1,0:T(2,128)S(1)} %add.203), channel_id=1, source_target_pairs={{0,16},{8,24},{16,0},{24,8},{1,17},{9,25},{17,1},{25,9},{2,18},{10... | collective-permute-start | bytes 13832 | tf_op jit(solution)/shard_map/ppermute | solution.py:996
  369.2 5.5 %collective-permute-start.28 = (f32[2,576]{1,0:T(2,128)S(1)}, f32[2,576]{1,0:T(2,128)}, u32[]{:S(2)}, u32[]{:S(2)}) collective-permute-start(f32[2,576]{1,0:T(2,128)S(1)} %add.203), channel_id=1, source_target_pairs={{0,24},{8,0},{16,8},{24,16},{1,25},{9,1},{17,9},{25,17},{2,26},{10... | collective-permute-start | bytes 13832 | tf_op jit(solution)/shard_map/ppermute | solution.py:996
  371.7 3.0 copy-start.17
  371.7 3.0 copy-start.20
  371.7 3.0 copy-start.21
  383.5 1.3 copy-start.7
Sparse Core Ops, SparseCore 0:
  29.1 36.7 all-gather.8
  68.3 31.2 all-gather.4
  101.5 26.5 all-gather.6
  130.4 44.9 all-gather.10
